TPU v7x, 256 devices: a whole 4x4x8 slice. The times are simulated.
256 devices in a mesh: gx: 64 (over z, y, core), gz: 4 (over x).
Axes of the slice: x: 4, y: 4, z: 8, core: 2. Of those that a mesh axis runs over, the one named last changes fastest.
Arguments:
- intensity: bfloat16 [512, 256, 512], P('gx', None, 'gz'), may hold values from 0 to 1
- membrane: bfloat16 [512, 256, 512], P('gx', None, 'gz'), may hold values from 0 to 1
- synapse: bfloat16 [512, 256, 512], P('gx', None, 'gz'), may hold values from 0 to 1
- transfer: float32 [4, 16], replicated, may hold values from 0 to 1
- occupancy: int32 [64, 32, 64], P('gx', None, 'gz'), may hold values from 0 to 1, as said below
Outputs:
- x_image: float32 [4, 256, 512], P(None, 'gx', 'gz')
- z_image: float32 [4, 512, 256], P(None, 'gx', 'gz')
Inputs may be any that keep to these rules, and one draw needn't show every extreme that they name: `occupancy`: 1 marks an occupied block; every cell of a block marked 0 is empty.
All inputs are finite; a program needn't handle non-finite values.
Results may differ from a plain program's by a relative error of at most 0.0003.
Values may be sent and summed in bfloat16 or wider, within the bound.
No kernel may reach another device: no remote copies, remote signals or barrier semaphores. Data moves between devices by JAX's collectives and lax.ppermute only.
A program may use at most 64 MiB of HBM per device.

v0:
```python
import jax
import jax.numpy as jnp
from jax import lax
from jax.sharding import PartitionSpec as P

MEMBRANE_COLOR = (0.9, 0.2, 0.1)
SYNAPSE_COLOR = (0.1, 0.8, 0.3)


def with_halo(block, sides, width):
    for axis, dim in sides:
        count = lax.axis_size(axis)
        forward = [(i, i + 1) for i in range(count - 1)]
        backward = [(target, source) for source, target in forward]
        low = lax.ppermute(
            lax.slice_in_dim(block, block.shape[dim] - width, None, axis=dim), axis, forward
        )
        high = lax.ppermute(lax.slice_in_dim(block, 0, width, axis=dim), axis, backward)
        block = jnp.concatenate([low, block, high], axis=dim)
    return block


def transfer_lookup(value, transfer):
    knots = transfer.shape[1]
    t_pos = jnp.clip(value, 0.0, 1.0) * (knots - 1)
    outs = [jnp.zeros_like(value) for c in range(4)]
    for k in range(knots):
        weight = jnp.maximum(0.0, 1.0 - jnp.abs(t_pos - k))
        for c in range(4):
            outs[c] = outs[c] + weight * transfer[c, k]
    return outs


def cell_terms(grad_x, grad_y, grad_z, lit, memb, syn, tables, occupied, spacing):
    norm = jnp.sqrt(grad_x * grad_x + grad_y * grad_y + grad_z * grad_z + 0.25)
    shade = 0.3 + 0.7 * jnp.abs(lit) / norm
    sigma = (tables[3] + 1.5 * memb + 0.5 * syn) * occupied
    alpha = 1.0 - jnp.exp(-sigma * spacing)
    colors = []
    for c in range(3):
        emission = shade * tables[c] + memb * MEMBRANE_COLOR[c] + syn * SYNAPSE_COLOR[c]
        colors.append(alpha * emission)
    return (jnp.stack(colors), alpha)


def exclusive_product(values, axis):
    running = jnp.cumprod(values, axis=axis)
    lead = jnp.ones_like(lax.slice_in_dim(values, 0, 1, axis=axis))
    rest = lax.slice_in_dim(running, 0, values.shape[axis] - 1, axis=axis)
    return (jnp.concatenate([lead, rest], axis=axis), running)


def local_composite(colors, alpha, axis):
    before, running = exclusive_product(1.0 - alpha, axis)
    rgb = jnp.sum(colors * jnp.expand_dims(before, 0), axis=axis + 1)
    total = lax.index_in_dim(running, alpha.shape[axis] - 1, axis, False)
    return jnp.concatenate([rgb, total[None]], axis=0)


def depth_composite(stacked):
    trans = stacked[3]
    before, running = exclusive_product(trans, 0)
    rgb = jnp.sum(stacked[:3] * before[None], axis=1)
    opacity = 1.0 - running[-1]
    return jnp.concatenate([rgb, opacity[None]], axis=0)


def body(intensity, membrane, synapse, transfer, occupancy):
    xdev, height, zdev = intensity.shape
    block = xdev // occupancy.shape[0]
    full_x = xdev * lax.axis_size("gx")
    full_z = zdev * lax.axis_size("gz")
    padded = with_halo(intensity, (("gx", 0), ("gz", 2)), 1).astype(jnp.float32)
    center = padded[1:-1, :, 1:-1]
    grad_x = 0.5 * (padded[2:, :, 1:-1] - padded[:-2, :, 1:-1])
    grad_z = 0.5 * (padded[1:-1, :, 2:] - padded[1:-1, :, :-2])
    side = jnp.pad(center, ((0, 0), (1, 1), (0, 0)))
    grad_y = 0.5 * (side[:, 2:, :] - side[:, :-2, :])
    memb = membrane.astype(jnp.float32)
    syn = synapse.astype(jnp.float32)
    flags = occupancy.astype(jnp.float32)[:, None, :, None, :, None]
    shape_six = (flags.shape[0], block, flags.shape[2], block, flags.shape[4], block)
    occupied = jnp.broadcast_to(flags, shape_six).reshape(xdev, height, zdev)
    tables = transfer_lookup(center, transfer)
    color_x, alpha_x = cell_terms(
        grad_x, grad_y, grad_z, grad_x, memb, syn, tables, occupied, 2.0 / full_x
    )
    partial_x = local_composite(color_x, alpha_x, 0)
    arrived = lax.all_to_all(partial_x[:, None], "gx", split_axis=2, concat_axis=1, tiled=True)
    x_image = depth_composite(arrived)
    color_z, alpha_z = cell_terms(
        grad_x, grad_y, grad_z, grad_z, memb, syn, tables, occupied, 2.0 / full_z
    )
    partial_z = local_composite(color_z, alpha_z, 2)
    arrived_z = lax.all_to_all(partial_z[:, None], "gz", split_axis=3, concat_axis=1, tiled=True)
    z_image = depth_composite(arrived_z)
    return (x_image, z_image)


def solution(mesh):
    in_specs = (
        P("gx", None, "gz"),
        P("gx", None, "gz"),
        P("gx", None, "gz"),
        P(),
        P("gx", None, "gz"),
    )
    out_specs = (P(None, "gx", "gz"), P(None, "gx", "gz"))
    return jax.shard_map(body, mesh=mesh, in_specs=in_specs, out_specs=out_specs, check_vma=False)
```

profile of v0, /device:TPU:1, one launch (start us, length us, event | category | flops | bytes accessed | tf_op | source)
XLA Modules:
  0.0 131.3 jit_solution(7053546465844893696)
XLA Ops:
  0.7 1.3 %copy.61 = bf16[8,256,128]{1,2,0:T(8,128)(2,1)S(1)} copy(bf16[8,256,128]{2,1,0:T(8,128)(2,1)} %param.5) | data formatting | bytes 1048576 | tf_op args[0]
  2.0 4.6 %collective-permute-start = (bf16[1,256,128]{1,2,0:T(8,128)(2,1)S(1)}, bf16[1,256,128]{1,2,0:T(8,128)(2,1)S(1)}, u32[]{:S(2)}, u32[]{:S(2)}) collective-permute-start(bf16[1,256,128]{1,2,0:T(8,128)(2,1)S(1)} %get-tuple-element.18), channel_id=1, source_target_pairs={{0,4},{4,8},{8,12},{12,16},{16,20},{20,24},{24,28},{28,32},{32,36}... | collective-permute-start | bytes 196616 | tf_op jit(solution)/shard_map/ppermute | solution.py:15
  6.6 1.9 %collective-permute-start.1 = (bf16[1,256,128]{1,2,0:T(8,128)(2,1)S(1)}, bf16[1,256,128]{1,2,0:T(8,128)(2,1)S(1)}, u32[]{:S(2)}, u32[]{:S(2)}) collective-permute-start(bf16[1,256,128]{1,2,0:T(8,128)(2,1)S(1)} %get-tuple-element.19), channel_id=1, source_target_pairs={{4,0},{8,4},{12,8},{16,12},{20,16},{24,20},{28,24},{32,28},{36,32}... | collective-permute-start | bytes 196616 | tf_op jit(solution)/shard_map/ppermute | solution.py:18
  8.6 2.1 %fusion.53 = (f32[1,1]{1,0:T(1,128)}, f32[1,1]{1,0:T(1,128)}, f32[1,1]{1,0:T(1,128)}, f32[1,1]{1,0:T(1,128)}, f32[1,1]{1,0:T(1,128)}, /*index=5*/f32[1,1]{1,0:T(...) fusion(f32[4,16]{1,0:T(4,128)} %param.8), kind=kLoop, calls=%fused_computation.103 | loop fusion | bytes 152 | tf_op jit(solution)/shard_map/slice | solution.py:30
  10.7 2.1 %fusion.52 = (f32[1,1]{1,0:T(1,128)}, f32[1,1]{1,0:T(1,128)}, f32[1,1]{1,0:T(1,128)}, f32[1,1]{1,0:T(1,128)}, f32[1,1]{1,0:T(1,128)}, /*index=5*/f32[1,1]{1,0:T(...) fusion(f32[4,16]{1,0:T(4,128)} %param.8), kind=kLoop, calls=%fused_computation.102 | loop fusion | bytes 152 | tf_op jit(solution)/shard_map/slice | solution.py:30
  13.5 2.1 %fusion.51 = (f32[1,1]{1,0:T(1,128)}, f32[1,1]{1,0:T(1,128)}, f32[1,1]{1,0:T(1,128)}, f32[1,1]{1,0:T(1,128)}, f32[1,1]{1,0:T(1,128)}, /*index=5*/f32[1,1]{1,0:T(...) fusion(f32[4,16]{1,0:T(4,128)} %param.8), kind=kLoop, calls=%fused_computation.101 | loop fusion | bytes 152 | tf_op jit(solution)/shard_map/slice | solution.py:30
  15.6 3.1 %collective-permute-start.2 = (bf16[10,256,1]{1,0,2:T(8,128)(2,1)S(1)}, bf16[10,256,1]{1,0,2:T(8,128)(2,1)S(1)}, u32[]{:S(2)}, u32[]{:S(2)}) collective-permute-start(bf16[10,256,1]{1,0,2:T(8,128)(2,1)S(1)} %copy.64), channel_id=1, source_target_pairs={{0,1},{1,2},{2,3},{4,5},{5,6},{6,7},{8,9},{9,10},{10,11},{12,13},{... | collective-permute-start | bytes 15368 | tf_op jit(solution)/shard_map/ppermute | solution.py:15
  18.8 1.3 collective-permute-start.3
  21.5 1.0 broadcast_in_dim.14
  23.2 1.2 maximum_convert_fusion
  24.5 27.4 %fusion.25 = (f32[1,8,256,128]{2,3,1,0:T(8,128)S(1)}, f32[8,256,128]{1,2,0:T(8,128)S(1)}, f32[8,256,128]{1,2,0:T(8,128)S(1)}, f32[8,256,128]{1,2,0:T(8,128)S(1)}, f32[8,256,128]{1,2,0:T(8,128)S(1)}) fusion(bf16[8,256,128]{1,2,0:T(8,128)(2,1)S(1)} %copy.69, bf16[8,256,128]{1,2,0:T(8,128)(2,1)S(1)} %copy.68, f32[10,256,130]{1,2,0:T(8,128)S(1)} %maximum_convert_fusion, ...), kind=kLoop, calls=%fused_computation.37 | loop fusion | flops 41680896 | bytes 12714112 | tf_op jit(solution)/shard_map/stack | solution.py:43
  52.5 13.6 %fusion.17 = (f32[1,8,256,128]{2,3,1,0:T(8,128)S(1)}, f32[8,256,128]{1,2,0:T(8,128)S(1)}) fusion(f32[8,256,128]{1,2,0:T(8,128)S(1)} %get-tuple-element.6, bf16[8,256,128]{1,2,0:T(8,128)(2,1)S(1)} %copy.69, bf16[8,256,128]{1,2,0:T(8,128)(2,1)S(1)} %copy.68, f32[8,256,128]{1,2,0:T(8,128)S(1)} %get-tuple-element.3, f32[]{:T(128)} %bitcast.66, f32[]{:T(128)} %bitcast.65, ...), kind=kLoop, calls=%fused_computation.29 | loop fusion | flops 27262976 | bytes 6291520 | tf_op jit(solution)/shard_map/stack | solution.py:43
  66.1 13.5 %fusion.21 = (f32[1,8,256,128]{2,3,1,0:T(8,128)S(1)}, f32[8,256,128]{1,2,0:T(8,128)S(1)}) fusion(f32[8,256,128]{1,2,0:T(8,128)S(1)} %get-tuple-element.6, bf16[8,256,128]{1,2,0:T(8,128)(2,1)S(1)} %copy.69, bf16[8,256,128]{1,2,0:T(8,128)(2,1)S(1)} %copy.68, f32[8,256,128]{1,2,0:T(8,128)S(1)} %get-tuple-element.3, f32[]{:T(128)} %bitcast.49, f32[]{:T(128)} %bitcast.48, ...), kind=kLoop, calls=%fused_computation.33 | loop fusion | flops 27262976 | bytes 6291520 | tf_op jit(solution)/shard_map/stack | solution.py:43
  79.6 1.6 %fusion.19 = (f32[1,8,256,128]{2,3,1,0:T(8,128)S(1)}, f32[1,8,256,128]{2,3,1,0:T(8,128)}, f32[8,256,128]{1,2,0:T(8,128)S(1)}) fusion(f32[8,256,128]{1,2,0:T(8,128)S(1)} %get-tuple-element.6, bf16[8,256,128]{1,2,0:T(8,128)(2,1)S(1)} %copy.69, bf16[8,256,128]{1,2,0:T(8,128)(2,1)S(1)} %copy.68, f32[8,256,128]{1,2,0:T(8,128)S(1)} %get-tuple-element.12, ...), kind=kLoop, calls=%fused_computation.31 | loop fusion | flops 3932160 | bytes 8388608 | tf_op jit(solution)/shard_map/stack | solution.py:43
  83.5 1.0 copy.78
  84.5 1.9 %bitcast_bitcast_fusion = f32[256,1,4,8]{3,2,1,0:T(4,128)} fusion(f32[4,8,256]{1,0,2:T(4,128)} %copy.78), kind=kLoop, calls=%fused_computation.105 | loop fusion | bytes 65536
  86.4 2.2 %reshape.27 = f32[4,1,2048]{2,1,0:T(1,128)} reshape(f32[256,1,4,8]{3,2,1,0:T(4,128)} %bitcast_bitcast_fusion) | data formatting | bytes 65536
  88.6 4.4 %all-to-all-start.1 = ((f32[4,1,2048]{2,1,0:T(1,128)}), f32[4,1,2048]{2,1,0:T(1,128)S(1)}, u32[]{:S(2)}, u32[]{:S(2)}) async-start(f32[4,1,2048]{2,1,0:T(1,128)} %reshape.27), calls=%async_computation.1 | async-start | bytes 65536 | tf_op jit(solution)/shard_map/all_to_all | solution.py:95
  93.1 1.1 copy-done.2
  95.1 1.0 copy.73
  96.2 1.1 all-to-all-done.1
  97.3 15.1 %all-to-all-start = ((f32[4,1,256,128]{3,1,0,2:T(1,128)}), f32[4,1,256,128]{3,1,0,2:T(1,128)S(1)}, u32[]{:S(2)}, u32[]{:S(2)}) async-start(f32[4,1,256,128]{3,1,0,2:T(1,128)} %copy.73), calls=%async_computation | async-start | bytes 1048576 | tf_op jit(solution)/shard_map/all_to_all | solution.py:89
  112.9 0.7 reduce
  115.1 15.0 %all-to-all-done = f32[4,1,256,128]{3,1,0,2:T(1,128)S(1)} async-done(((f32[4,1,256,128]{3,1,0,2:T(1,128)}), f32[4,1,256,128]{3,1,0,2:T(1,128)S(1)}, u32[]{:S(2)}, u32[]{:S(2)}) %all-to-all-start) | async-done | bytes 524320 | tf_op jit(solution)/shard_map/all_to_all | solution.py:89
  (63 shorter events, 9.9 us)
Async XLA Ops:
  0.6 19.4 %copy-start.3 = (f32[4,16]{1,0:T(4,128)S(1)}, f32[4,16]{1,0:T(4,128)}, u32[]{:S(2)}) copy-start(f32[4,16]{1,0:T(4,128)} %param.8) | copy-start | bytes 772
  0.6 20.1 %copy-start.4 = (bf16[8,256,128]{2,1,0:T(8,128)(2,1)S(1)}, bf16[8,256,128]{2,1,0:T(8,128)(2,1)}, u32[]{:S(2)}) copy-start(bf16[8,256,128]{2,1,0:T(8,128)(2,1)} %param.6) | copy-start | bytes 1572868
  0.7 20.3 %copy-start.5 = (bf16[8,256,128]{2,1,0:T(8,128)(2,1)S(1)}, bf16[8,256,128]{2,1,0:T(8,128)(2,1)}, u32[]{:S(2)}) copy-start(bf16[8,256,128]{2,1,0:T(8,128)(2,1)} %param.7) | copy-start | bytes 1572868
  2.0 18.1 %copy-start = (bf16[8,256,128]{1,2,0:T(8,128)(2,1)}, bf16[8,256,128]{1,2,0:T(8,128)(2,1)S(1)}, u32[]{:S(2)}) copy-start(bf16[8,256,128]{1,2,0:T(8,128)(2,1)S(1)} %copy.61) | copy-start | bytes 1572868
  2.0 13.5 %collective-permute-start = (bf16[1,256,128]{1,2,0:T(8,128)(2,1)S(1)}, bf16[1,256,128]{1,2,0:T(8,128)(2,1)S(1)}, u32[]{:S(2)}, u32[]{:S(2)}) collective-permute-start(bf16[1,256,128]{1,2,0:T(8,128)(2,1)S(1)} %get-tuple-element.18), channel_id=1, source_target_pairs={{0,4},{4,8},{8,12},{12,16},{16,20},{20,24},{24,28},{28,32},{32,36}... | collective-permute-start | bytes 196616 | tf_op jit(solution)/shard_map/ppermute | solution.py:15
  6.6 8.9 %collective-permute-start.1 = (bf16[1,256,128]{1,2,0:T(8,128)(2,1)S(1)}, bf16[1,256,128]{1,2,0:T(8,128)(2,1)S(1)}, u32[]{:S(2)}, u32[]{:S(2)}) collective-permute-start(bf16[1,256,128]{1,2,0:T(8,128)(2,1)S(1)} %get-tuple-element.19), channel_id=1, source_target_pairs={{4,0},{8,4},{12,8},{16,12},{20,16},{24,20},{28,24},{32,28},{36,32}... | collective-permute-start | bytes 196616 | tf_op jit(solution)/shard_map/ppermute | solution.py:18
  15.6 7.0 %collective-permute-start.2 = (bf16[10,256,1]{1,0,2:T(8,128)(2,1)S(1)}, bf16[10,256,1]{1,0,2:T(8,128)(2,1)S(1)}, u32[]{:S(2)}, u32[]{:S(2)}) collective-permute-start(bf16[10,256,1]{1,0,2:T(8,128)(2,1)S(1)} %copy.64), channel_id=1, source_target_pairs={{0,1},{1,2},{2,3},{4,5},{5,6},{6,7},{8,9},{9,10},{10,11},{12,13},{... | collective-permute-start | bytes 15368 | tf_op jit(solution)/shard_map/ppermute | solution.py:15
  18.8 4.4 %collective-permute-start.3 = (bf16[10,256,1]{1,0,2:T(8,128)(2,1)S(1)}, bf16[10,256,1]{1,0,2:T(8,128)(2,1)S(1)}, u32[]{:S(2)}, u32[]{:S(2)}) collective-permute-start(bf16[10,256,1]{1,0,2:T(8,128)(2,1)S(1)} %copy.65), channel_id=1, source_target_pairs={{1,0},{2,1},{3,2},{5,4},{6,5},{7,6},{9,8},{10,9},{11,10},{13,12},{... | collective-permute-start | bytes 15368 | tf_op jit(solution)/shard_map/ppermute | solution.py:18
  82.1 1.0 copy-start.1
  83.5 9.5 %slice-start = ((f32[8,256,128]{1,2,0:T(8,128)}), f32[7,256,128]{1,2,0:T(8,128)S(1)}, s32[]{:S(2)}) async-start(f32[8,256,128]{1,2,0:T(8,128)} %copy-done.1), calls=%async_computation.2 | async-start | bytes 1835008 | tf_op jit(solution)/shard_map/slice | solution.py:49
  88.6 8.7 %all-to-all-start.1 = ((f32[4,1,2048]{2,1,0:T(1,128)}), f32[4,1,2048]{2,1,0:T(1,128)S(1)}, u32[]{:S(2)}, u32[]{:S(2)}) async-start(f32[4,1,2048]{2,1,0:T(1,128)} %reshape.27), calls=%async_computation.1 | async-start | bytes 65536 | tf_op jit(solution)/shard_map/all_to_all | solution.py:95
  93.0 1.2 copy-start.2
  94.2 0.9 slice-start.1
  97.3 32.8 %all-to-all-start = ((f32[4,1,256,128]{3,1,0,2:T(1,128)}), f32[4,1,256,128]{3,1,0,2:T(1,128)S(1)}, u32[]{:S(2)}, u32[]{:S(2)}) async-start(f32[4,1,256,128]{3,1,0,2:T(1,128)} %copy.73), calls=%async_computation | async-start | bytes 1048576 | tf_op jit(solution)/shard_map/all_to_all | solution.py:89
where the time goes:
time: 133 us; the launch traced here: 131 us
  other arithmetic  62.2 us (47%)
  starting transfers between devices  30.4 us (23%)
  local copies, waits for them, and re-layouts  21.1 us (16%)
  waiting for transfers between devices  16.5 us (12%)
    another operation x5, other arithmetic, cell_terms(): return (jnp.stack(colors), alpha)  56.7 us
    all_to_all x1, starting transfers between devices, body(): lax.all_to_all(partial_x[:, None], 'gx', split_axis=2, concat_axis=1, til...  15.1 us
    all_to_all x1, waiting for transfers between devices, body(): lax.all_to_all(partial_x[:, None], 'gx', split_axis=2, concat_axis=1, til...  15 us
    unnamed x20, local copies, waits for them, and re-layouts  8.6 us
    ppermute x2, starting transfers between devices, with_halo(): lax.ppermute(lax.slice_in_dim(block, block.shape[dim] - width, None, axis...  7.71 us
    slice x4, local copies, waits for them, and re-layouts, transfer_lookup(): outs[c] = outs[c] + weight * transfer[c, k]  6.95 us
    all_to_all x1, starting transfers between devices, body(): lax.all_to_all(partial_z[:, None], 'gz', split_axis=3, concat_axis=1, til...  4.41 us
    ppermute x2, starting transfers between devices, with_halo(): lax.ppermute(lax.slice_in_dim(block, 0, width, axis=dim), axis, backward)  3.21 us
  transfers between devices with their start and end apart: 6, of which 3 were waited for; matrix products, arithmetic and copies ran while one was open for 10% of the time, Pallas kernels for 0%

commit v1 on v0

v1 whole, which is shorter than its diff:
```python
import jax
import jax.numpy as jnp
from jax import lax
from jax.experimental import pallas as pl
from jax.experimental.pallas import tpu as pltpu
from jax.sharding import Mesh, PartitionSpec as P

MEMBRANE_COLOR = (0.9, 0.2, 0.1)
SYNAPSE_COLOR = (0.1, 0.8, 0.3)
LX, H, LZ = 8, 256, 128
KNOTS = 16
ROWS = 64
CHIPS = 32
F32, BF16 = jnp.float32, jnp.bfloat16
CODE_SCALE = 32760.0 / 12.0
CODE_MID = 13.0
LN2 = 0.6931471805599453
NN = (((1,), (0,)), ((), ()))
NT = (((1,), (1,)), ((), ()))
TN = (((0,), (0,)), ((), ()))


def mxu(a, b, dims):
    return lax.dot_general(a, b, dims, preferred_element_type=F32)


def iota(shape, dim):
    return lax.broadcasted_iota(jnp.int32, shape, dim)


def as_bf16(mask, value=1.0):
    return jnp.where(mask, value, 0.0).astype(BF16)


def split(value):
    high = value.astype(BF16)
    return high, (value - high.astype(F32)).astype(BF16)


def faces_kernel(pos, intensity, even_x, odd_x, face_a, face_b):
    core, odd_z = pos[0], pos[1] % 2
    even_x[...] = intensity[jnp.where(core == 0, LX - 1, 0)]
    odd_x[...] = intensity[jnp.where(core == 0, 0, LX - 1)]
    row, lane = iota((16, LZ), 0), iota((16, LZ), 1)
    lane_a = jnp.where(odd_z == 0, LZ - 1, 0)
    wanted = jnp.where(row < LX, lane_a, LZ - 1 - lane_a)
    total = jnp.zeros((16, H), F32)
    for x in range(LX):
        pick = as_bf16((row % LX == x) & (lane == wanted))
        total = total + mxu(pick, intensity[x], NT)
    face_a[...] = total[:LX]
    face_b[...] = total[LX:]


def brick_kernel(
    pos, inten, memb, syn, transfer, occ, even_x, odd_x, face_a, face_b,
    keep, send, z0, z1, z2, z3,
    pad, halo, table, occ_rows, dy, dz, prefix, depth, parts, zsum,
):
    core, zpos = pos[0], pos[1]
    odd_z = zpos % 2
    zero = jnp.zeros((16, LZ), BF16)
    for x in range(LX + 2):
        pad[x, 0:16, :] = zero
        pad[x, 16 + H :, :] = zero
    low = jnp.where(core == 0, odd_x[...].astype(F32), even_x[...].astype(F32))
    high = jnp.where(core == 0, even_x[...].astype(F32), odd_x[...].astype(F32))
    pad[0, 16 : 16 + H, :] = low.astype(BF16)
    pad[LX + 1, 16 : 16 + H, :] = high.astype(BF16)
    for x in range(LX):
        pad[x + 1, 16 : 16 + H, :] = inten[x]
    near = jnp.where(odd_z == 0, face_b[...], face_a[...])
    far = jnp.where(odd_z == 0, face_a[...], face_b[...])
    both = jnp.concatenate([near, far], axis=0).astype(BF16)
    halo[...] = mxu(both, as_bf16(iota((16, LZ), 0) == iota((16, LZ), 1)), TN).astype(BF16)
    table[...] = jnp.zeros((8, LZ), F32)
    table[0:4, 0:KNOTS] = transfer[...]
    spread = as_bf16(iota((KNOTS, LZ), 1) // 8 == iota((KNOTS, LZ), 0))
    occ_rows[...] = mxu(occ[0].astype(F32).astype(BF16), spread, NN)

    knots = table[...]
    steps = pltpu.roll(knots, LZ - 1, 1) - knots
    scale = 2.0 / (LX * 64)
    firsts, slopes = [], []
    for c in range(4):
        factor = scale if c == 3 else 1.0
        firsts.append(jnp.broadcast_to(knots[c : c + 1], (16, LZ)) * factor)
        slopes.append(jnp.broadcast_to(steps[c : c + 1], (16, LZ)) * factor)

    k, n = iota((2 * LZ, LZ), 0), iota((2 * LZ, LZ), 1)
    up = ((k < LZ) & (k == n + 1)) | ((k >= LZ + LX) & (k < LZ + 2 * LX) & (n == LZ - 1))
    down = ((k < LZ) & (k == n - 1)) | ((k >= LZ) & (k < LZ + LX) & (n == 0))
    diff_z = (jnp.where(up, 1.0, 0.0) - jnp.where(down, 1.0, 0.0)).astype(BF16)
    before = as_bf16(k % LZ < n)
    r, k2 = iota((ROWS, ROWS + 32), 0), iota((ROWS, ROWS + 32), 1)
    diff_y = (jnp.where(k2 == r + 17, 1.0, 0.0) - jnp.where(k2 == r + 15, 1.0, 0.0)).astype(BF16)
    lanes = iota((ROWS, LZ), 1)
    ones_row = iota((8, 2 * LZ), 0)

    def lookup(value):
        t = jnp.clip(value, 0.0, 1.0) * (KNOTS - 1.0)
        index = jnp.minimum(t.astype(jnp.int32), KNOTS - 2)
        return index, t - index.astype(F32)

    def interpolate(c, index, frac):
        first = jnp.take_along_axis(firsts[c], index, axis=1)
        return first + frac * jnp.take_along_axis(slopes[c], index, axis=1)

    def chunk(j, carry):
        base = pl.multiple_of(j * ROWS, ROWS)
        halo_rows = halo[pl.ds(base, ROWS), :]
        for x in range(LX):
            rows = pl.ds(pl.multiple_of(base + 16, 16), ROWS)
            mine = jnp.where((lanes == x) | (lanes == LX + x), halo_rows, jnp.zeros_like(halo_rows))
            left = jnp.concatenate([pad[x + 1, rows, :], mine], axis=1)
            dz[x] = mxu(left, diff_z, NN)
            dy[x] = mxu(diff_y, pad[x + 1, pl.ds(base, ROWS + 32), :], NN)
        for x in range(LX):
            for b in range(0, ROWS, 16):
                rows = pl.ds(pl.multiple_of(base + b, 16), 16)
                value = pad[x + 1, pl.ds(pl.multiple_of(base + 16 + b, 16), 16), :].astype(F32)
                index, frac = lookup(value)
                sigma = interpolate(3, index, frac)
                sigma = sigma + memb[x, rows, :].astype(F32) * (1.5 * scale)
                sigma = sigma + syn[x, rows, :].astype(F32) * (0.5 * scale)
                block = pl.ds(base // 8 + b // 8, 2)
                mask = occ_rows[block, :]
                mask = jnp.concatenate(
                    [jnp.broadcast_to(mask[0:1], (8, LZ)), jnp.broadcast_to(mask[1:2], (8, LZ))], axis=0
                )
                sigma = sigma * mask
                depth[x, b : b + 16, :] = sigma
                high, low = split(sigma)
                parts[3, x * ROWS + b : x * ROWS + b + 16, 0:LZ] = high
                parts[3, x * ROWS + b : x * ROWS + b + 16, LZ:] = low
        prefix[...] = mxu(parts[3], before, NN)
        for b in range(0, ROWS, 16):
            rows = pl.ds(pl.multiple_of(base + b, 16), 16)
            trans = jnp.ones((16, LZ), F32)
            total = jnp.zeros((16, LZ), F32)
            acc = [jnp.zeros((16, LZ), F32) for c in range(3)]
            for x in range(LX):
                here = pl.ds(pl.multiple_of(base + 16 + b, 16), 16)
                value = pad[x + 1, here, :].astype(F32)
                grad_x = pad[x + 2, here, :].astype(F32) - pad[x, here, :].astype(F32)
                grad_y, grad_z = dy[x, b : b + 16, :], dz[x, b : b + 16, :]
                norm = lax.rsqrt(grad_x * grad_x + grad_y * grad_y + grad_z * grad_z + 1.0) * 0.7
                shade_x = 0.3 + jnp.abs(grad_x) * norm
                shade_z = 0.3 + jnp.abs(grad_z) * norm
                sigma = depth[x, b : b + 16, :]
                passed = jnp.exp(-sigma)
                alpha = 1.0 - passed
                weight_x = trans * alpha
                trans = trans * passed
                total = total + sigma
                row = x * ROWS + b
                weight_z = jnp.exp(-prefix[row : row + 16, :]) * alpha
                index, frac = lookup(value)
                mem = memb[x, rows, :].astype(F32)
                sy = syn[x, rows, :].astype(F32)
                for c in range(3):
                    color = interpolate(c, index, frac)
                    own = mem * MEMBRANE_COLOR[c] + sy * SYNAPSE_COLOR[c]
                    acc[c] = acc[c] + weight_x * (shade_x * color + own)
                    high, low = split(weight_z * (shade_z * color + own))
                    parts[c, row : row + 16, 0:LZ] = high
                    parts[c, row : row + 16, LZ:] = low
            first_half = iota((8, LZ), 0) < 4
            for s in range(2):
                a, d, g, t = [v[8 * s : 8 * s + 8] for v in (*acc, total)]
                swap = lambda v: pltpu.roll(v, 4, 0)
                for_0 = (jnp.where(first_half, a, swap(d)), jnp.where(first_half, g, swap(t)))
                for_1 = (jnp.where(first_half, swap(a), d), jnp.where(first_half, swap(g), t))
                chip = base // 8 + b // 8 + s
                for i in range(2):
                    keep[chip, 8 * i : 8 * i + 8, :] = jnp.where(core == 0, for_0[i], for_1[i])
                    send[chip, 8 * i : 8 * i + 8, :] = jnp.where(core == 0, for_1[i], for_0[i])
        sums = jnp.zeros((8, LX * ROWS), F32)
        for c in range(4):
            sums = sums + mxu(as_bf16(ones_row == c), parts[c], NT)
        zsum[j] = sums
        return carry

    lax.fori_loop(0, H // ROWS, chunk, 0)
    for i, out in enumerate((z0, z1, z2, z3)):
        out[...] = zsum[zpos ^ i]


def depth_rows(b):
    return jnp.where(iota((8, LZ), 0) < 4, pltpu.roll(b, 4, 0), b)


def pair_kernel(pos, mine, other, code):
    core = pos[0]
    first_half = iota((8, LZ), 0) < 4

    def chip(i, carry):
        ma, mb = mine[i, 0:8, :], mine[i, 8:16, :]
        oa, ob = other[i, 0:8, :], other[i, 8:16, :]
        fa, fb = jnp.where(core == 0, ma, oa), jnp.where(core == 0, mb, ob)
        sa, sb = jnp.where(core == 0, oa, ma), jnp.where(core == 0, ob, mb)
        passed = jnp.exp(-depth_rows(fb))
        a = fa + passed * sa
        b = fb + jnp.where(first_half, passed, 1.0) * sb
        v = jnp.concatenate([a, b], axis=0)
        q = (jnp.log(jnp.maximum(v, 2.0**-25)) * (1.0 / LN2) + CODE_MID) * CODE_SCALE
        q = jnp.where(v > 2.0**-25, jnp.round(jnp.clip(q, -32766.0, 32766.0)), -32768.0)
        code[i] = q.astype(jnp.int32).astype(jnp.int16)
        return carry

    lax.fori_loop(0, CHIPS, chip, 0, unroll=4)


def final_kernel(pos, code, z0, z1, z2, z3, x_image, z_image, decoded):
    zpos = pos[1]

    def decode(i, carry):
        q = code[i].astype(F32)
        v = jnp.exp(q * (LN2 / CODE_SCALE) - CODE_MID * LN2)
        decoded[i] = jnp.where(q < -32767.0, 0.0, v)
        return carry

    lax.fori_loop(0, CHIPS, decode, 0, unroll=4)

    def chip(i, carry):
        a, b, deep = carry
        passed = jnp.exp(-deep)
        here = decoded[i, 8:16, :]
        return (a + passed * decoded[i, 0:8, :], b + passed * here, deep + depth_rows(here))

    empty = jnp.zeros((8, LZ), F32)
    a, b, deep = lax.fori_loop(0, CHIPS, chip, (empty, empty, empty), unroll=4)
    x_image[0] = a[0:4]
    x_image[1] = a[4:8]
    x_image[2] = b[0:4]
    x_image[3] = (1.0 - jnp.exp(-deep))[0:4]

    shape = (8, LX * ROWS)
    terms = [z[...] for z in (z0, z1, z2, z3)]
    depths = [jnp.broadcast_to(t[3:4], shape) for t in terms]
    image = jnp.zeros(shape, F32)
    whole = jnp.zeros(shape, F32)
    for i in range(4):
        ahead = jnp.zeros(shape, F32)
        for m in range(4):
            if m != i:
                ahead = ahead + jnp.where((zpos ^ m) < (zpos ^ i), depths[m], 0.0)
        image = image + jnp.exp(-ahead) * terms[i]
        whole = whole + depths[i]
    image = jnp.where(iota(shape, 0) == 3, 1.0 - jnp.exp(-whole), image)
    for x in range(LX):
        z_image[:, x, :] = image[0:4, x * ROWS : (x + 1) * ROWS]


def call(kernel, out_shape, scratch, cost, *operands):
    specs = [pl.BlockSpec(memory_space=pltpu.SMEM)] + [pl.BlockSpec(memory_space=pltpu.VMEM)] * (len(operands) - 1)
    return pl.pallas_call(
        kernel,
        out_shape=out_shape,
        in_specs=specs,
        out_specs=[pl.BlockSpec(memory_space=pltpu.VMEM)] * len(out_shape),
        scratch_shapes=scratch,
        compiler_params=pltpu.CompilerParams(vmem_limit_bytes=40 * 2**20),
        cost_estimate=pl.CostEstimate(flops=cost, bytes_accessed=2**20, transcendentals=0),
    )(*operands)


def body(intensity, membrane, synapse, transfer, occupancy):
    shape = jax.ShapeDtypeStruct
    core, zpos = lax.axis_index("core"), lax.axis_index("x")
    pos = jnp.stack([core, zpos]).astype(jnp.int32)
    layer, face = shape((H, LZ), BF16), shape((LX, H), F32)
    even_x, odd_x, face_a, face_b = call(
        faces_kernel, [layer, layer, face, face], [], 10**6, pos, intensity
    )
    gx = ("z", "y", "core")
    even = [p for i in range(0, 64, 2) for p in ((i, i + 1), (i + 1, i))]
    odd = [p for i in range(1, 63, 2) for p in ((i, i + 1), (i + 1, i))]
    odd_x = lax.ppermute(odd_x, gx, odd)
    face_a = lax.ppermute(face_a, "x", [(0, 1), (1, 0), (2, 3), (3, 2)])
    face_b = lax.ppermute(face_b, "x", [(1, 2), (2, 1)])
    even_x = lax.ppermute(even_x, gx, even)
    half = shape((CHIPS, 16, LZ), F32)
    zpart = shape((8, LX * ROWS), F32)
    scratch = [
        pltpu.VMEM((LX + 2, H + 32, LZ), BF16),
        pltpu.VMEM((H, LZ), BF16),
        pltpu.VMEM((8, LZ), F32),
        pltpu.VMEM((H // 8, LZ), F32),
        pltpu.VMEM((LX, ROWS, LZ), F32),
        pltpu.VMEM((LX, ROWS, LZ), F32),
        pltpu.VMEM((LX * ROWS, LZ), F32),
        pltpu.VMEM((LX, ROWS, LZ), F32),
        pltpu.VMEM((4, LX * ROWS, 2 * LZ), BF16),
        pltpu.VMEM((H // ROWS, 8, LX * ROWS), F32),
    ]
    keep, send, *zs = call(
        brick_kernel, [half, half] + [zpart] * 4, scratch, 10**8,
        pos, intensity, membrane, synapse, transfer, occupancy, even_x, odd_x, face_a, face_b,
    )
    other = lax.ppermute(send, "core", [(0, 1), (1, 0)])
    for i in range(1, 4):
        zs[i] = lax.ppermute(zs[i], "x", [(d, d ^ i) for d in range(4)])
    (code,) = call(pair_kernel, [shape((CHIPS, 16, LZ), jnp.int16)], [], 10**6, pos, keep, other)
    code = lax.all_to_all(code, ("z", "y"), split_axis=0, concat_axis=0, tiled=True)
    images = [shape((4, 4, LZ), F32), shape((4, LX, ROWS), F32)]
    scratch = [pltpu.VMEM((CHIPS, 16, LZ), F32)]
    return tuple(call(final_kernel, images, scratch, 10**6, pos, code, *zs))


def solution(mesh):
    split_mesh = Mesh(mesh.devices.reshape(8, 4, 2, 4), ("z", "y", "core", "x"))
    gx = ("z", "y", "core")
    brick = P(gx, None, "x")
    return jax.shard_map(
        body,
        mesh=split_mesh,
        in_specs=(brick, brick, brick, P(), brick),
        out_specs=(P(None, gx, "x"), P(None, gx, "x")),
        check_vma=False,
    )
```

time: 133 us -> 48.3 us (0.36)
  the two profiles are of different devices: /device:TPU:1 before, /device:TPU:4 now
where the time goes in v1:
time: 48.3 us; the launch traced here: 47.9 us
  starting transfers between devices  23 us (48%)
  Pallas kernels  10.6 us (22%)
  waiting for transfers between devices  10.3 us (21%)
  local copies, waits for them, and re-layouts  3.21 us (7%)
  between operations  0.71 us (1%)
    all_to_all x1, starting transfers between devices, body(): lax.all_to_all(code, ('z', 'y'), split_axis=0, concat_axis=0, tiled=True)  12.3 us
    pallas_call x4, Pallas kernels, call(): pl.pallas_call(kernel, out_shape=out_shape, in_specs=specs, out_specs=[pl...  10.6 us
    all_to_all x1, waiting for transfers between devices, body(): lax.all_to_all(code, ('z', 'y'), split_axis=0, concat_axis=0, tiled=True)  5.3 us
    ppermute x1, starting transfers between devices, body(): face_b = lax.ppermute(face_b, 'x', [(1, 2), (2, 1)])  3.64 us
    ppermute x3, starting transfers between devices, body(): zs[i] = lax.ppermute(zs[i], 'x', [(d, d ^ i) for d in range(4)])  3.57 us
    unnamed x13, local copies, waits for them, and re-layouts  3.21 us
    ppermute x1, waiting for transfers between devices, body(): face_b = lax.ppermute(face_b, 'x', [(1, 2), (2, 1)])  1.93 us
    ppermute x3, waiting for transfers between devices, body(): zs[i] = lax.ppermute(zs[i], 'x', [(d, d ^ i) for d in range(4)])  1.9 us
  transfers between devices with their start and end apart: 9, of which 5 were waited for; matrix products, arithmetic and copies ran while one was open for 0% of the time, Pallas kernels for 0%

profile of v1, /device:TPU:4, one launch (start us, length us, event | category | flops | bytes accessed | tf_op | source)
XLA Modules:
  0.0 47.9 jit_solution(2204562777336610681)
XLA Ops:
  0.6 0.1 pad_add_fusion.pos
  0.7 1.0 %copy-done = bf16[8,256,128]{2,1,0:T(8,128)(2,1)S(1)} copy-done((bf16[8,256,128]{2,1,0:T(8,128)(2,1)S(1)}, bf16[8,256,128]{2,1,0:T(8,128)(2,1)}, u32[]{:S(2)}) %copy-start) | copy-done | bytes 524312
  1.8 0.8 %shard_map.68 = (bf16[256,128]{1,0:T(8,128)(2,1)S(1)}, bf16[256,128]{1,0:T(8,128)(2,1)S(1)}, f32[8,256]{1,0:T(8,128)S(1)}, f32[8,256]{1,0:T(8,128)S(1)}) custom-call(s32[2]{0:T(128)S(1)} %pad_add_fusion.pos, bf16[8,256,128]{2,1,0:T(8,128)(2,1)S(1)} %copy-done), custom_call_target="tpu_custom_call" | custom-call | flops 1000000 | bytes 1048576 | tf_op jit(solution)/shard_map/pallas_call | solution.py:257
  2.5 0.7 %collective-permute-start.1 = (bf16[256,128]{1,0:T(8,128)(2,1)S(1)}, bf16[256,128]{1,0:T(8,128)(2,1)S(1)}, u32[]{:S(2)}, u32[]{:S(2)}) collective-permute-start(bf16[256,128]{1,0:T(8,128)(2,1)S(1)} %get-tuple-element.13), channel_id=1, source_target_pairs={{4,8},{8,4},{12,16},{16,12},{20,24},{24,20},{28,32},{32,28},{36,40... | collective-permute-start | bytes 196616 | tf_op jit(solution)/shard_map/ppermute | solution.py:279
  3.2 1.3 %collective-permute-start.2 = (f32[8,256]{1,0:T(8,128)S(1)}, f32[8,256]{1,0:T(8,128)S(1)}, u32[]{:S(2)}, u32[]{:S(2)}) collective-permute-start(f32[8,256]{1,0:T(8,128)S(1)} %get-tuple-element.14), channel_id=1, source_target_pairs={{0,1},{1,0},{2,3},{3,2},{4,5},{5,4},{6,7},{7,6},{8,9},{9,8},{10,11... | collective-permute-start | bytes 24584 | tf_op jit(solution)/shard_map/ppermute | solution.py:280
  4.5 3.6 %collective-permute-start.3 = (f32[8,256]{1,0:T(8,128)S(1)}, f32[8,256]{1,0:T(8,128)S(1)}, u32[]{:S(2)}, u32[]{:S(2)}) collective-permute-start(f32[8,256]{1,0:T(8,128)S(1)} %get-tuple-element.15), channel_id=1, source_target_pairs={{1,2},{2,1},{5,6},{6,5},{9,10},{10,9},{13,14},{14,13},{17,18},{18,... | collective-permute-start | bytes 24584 | tf_op jit(solution)/shard_map/ppermute | solution.py:281
  8.2 0.1 copy.7.occ
  8.2 1.9 %collective-permute-done.3.face_b = f32[8,256]{1,0:T(8,128)S(1)} collective-permute-done((f32[8,256]{1,0:T(8,128)S(1)}, f32[8,256]{1,0:T(8,128)S(1)}, u32[]{:S(2)}, u32[]{:S(2)}) %collective-permute-start.3) | collective-permute-done | bytes 8224 | tf_op jit(solution)/shard_map/ppermute | solution.py:281
  10.2 0.0 collective-permute-done.even_x
  10.2 0.0 copy-start.2
  10.2 1.0 %copy-done.2 = bf16[8,256,128]{2,1,0:T(8,128)(2,1)S(1)} copy-done((bf16[8,256,128]{2,1,0:T(8,128)(2,1)S(1)}, bf16[8,256,128]{2,1,0:T(8,128)(2,1)}, u32[]{:S(2)}) %copy-start.2) | copy-done | bytes 524312
  11.2 1.0 %copy-done.3 = bf16[8,256,128]{2,1,0:T(8,128)(2,1)S(1)} copy-done((bf16[8,256,128]{2,1,0:T(8,128)(2,1)S(1)}, bf16[8,256,128]{2,1,0:T(8,128)(2,1)}, u32[]{:S(2)}) %copy-start.3) | copy-done | bytes 524312
  12.3 6.8 %shard_map.69 = (f32[32,16,128]{2,1,0:T(8,128)S(1)}, f32[32,16,128]{2,1,0:T(8,128)S(1)}, f32[8,512]{1,0:T(8,128)S(1)}, f32[8,512]{1,0:T(8,128)S(1)}, f32[8,512]{1,0:T(8,128)S(1)}, /*index=5*/f32[8,512]{1,0:T(8,128)S(1)}) custom-call(s32[2]{0:T(128)S(1)} %pad_add_fusion.pos, bf16[8,256,128]{2,1,0:T(8,128)(2,1)S(1)} %copy-done.1, ...), custom_call_target="tpu_custom_call" | custom-call | flops 100000000 | bytes 1048576 | tf_op jit(solution)/shard_map/pallas_call | solution.py:257
  19.1 1.6 %collective-permute-start.4 = (f32[32,16,128]{2,1,0:T(8,128)S(1)}, f32[32,16,128]{2,1,0:T(8,128)S(1)}, u32[]{:S(2)}, u32[]{:S(2)}) collective-permute-start(f32[32,16,128]{2,1,0:T(8,128)S(1)} %get-tuple-element.17), channel_id=1, source_target_pairs={{0,4},{4,0},{1,5},{5,1},{2,6},{6,2},{3,7},{7,3},{8,12},{12,8},{9,1... | collective-permute-start | bytes 786440 | tf_op jit(solution)/shard_map/ppermute | solution.py:301
  20.6 1.2 %collective-permute-done.4.other = f32[32,16,128]{2,1,0:T(8,128)S(1)} collective-permute-done((f32[32,16,128]{2,1,0:T(8,128)S(1)}, f32[32,16,128]{2,1,0:T(8,128)S(1)}, u32[]{:S(2)}, u32[]{:S(2)}) %collective-permute-start.4) | collective-permute-done | bytes 262176 | tf_op jit(solution)/shard_map/ppermute | solution.py:301
  21.8 1.5 %shard_map.70 = s16[32,16,128]{2,1,0:T(8,128)(2,1)} custom-call(s32[2]{0:T(128)S(1)} %pad_add_fusion.pos, f32[32,16,128]{2,1,0:T(8,128)S(1)} %get-tuple-element.16.mine, f32[32,16,128]{2,1,0:T(8,128)S(1)} %collective-permute-done.4.other), custom_call_target="tpu_custom_call" | custom-call | flops 1000000 | bytes 1048576 | tf_op jit(solution)/shard_map/pallas_call | solution.py:257
  23.3 12.3 %all-to-all-start = ((s16[32,16,128]{2,1,0:T(8,128)(2,1)}), s16[32,16,128]{2,1,0:T(8,128)(2,1)S(1)}, u32[]{:S(2)}, u32[]{:S(2)}) async-start(s16[32,16,128]{2,1,0:T(8,128)(2,1)} %shard_map.70), calls=%async_computation | async-start | bytes 262144 | tf_op jit(solution)/shard_map/all_to_all | solution.py:305
  35.6 0.1 collective-permute-start.5
  35.7 1.5 %collective-permute-start.6 = (f32[8,512]{1,0:T(8,128)S(1)}, f32[8,512]{1,0:T(8,128)S(1)}, u32[]{:S(2)}, u32[]{:S(2)}) collective-permute-start(f32[8,512]{1,0:T(8,128)S(1)} %get-tuple-element.20), channel_id=1, source_target_pairs={{0,2},{1,3},{2,0},{3,1},{4,6},{5,7},{6,4},{7,5},{8,10},{9,11},{10,... | collective-permute-start | bytes 49160 | tf_op jit(solution)/shard_map/ppermute | solution.py:303
  37.2 2.0 %collective-permute-start.7 = (f32[8,512]{1,0:T(8,128)S(1)}, f32[8,512]{1,0:T(8,128)S(1)}, u32[]{:S(2)}, u32[]{:S(2)}) collective-permute-start(f32[8,512]{1,0:T(8,128)S(1)} %get-tuple-element.21), channel_id=1, source_target_pairs={{0,3},{1,2},{2,1},{3,0},{4,7},{5,6},{6,5},{7,4},{8,11},{9,10},{10,... | collective-permute-start | bytes 49160 | tf_op jit(solution)/shard_map/ppermute | solution.py:303
  39.2 0.2 collective-permute-done.5.z1
  39.4 1.7 %collective-permute-done.6.z2 = f32[8,512]{1,0:T(8,128)S(1)} collective-permute-done((f32[8,512]{1,0:T(8,128)S(1)}, f32[8,512]{1,0:T(8,128)S(1)}, u32[]{:S(2)}, u32[]{:S(2)}) %collective-permute-start.6) | collective-permute-done | bytes 16416 | tf_op jit(solution)/shard_map/ppermute | solution.py:303
  41.1 5.3 %all-to-all-done.code = s16[32,16,128]{2,1,0:T(8,128)(2,1)S(1)} async-done(((s16[32,16,128]{2,1,0:T(8,128)(2,1)}), s16[32,16,128]{2,1,0:T(8,128)(2,1)S(1)}, u32[]{:S(2)}, u32[]{:S(2)}) %all-to-all-start) | async-done | bytes 131104 | tf_op jit(solution)/shard_map/all_to_all | solution.py:305
  46.4 1.6 %shard_map.71 = (f32[4,4,128]{2,1,0:T(4,128)}, f32[4,8,64]{2,1,0:T(8,128)}) custom-call(s32[2]{0:T(128)S(1)} %pad_add_fusion.pos, s16[32,16,128]{2,1,0:T(8,128)(2,1)S(1)} %all-to-all-done.code, f32[8,512]{1,0:T(8,128)S(1)} %get-tuple-element.18.z0, f32[8,512]{1,0:T(8,128)S(1)} %collective-permute-done.5.z1, f32[8,512]{1,0:T(8,128)S(1)} %collective-permute-done.6.z2, ...), custom_call_target="tpu_custom_call" | custom-call | flops 1000000 | bytes 1048576 | tf_op jit(solution)/shard_map/pallas_call | solution.py:257
  (12 shorter events, 0.0 us)
Async XLA Ops:
  0.7 1.0 %copy-start = (bf16[8,256,128]{2,1,0:T(8,128)(2,1)S(1)}, bf16[8,256,128]{2,1,0:T(8,128)(2,1)}, u32[]{:S(2)}) copy-start(bf16[8,256,128]{2,1,0:T(8,128)(2,1)} %inten.1) | copy-start | bytes 1572868
  1.8 6.4 %copy-start.5 = (s32[1,32,16]{1,2,0:T(8,128)S(1)}, s32[1,32,16]{1,2,0:T(8,128)}, u32[]{:S(2)}) copy-start(s32[1,32,16]{1,2,0:T(8,128)} %param.9) | copy-start | bytes 6148
  1.8 8.4 %copy-start.1 = (bf16[8,256,128]{2,1,0:T(8,128)(2,1)S(1)}, bf16[8,256,128]{2,1,0:T(8,128)(2,1)}, u32[]{:S(2)}) copy-start(bf16[8,256,128]{2,1,0:T(8,128)(2,1)} %inten.1) | copy-start | bytes 1572868
  2.5 7.6 %collective-permute-start = (bf16[256,128]{1,0:T(8,128)(2,1)S(1)}, bf16[256,128]{1,0:T(8,128)(2,1)S(1)}, u32[]{:S(2)}, u32[]{:S(2)}) collective-permute-start(bf16[256,128]{1,0:T(8,128)(2,1)S(1)} %get-tuple-element.12), channel_id=1, source_target_pairs={{0,4},{4,0},{8,12},{12,8},{16,20},{20,16},{24,28},{28,24},{32,36},... | collective-permute-start | bytes 196616 | tf_op jit(solution)/shard_map/ppermute | solution.py:282
  2.5 7.6 %collective-permute-start.1 = (bf16[256,128]{1,0:T(8,128)(2,1)S(1)}, bf16[256,128]{1,0:T(8,128)(2,1)S(1)}, u32[]{:S(2)}, u32[]{:S(2)}) collective-permute-start(bf16[256,128]{1,0:T(8,128)(2,1)S(1)} %get-tuple-element.13), channel_id=1, source_target_pairs={{4,8},{8,4},{12,16},{16,12},{20,24},{24,20},{28,32},{32,28},{36,40... | collective-permute-start | bytes 196616 | tf_op jit(solution)/shard_map/ppermute | solution.py:279
  3.2 5.0 %collective-permute-start.2 = (f32[8,256]{1,0:T(8,128)S(1)}, f32[8,256]{1,0:T(8,128)S(1)}, u32[]{:S(2)}, u32[]{:S(2)}) collective-permute-start(f32[8,256]{1,0:T(8,128)S(1)} %get-tuple-element.14), channel_id=1, source_target_pairs={{0,1},{1,0},{2,3},{3,2},{4,5},{5,4},{6,7},{7,6},{8,9},{9,8},{10,11... | collective-permute-start | bytes 24584 | tf_op jit(solution)/shard_map/ppermute | solution.py:280
  4.5 5.7 %copy-start.4 = (f32[4,16]{1,0:T(4,128)S(1)}, f32[4,16]{1,0:T(4,128)}, u32[]{:S(2)}) copy-start(f32[4,16]{1,0:T(4,128)} %transfer.1) | copy-start | bytes 772
  4.5 5.7 %collective-permute-start.3 = (f32[8,256]{1,0:T(8,128)S(1)}, f32[8,256]{1,0:T(8,128)S(1)}, u32[]{:S(2)}, u32[]{:S(2)}) collective-permute-start(f32[8,256]{1,0:T(8,128)S(1)} %get-tuple-element.15), channel_id=1, source_target_pairs={{1,2},{2,1},{5,6},{6,5},{9,10},{10,9},{13,14},{14,13},{17,18},{18,... | collective-permute-start | bytes 24584 | tf_op jit(solution)/shard_map/ppermute | solution.py:281
  10.2 1.0 %copy-start.2 = (bf16[8,256,128]{2,1,0:T(8,128)(2,1)S(1)}, bf16[8,256,128]{2,1,0:T(8,128)(2,1)}, u32[]{:S(2)}) copy-start(bf16[8,256,128]{2,1,0:T(8,128)(2,1)} %memb.1) | copy-start | bytes 1572868
  11.2 1.0 %copy-start.3 = (bf16[8,256,128]{2,1,0:T(8,128)(2,1)S(1)}, bf16[8,256,128]{2,1,0:T(8,128)(2,1)}, u32[]{:S(2)}) copy-start(bf16[8,256,128]{2,1,0:T(8,128)(2,1)} %syn.1) | copy-start | bytes 1572868
  19.1 2.7 %collective-permute-start.4 = (f32[32,16,128]{2,1,0:T(8,128)S(1)}, f32[32,16,128]{2,1,0:T(8,128)S(1)}, u32[]{:S(2)}, u32[]{:S(2)}) collective-permute-start(f32[32,16,128]{2,1,0:T(8,128)S(1)} %get-tuple-element.17), channel_id=1, source_target_pairs={{0,4},{4,0},{1,5},{5,1},{2,6},{6,2},{3,7},{7,3},{8,12},{12,8},{9,1... | collective-permute-start | bytes 786440 | tf_op jit(solution)/shard_map/ppermute | solution.py:301
  23.3 23.1 %all-to-all-start = ((s16[32,16,128]{2,1,0:T(8,128)(2,1)}), s16[32,16,128]{2,1,0:T(8,128)(2,1)S(1)}, u32[]{:S(2)}, u32[]{:S(2)}) async-start(s16[32,16,128]{2,1,0:T(8,128)(2,1)} %shard_map.70), calls=%async_computation | async-start | bytes 262144 | tf_op jit(solution)/shard_map/all_to_all | solution.py:305
  35.6 3.8 %collective-permute-start.5 = (f32[8,512]{1,0:T(8,128)S(1)}, f32[8,512]{1,0:T(8,128)S(1)}, u32[]{:S(2)}, u32[]{:S(2)}) collective-permute-start(f32[8,512]{1,0:T(8,128)S(1)} %get-tuple-element.19), channel_id=1, source_target_pairs={{0,1},{1,0},{2,3},{3,2},{4,5},{5,4},{6,7},{7,6},{8,9},{9,8},{10,11... | collective-permute-start | bytes 49160 | tf_op jit(solution)/shard_map/ppermute | solution.py:303
  35.7 5.4 %collective-permute-start.6 = (f32[8,512]{1,0:T(8,128)S(1)}, f32[8,512]{1,0:T(8,128)S(1)}, u32[]{:S(2)}, u32[]{:S(2)}) collective-permute-start(f32[8,512]{1,0:T(8,128)S(1)} %get-tuple-element.20), channel_id=1, source_target_pairs={{0,2},{1,3},{2,0},{3,1},{4,6},{5,7},{6,4},{7,5},{8,10},{9,11},{10,... | collective-permute-start | bytes 49160 | tf_op jit(solution)/shard_map/ppermute | solution.py:303
  37.2 3.9 %collective-permute-start.7 = (f32[8,512]{1,0:T(8,128)S(1)}, f32[8,512]{1,0:T(8,128)S(1)}, u32[]{:S(2)}, u32[]{:S(2)}) collective-permute-start(f32[8,512]{1,0:T(8,128)S(1)} %get-tuple-element.21), channel_id=1, source_target_pairs={{0,3},{1,2},{2,1},{3,0},{4,7},{5,6},{6,5},{7,4},{8,11},{9,10},{10,... | collective-permute-start | bytes 49160 | tf_op jit(solution)/shard_map/ppermute | solution.py:303

commit v2 on v1

v2 whole, which is shorter than its diff:
```python
import jax
import jax.numpy as jnp
from jax import lax
from jax.experimental import pallas as pl
from jax.experimental.pallas import tpu as pltpu
from jax.sharding import Mesh, PartitionSpec as P

MEMBRANE_COLOR = (0.9, 0.2, 0.1)
SYNAPSE_COLOR = (0.1, 0.8, 0.3)
LX, H, LZ = 8, 256, 128
KNOTS = 16
ROWS = 64
CHIPS = 32
WIDE = 52 * 2**20
F32, BF16 = jnp.float32, jnp.bfloat16
CODE_SCALE = 32760.0 / 12.0
CODE_MID = 13.0
LN2 = 0.6931471805599453
NN = (((1,), (0,)), ((), ()))
NT = (((1,), (1,)), ((), ()))
TN = (((0,), (0,)), ((), ()))


def mxu(a, b, dims):
    return lax.dot_general(a, b, dims, preferred_element_type=F32)


def iota(shape, dim):
    return lax.broadcasted_iota(jnp.int32, shape, dim)


def as_bf16(mask, value=1.0):
    return jnp.where(mask, value, 0.0).astype(BF16)


def split(value):
    high = value.astype(BF16)
    return high, (value - high.astype(F32)).astype(BF16)


def faces_kernel(
    pos, inten_hbm, memb_hbm, syn_hbm, transfer_hbm,
    even_x, odd_x, face_a, face_b, intensity, memb, syn, transfer, sems,
):
    pairs = ((inten_hbm, intensity), (memb_hbm, memb), (syn_hbm, syn), (transfer_hbm, transfer))
    copies = [pltpu.make_async_copy(a, b, sems.at[i]) for i, (a, b) in enumerate(pairs)]
    for copy in copies:
        copy.start()
    copies[0].wait()
    core, odd_z = pos[0], pos[1] % 2
    even_x[...] = intensity[jnp.where(core == 0, LX - 1, 0)]
    odd_x[...] = intensity[jnp.where(core == 0, 0, LX - 1)]
    row, lane = iota((16, LZ), 0), iota((16, LZ), 1)
    lane_a = jnp.where(odd_z == 0, LZ - 1, 0)
    wanted = jnp.where(row < LX, lane_a, LZ - 1 - lane_a)
    total = jnp.zeros((16, H), F32)
    for x in range(LX):
        pick = as_bf16((row % LX == x) & (lane == wanted))
        total = total + mxu(pick, intensity[x], NT)
    face_a[...] = total[:LX]
    face_b[...] = total[LX:]
    for copy in copies[1:]:
        copy.wait()


def lookup(value):
    t = jnp.clip(value, 0.0, 1.0) * (KNOTS - 1.0)
    index = jnp.minimum(t.astype(jnp.int32), KNOTS - 2)
    return index, t - index.astype(F32)


def gather(table, index):
    numbers = lax.GatherDimensionNumbers(
        offset_dims=(), collapsed_slice_dims=(1,), start_index_map=(1,),
        operand_batching_dims=(0,), start_indices_batching_dims=(0,),
    )
    return lax.gather(
        table, index[..., None], numbers, (1, 1), mode=lax.GatherScatterMode.PROMISE_IN_BOUNDS
    )


def knot_tables(transfer, table, channels, factor):
    table[...] = jnp.zeros((8, LZ), F32)
    table[0:4, 0:KNOTS] = transfer[...] * factor
    knots = table[...]
    steps = pltpu.roll(knots, LZ - 1, 1) - knots
    return [
        (jnp.broadcast_to(knots[c : c + 1], (16, LZ)), jnp.broadcast_to(steps[c : c + 1], (16, LZ)))
        for c in channels
    ]


def interpolate(pair, index, frac):
    return gather(pair[0], index) + frac * gather(pair[1], index)


def depth_kernel(
    inten, memb, syn, transfer, occ,
    weight_x, weight_z, steep, spot, along, total_x, total_z,
    table, occ_rows, sigma, parts,
):
    scale = -2.0 / (LX * 64) / LN2
    (knots,) = knot_tables(transfer, table, (3,), scale)
    spread = as_bf16(iota((KNOTS, LZ), 1) // 8 == iota((KNOTS, LZ), 0))
    occ_rows[...] = mxu(occ[0].astype(F32).astype(BF16), spread, NN)
    r, k = iota((H, H), 0), iota((H, H), 1)
    diff_y = (jnp.where(k == r + 1, 1.0, 0.0) - jnp.where(k == r - 1, 1.0, 0.0)).astype(BF16)
    k, n = iota((2 * LZ, LZ), 0), iota((2 * LZ, LZ), 1)
    before = as_bf16(k % LZ < n)
    ones = jnp.ones((8, 2 * LZ), BF16)
    for x in range(LX):
        grad_y = mxu(diff_y, inten[x], NN)
        steep[x] = grad_y * grad_y + 1.0
    for j in range(H // ROWS):
        buf = j % 2
        for b in range(0, ROWS, 16):
            rows = pl.ds(j * ROWS + b, 16)
            block = (j * ROWS + b) // 8
            mask = jnp.concatenate(
                [jnp.broadcast_to(occ_rows[block + i : block + i + 1, :], (8, LZ)) for i in range(2)], axis=0
            )
            total = jnp.zeros((16, LZ), F32)
            trans = jnp.ones((16, LZ), F32)
            for x in range(LX):
                index, frac = lookup(inten[x, rows, :].astype(F32))
                spot[x, rows, :] = index
                along[x, rows, :] = frac
                depth = interpolate(knots, index, frac)
                depth = depth + memb[x, rows, :].astype(F32) * (1.5 * scale)
                depth = (depth + syn[x, rows, :].astype(F32) * (0.5 * scale)) * mask
                high, low = split(depth)
                row = x * ROWS + b
                parts[buf, row : row + 16, 0:LZ] = high
                parts[buf, row : row + 16, LZ:] = low
                passed = jnp.exp2(depth)
                alpha = 1.0 - passed
                sigma[buf, row : row + 16, :] = alpha
                weight_x[x, rows, :] = trans * alpha
                trans = trans * passed
                total = total + depth
            total_x[rows, :] = total
        prefix = mxu(parts[buf], before, NN)
        for x in range(LX):
            here = slice(x * ROWS, x * ROWS + ROWS)
            weight_z[x, j * ROWS : (j + 1) * ROWS, :] = jnp.exp2(prefix[here]) * sigma[buf, here, :]
        total_z[j] = mxu(ones, parts[buf], NT)


def shade_kernel(
    pos, inten, memb, syn, transfer, weight_x, weight_z, steep, spot, along, total_x, total_z,
    even_x, odd_x, face_a, face_b,
    keep, send, z_keep, z_send,
    pad, halo, table, left, dz, parts, zsum,
):
    core, zpos = pos[0], pos[1]
    odd_z = zpos % 2
    gx = pos[2]
    low = jnp.where(core == 0, odd_x[...].astype(F32), even_x[...].astype(F32))
    high = jnp.where(core == 0, even_x[...].astype(F32), odd_x[...].astype(F32))
    pad[0] = jnp.where(gx == 0, 0.0, low)
    pad[1] = jnp.where(gx == 63, 0.0, high)
    near = jnp.where(zpos == 0, 0.0, jnp.where(odd_z == 0, face_b[...], face_a[...]))
    far = jnp.where(zpos == 3, 0.0, jnp.where(odd_z == 0, face_a[...], face_b[...]))
    both = jnp.concatenate([near, far], axis=0).astype(BF16)
    halo[...] = mxu(both, as_bf16(iota((16, LZ), 0) == iota((16, LZ), 1)), TN).astype(BF16)
    knots = knot_tables(transfer, table, (0, 1, 2), 1.0)
    k, n = iota((2 * LZ, LZ), 0), iota((2 * LZ, LZ), 1)
    up = ((k < LZ) & (k == n + 1)) | ((k >= LZ + LX) & (k < LZ + 2 * LX) & (n == LZ - 1))
    down = ((k < LZ) & (k == n - 1)) | ((k >= LZ) & (k < LZ + LX) & (n == 0))
    diff_z = (jnp.where(up, 1.0, 0.0) - jnp.where(down, 1.0, 0.0)).astype(BF16)
    lanes = iota((ROWS, LZ), 1)
    ones_row = iota((8, 2 * LZ), 0)
    first_half = iota((8, LZ), 0) < 4

    for j in range(H // ROWS):
        buf = j % 2
        base = j * ROWS
        halo_rows = halo[base : base + ROWS, :]
        for x in range(LX):
            mine = jnp.where((lanes == x) | (lanes == LX + x), halo_rows, jnp.zeros_like(halo_rows))
            left[buf, x * ROWS : (x + 1) * ROWS, 0:LZ] = inten[x, base : base + ROWS, :]
            left[buf, x * ROWS : (x + 1) * ROWS, LZ:] = mine
        dz[buf] = mxu(left[buf], diff_z, NN)
        for b in range(0, ROWS, 16):
            rows = pl.ds(base + b, 16)
            acc = [jnp.zeros((16, LZ), F32) for c in range(3)]
            values = [pad[0, rows, :]] + [inten[x, rows, :].astype(F32) for x in range(LX)] + [pad[1, rows, :]]
            for x in range(LX):
                row = x * ROWS + b
                grad_x = values[x + 2] - values[x]
                grad_z = dz[buf, row : row + 16, :]
                norm = lax.rsqrt(grad_x * grad_x + (grad_z * grad_z + steep[x, rows, :])) * 0.7
                shade_x = 0.3 + jnp.abs(grad_x) * norm
                shade_z = 0.3 + jnp.abs(grad_z) * norm
                wx, wz = weight_x[x, rows, :], weight_z[x, rows, :]
                index, frac = spot[x, rows, :], along[x, rows, :]
                mem = memb[x, rows, :].astype(F32)
                sy = syn[x, rows, :].astype(F32)
                for c in range(3):
                    color = interpolate(knots[c], index, frac)
                    own = mem * MEMBRANE_COLOR[c] + sy * SYNAPSE_COLOR[c]
                    acc[c] = acc[c] + wx * (shade_x * color + own)
                    high, low = split(wz * (shade_z * color + own))
                    parts[buf, c, row : row + 16, 0:LZ] = high
                    parts[buf, c, row : row + 16, LZ:] = low
            total = -total_x[rows, :]
            for s in range(2):
                a, d, g, t = [v[8 * s : 8 * s + 8] for v in (*acc, total)]
                swap = lambda v: pltpu.roll(v, 4, 0)
                for_0 = (jnp.where(first_half, a, swap(d)), jnp.where(first_half, g, swap(t)))
                for_1 = (jnp.where(first_half, swap(a), d), jnp.where(first_half, swap(g), t))
                chip = (base + b) // 8 + s
                for i in range(2):
                    keep[chip, 8 * i : 8 * i + 8, :] = jnp.where(core == 0, for_0[i], for_1[i])
                    send[chip, 8 * i : 8 * i + 8, :] = jnp.where(core == 0, for_1[i], for_0[i])
        sums = jnp.where(iota((8, LX * ROWS), 0) % 4 == 3, -total_z[j], 0.0)
        for c in range(3):
            sums = sums + mxu(as_bf16(ones_row % 4 == c), parts[buf, c], NT)
        zsum[j] = sums
    for out, chip in ((z_keep, zpos), (z_send, zpos ^ 1)):
        out[...] = jnp.where(iota((8, LX * ROWS), 0) < 4, zsum[chip], zsum[3 - chip])


def depth_rows(b):
    return jnp.where(iota((8, LZ), 0) < 4, pltpu.roll(b, 4, 0), b)


def z_rows(z):
    upper = iota(z.shape, 0) < 4
    return jnp.where(upper, jnp.broadcast_to(z[3:4], z.shape), jnp.broadcast_to(z[7:8], z.shape))


def z_merge(first, second):
    depth_row = iota(first.shape, 0) % 4 == 3
    return first + jnp.where(depth_row, 1.0, jnp.exp2(-z_rows(first))) * second


def pair_kernel(pos, mine, other, z_mine, z_other, code, z_pair):
    core = pos[0]
    even = pos[1] % 2 == 0
    zm, zo = z_mine[...], z_other[...]
    z_pair[...] = z_merge(jnp.where(even, zm, zo), jnp.where(even, zo, zm))
    first_half = iota((8, LZ), 0) < 4
    for i in range(CHIPS):
        ma, mb = mine[i, 0:8, :], mine[i, 8:16, :]
        oa, ob = other[i, 0:8, :], other[i, 8:16, :]
        fa, fb = jnp.where(core == 0, ma, oa), jnp.where(core == 0, mb, ob)
        sa, sb = jnp.where(core == 0, oa, ma), jnp.where(core == 0, ob, mb)
        passed = jnp.exp2(-depth_rows(fb))
        a = fa + passed * sa
        b = fb + jnp.where(first_half, passed, 1.0) * sb
        v = jnp.concatenate([a, b], axis=0)
        q = jnp.log2(jnp.maximum(v, 2.0**-25)) * CODE_SCALE + (CODE_MID * CODE_SCALE)
        q = jnp.where(v > 2.0**-25, jnp.round(jnp.minimum(q, 32766.0)), -32768.0)
        code[i] = q.astype(jnp.int32).astype(jnp.int16)


def final_kernel(pos, code, z_mine, z_other, x_image, z_image):
    front = pos[1] < 2
    a = b = deep = jnp.zeros((8, LZ), F32)
    for i in range(CHIPS):
        q = code[i].astype(F32)
        v = jnp.exp2(q * (1.0 / CODE_SCALE) - CODE_MID)
        v = jnp.where(q < -32767.0, 0.0, v)
        passed = jnp.exp2(-deep)
        a = a + passed * v[0:8]
        b = b + passed * v[8:16]
        deep = deep + depth_rows(v[8:16])
    x_image[0] = a[0:4]
    x_image[1] = a[4:8]
    x_image[2] = b[0:4]
    x_image[3] = (1.0 - jnp.exp2(-deep))[0:4]

    zm, zo = z_mine[...], pltpu.roll(z_other[...], 4, 0)
    image = z_merge(jnp.where(front, zm, zo), jnp.where(front, zo, zm))
    image = jnp.where(iota(image.shape, 0) == 3, 1.0 - jnp.exp2(-image), image)
    for x in range(LX):
        z_image[:, x, :] = image[0:4, x * ROWS : (x + 1) * ROWS]


def call(kernel, out_shape, scratch, cost, *operands, wide=False):
    specs = [
        pl.BlockSpec(memory_space=pltpu.SMEM if a.shape == (3,) else pl.ANY if wide else pltpu.VMEM)
        for a in operands
    ]
    return pl.pallas_call(
        kernel,
        out_shape=out_shape,
        in_specs=specs,
        out_specs=[pl.BlockSpec(memory_space=pltpu.VMEM)] * len(out_shape),
        scratch_shapes=scratch,
        compiler_params=pltpu.CompilerParams(vmem_limit_bytes=WIDE if wide else 32 * 2**20),
        cost_estimate=pl.CostEstimate(flops=cost, bytes_accessed=2**20, transcendentals=0),
    )(*operands)


LAYER, FACE = jax.ShapeDtypeStruct((H, LZ), BF16), jax.ShapeDtypeStruct((LX, H), F32)
BRICK = jax.ShapeDtypeStruct((LX, H, LZ), F32)
HALF = jax.ShapeDtypeStruct((CHIPS, 16, LZ), F32)
ZPART = jax.ShapeDtypeStruct((8, LX * ROWS), F32)
IMAGES = [jax.ShapeDtypeStruct((4, 4, LZ), F32), jax.ShapeDtypeStruct((4, LX, ROWS), F32)]
CODE = jax.ShapeDtypeStruct((CHIPS, 16, LZ), jnp.int16)


def faces(*operands):
    brick = jax.ShapeDtypeStruct((LX, H, LZ), BF16)
    outs = [LAYER, LAYER, FACE, FACE, brick, brick, brick, jax.ShapeDtypeStruct((4, KNOTS), F32)]
    return call(faces_kernel, outs, [pltpu.SemaphoreType.DMA((4,))], 10**6, *operands, wide=True)


def depths(intensity, membrane, synapse, transfer, occupancy):
    outs = [BRICK] * 3 + [jax.ShapeDtypeStruct((LX, H, LZ), jnp.int32), BRICK] + [
        jax.ShapeDtypeStruct((H, LZ), F32),
        jax.ShapeDtypeStruct((H // ROWS, 8, LX * ROWS), F32),
    ]
    scratch = [
        pltpu.VMEM((8, LZ), F32),
        pltpu.VMEM((H // 8, LZ), F32),
        pltpu.VMEM((2, LX * ROWS, LZ), F32),
        pltpu.VMEM((2, LX * ROWS, 2 * LZ), BF16),
    ]
    return call(depth_kernel, outs, scratch, 10**8, intensity, membrane, synapse, transfer, occupancy)


def shades(*operands):
    scratch = [
        pltpu.VMEM((2, H, LZ), F32),
        pltpu.VMEM((H, LZ), BF16),
        pltpu.VMEM((8, LZ), F32),
        pltpu.VMEM((2, LX * ROWS, 2 * LZ), BF16),
        pltpu.VMEM((2, LX * ROWS, LZ), F32),
        pltpu.VMEM((2, 3, LX * ROWS, 2 * LZ), BF16),
        pltpu.VMEM((H // ROWS, 8, LX * ROWS), F32),
    ]
    return call(shade_kernel, [HALF, HALF, ZPART, ZPART], scratch, 10**8, *operands)


def body(intensity, membrane, synapse, transfer, occupancy):
    gx = ("z", "y", "core")
    pos = jnp.stack([lax.axis_index("core"), lax.axis_index("x"), lax.axis_index(gx)]).astype(jnp.int32)
    even_x, odd_x, face_a, face_b, intensity, membrane, synapse, transfer = faces(
        pos, intensity, membrane, synapse, transfer
    )
    even = [p for i in range(0, 64, 2) for p in ((i, i + 1), (i + 1, i))]
    odd = [p for i in range(1, 64, 2) for p in ((i, (i + 1) % 64), ((i + 1) % 64, i))]
    odd_x = lax.ppermute(odd_x, gx, odd)
    face_a = lax.ppermute(face_a, "x", [(0, 1), (1, 0), (2, 3), (3, 2)])
    face_b = lax.ppermute(face_b, "x", [(1, 2), (2, 1), (3, 0), (0, 3)])
    even_x = lax.ppermute(even_x, gx, even)
    deep = depths(intensity, membrane, synapse, transfer, occupancy)
    keep, send, z_keep, z_send = shades(
        pos, intensity, membrane, synapse, transfer, *deep, even_x, odd_x, face_a, face_b
    )
    other = lax.ppermute(send, "core", [(0, 1), (1, 0)])
    z_other = lax.ppermute(z_send, "x", [(0, 1), (1, 0), (2, 3), (3, 2)])
    code, z_pair = call(pair_kernel, [CODE, ZPART], [], 10**6, pos, keep, other, z_keep, z_other)
    z_other = lax.ppermute(z_pair, "x", [(0, 3), (3, 0), (1, 2), (2, 1)])
    code = lax.all_to_all(code, ("z", "y"), split_axis=0, concat_axis=0, tiled=True)
    return tuple(call(final_kernel, IMAGES, [], 10**6, pos, code, z_pair, z_other))


def solution(mesh):
    split_mesh = Mesh(mesh.devices.reshape(8, 4, 2, 4), ("z", "y", "core", "x"))
    gx = ("z", "y", "core")
    brick = P(gx, None, "x")
    return jax.shard_map(
        body,
        mesh=split_mesh,
        in_specs=(brick, brick, brick, P(), brick),
        out_specs=(P(None, gx, "x"), P(None, gx, "x")),
        check_vma=False,
    )
```

time: 48.3 us -> 43.3 us (0.90)
  the two profiles are of different devices: /device:TPU:4 before, /device:TPU:1 now
where the time goes in v2:
time: 43.3 us; the launch traced here: 42.9 us
  starting transfers between devices  20.2 us (47%)
  Pallas kernels  10.9 us (25%)
  waiting for transfers between devices  10.3 us (24%)
  between operations  0.69 us (2%)
  local copies, waits for them, and re-layouts  0.68 us (2%)
    pallas_call x5, Pallas kernels, call(): pl.pallas_call(kernel, out_shape=out_shape, in_specs=specs, out_specs=[pl...  10.9 us
    ppermute x1, starting transfers between devices, body(): other = lax.ppermute(send, 'core', [(0, 1), (1, 0)])  8.58 us
    all_to_all x1, waiting for transfers between devices, body(): lax.all_to_all(code, ('z', 'y'), split_axis=0, concat_axis=0, tiled=True)  5.52 us
    all_to_all x1, starting transfers between devices, body(): lax.all_to_all(code, ('z', 'y'), split_axis=0, concat_axis=0, tiled=True)  3.85 us
    ppermute x1, starting transfers between devices, body(): even_x = lax.ppermute(even_x, gx, even)  3.33 us
    ppermute x1, waiting for transfers between devices, body(): z_other = lax.ppermute(z_send, 'x', [(0, 1), (1, 0), (2, 3), (3, 2)])  2.6 us
    ppermute x1, waiting for transfers between devices, body(): z_other = lax.ppermute(z_pair, 'x', [(0, 3), (3, 0), (1, 2), (2, 1)])  1.98 us
    ppermute x1, starting transfers between devices, body(): z_other = lax.ppermute(z_pair, 'x', [(0, 3), (3, 0), (1, 2), (2, 1)])  1.9 us
  transfers between devices with their start and end apart: 8, of which 4 were waited for; matrix products, arithmetic and copies ran while one was open for 0% of the time, Pallas kernels for 4%

profile of v2, /device:TPU:1, one launch (start us, length us, event | category | flops | bytes accessed | tf_op | source)
XLA Modules:
  0.0 42.9 jit_solution(2774294147886048618)
XLA Ops:
  0.6 0.1 pad_add_fusion.pos
  0.7 0.6 %copy-done = f32[4,16]{1,0:T(4,128)S(1)} copy-done((f32[4,16]{1,0:T(4,128)S(1)}, f32[4,16]{1,0:T(4,128)}, u32[]{:S(2)}) %copy-start) | copy-done | bytes 280
  1.3 1.9 %shard_map.68 = (bf16[256,128]{1,0:T(8,128)(2,1)S(1)}, bf16[256,128]{1,0:T(8,128)(2,1)S(1)}, f32[8,256]{1,0:T(8,128)S(1)}, f32[8,256]{1,0:T(8,128)S(1)}, bf16[8,...) custom-call(s32[3]{0:T(128)S(1)} %pad_add_fusion.pos, ...), custom_call_target="tpu_custom_call" | custom-call | flops 1000000 | bytes 1048576 | tf_op jit(solution)/shard_map/pallas_call | solution.py:286
  3.3 3.3 %collective-permute-start = (bf16[256,128]{1,0:T(8,128)(2,1)S(1)}, bf16[256,128]{1,0:T(8,128)(2,1)S(1)}, u32[]{:S(2)}, u32[]{:S(2)}) collective-permute-start(bf16[256,128]{1,0:T(8,128)(2,1)S(1)} %get-tuple-element.34), channel_id=1, source_target_pairs={{0,4},{4,0},{8,12},{12,8},{16,20},{20,16},{24,28},{28,24},{32,36},... | collective-permute-start | bytes 196616 | tf_op jit(solution)/shard_map/ppermute | solution.py:349
  6.6 0.0 collective-permute-start.1
  6.6 0.8 %collective-permute-start.2 = (f32[8,256]{1,0:T(8,128)S(1)}, f32[8,256]{1,0:T(8,128)S(1)}, u32[]{:S(2)}, u32[]{:S(2)}) collective-permute-start(f32[8,256]{1,0:T(8,128)S(1)} %get-tuple-element.36), channel_id=1, source_target_pairs={{0,1},{1,0},{2,3},{3,2},{4,5},{5,4},{6,7},{7,6},{8,9},{9,8},{10,11... | collective-permute-start | bytes 24584 | tf_op jit(solution)/shard_map/ppermute | solution.py:347
  7.3 1.8 %collective-permute-start.3 = (f32[8,256]{1,0:T(8,128)S(1)}, f32[8,256]{1,0:T(8,128)S(1)}, u32[]{:S(2)}, u32[]{:S(2)}) collective-permute-start(f32[8,256]{1,0:T(8,128)S(1)} %get-tuple-element.37), channel_id=1, source_target_pairs={{1,2},{2,1},{3,0},{0,3},{5,6},{6,5},{7,4},{4,7},{9,10},{10,9},{11,... | collective-permute-start | bytes 24584 | tf_op jit(solution)/shard_map/ppermute | solution.py:348
  9.2 0.1 copy.7.occ
  9.2 1.6 %shard_map.69 = (f32[8,256,128]{2,1,0:T(8,128)S(1)}, f32[8,256,128]{2,1,0:T(8,128)S(1)}, f32[8,256,128]{2,1,0:T(8,128)S(1)}, s32[8,256,128]{2,1,0:T(8,128)S(1)},...) custom-call(bf16[8,256,128]{2,1,0:T(8,128)(2,1)S(1)} %get-tuple-element.23.inten, ...), custom_call_target="tpu_custom_call" | custom-call | flops 100000000 | bytes 1048576 | tf_op jit(solution)/shard_map/pallas_call | solution.py:286
  10.9 0.0 collective-permute-done.2.face_a
  10.9 0.2 collective-permute-done.3.face_b
  11.1 0.0 collective-permute-done.even_x
  11.1 0.0 collective-permute-done.1.odd_x
  11.1 4.8 %shard_map.70 = (f32[32,16,128]{2,1,0:T(8,128)S(1)}, f32[32,16,128]{2,1,0:T(8,128)S(1)}, f32[8,512]{1,0:T(8,128)S(1)}, f32[8,512]{1,0:T(8,128)S(1)}) custom-call(s32[3]{0:T(128)S(1)} %pad_add_fusion.pos, bf16[8,256,128]{2,1,0:T(8,128)(2,1)S(1)} %get-tuple-element.23.inten, bf16[8,256,128]{2,1,0:T(8,128)(2,1)S(1)} %get-tuple-element.24.memb, ...), custom_call_target="tpu_custom_call" | custom-call | flops 100000000 | bytes 1048576 | tf_op jit(solution)/shard_map/pallas_call | solution.py:286
  15.8 8.6 %collective-permute-start.4 = (f32[32,16,128]{2,1,0:T(8,128)S(1)}, f32[32,16,128]{2,1,0:T(8,128)S(1)}, u32[]{:S(2)}, u32[]{:S(2)}) collective-permute-start(f32[32,16,128]{2,1,0:T(8,128)S(1)} %get-tuple-element.39), channel_id=1, source_target_pairs={{0,4},{4,0},{1,5},{5,1},{2,6},{6,2},{3,7},{7,3},{8,12},{12,8},{9,1... | collective-permute-start | bytes 786440 | tf_op jit(solution)/shard_map/ppermute | solution.py:354
  24.4 0.0 collective-permute-start.5
  24.4 2.6 %collective-permute-done.5.z_other = f32[8,512]{1,0:T(8,128)S(1)} collective-permute-done((f32[8,512]{1,0:T(8,128)S(1)}, f32[8,512]{1,0:T(8,128)S(1)}, u32[]{:S(2)}, u32[]{:S(2)}) %collective-permute-start.5) | collective-permute-done | bytes 16416 | tf_op jit(solution)/shard_map/ppermute | solution.py:355
  27.0 0.0 collective-permute-done.4.other
  27.0 1.4 %shard_map.71 = (s16[32,16,128]{2,1,0:T(8,128)(2,1)}, f32[8,512]{1,0:T(8,128)S(1)}) custom-call(s32[3]{0:T(128)S(1)} %pad_add_fusion.pos, f32[32,16,128]{2,1,0:T(8,128)S(1)} %get-tuple-element.38.mine, f32[32,16,128]{2,1,0:T(8,128)S(1)} %collective-permute-done.4.other, f32[8,512]{1,0:T(8,128)S(1)} %get-tuple-element.40.z_mine, ...), custom_call_target="tpu_custom_call" | custom-call | flops 1000000 | bytes 1048576 | tf_op jit(solution)/shard_map/pallas_call | solution.py:286
  28.4 3.8 %all-to-all-start = ((s16[32,16,128]{2,1,0:T(8,128)(2,1)}), s16[32,16,128]{2,1,0:T(8,128)(2,1)S(1)}, u32[]{:S(2)}, u32[]{:S(2)}) async-start(s16[32,16,128]{2,1,0:T(8,128)(2,1)} %get-tuple-element.42), calls=%async_computation | async-start | bytes 262144 | tf_op jit(solution)/shard_map/all_to_all | solution.py:358
  32.2 1.9 %collective-permute-start.6 = (f32[8,512]{1,0:T(8,128)S(1)}, f32[8,512]{1,0:T(8,128)S(1)}, u32[]{:S(2)}, u32[]{:S(2)}) collective-permute-start(f32[8,512]{1,0:T(8,128)S(1)} %get-tuple-element.43.z_mine), channel_id=1, source_target_pairs={{0,3},{3,0},{1,2},{2,1},{4,7},{7,4},{5,6},{6,5},{8,11},{11,8},{9,1... | collective-permute-start | bytes 49160 | tf_op jit(solution)/shard_map/ppermute | solution.py:357
  34.1 2.0 %collective-permute-done.6.z_other = f32[8,512]{1,0:T(8,128)S(1)} collective-permute-done((f32[8,512]{1,0:T(8,128)S(1)}, f32[8,512]{1,0:T(8,128)S(1)}, u32[]{:S(2)}, u32[]{:S(2)}) %collective-permute-start.6) | collective-permute-done | bytes 16416 | tf_op jit(solution)/shard_map/ppermute | solution.py:357
  36.1 5.5 %all-to-all-done.code = s16[32,16,128]{2,1,0:T(8,128)(2,1)S(1)} async-done(((s16[32,16,128]{2,1,0:T(8,128)(2,1)}), s16[32,16,128]{2,1,0:T(8,128)(2,1)S(1)}, u32[]{:S(2)}, u32[]{:S(2)}) %all-to-all-start) | async-done | bytes 131104 | tf_op jit(solution)/shard_map/all_to_all | solution.py:358
  41.6 1.3 %shard_map.72 = (f32[4,4,128]{2,1,0:T(4,128)}, f32[4,8,64]{2,1,0:T(8,128)}) custom-call(s32[3]{0:T(128)S(1)} %pad_add_fusion.pos, s16[32,16,128]{2,1,0:T(8,128)(2,1)S(1)} %all-to-all-done.code, f32[8,512]{1,0:T(8,128)S(1)} %get-tuple-element.43.z_mine, f32[8,512]{1,0:T(8,128)S(1)} %collective-permute-done.6.z_other), custom_call_target="tpu_custom_call" | custom-call | flops 1000000 | bytes 1048576 | tf_op jit(solution)/shard_map/pallas_call | solution.py:286
  (3 shorter events, 0.0 us)
Async XLA Ops:
  0.6 0.7 %copy-start = (f32[4,16]{1,0:T(4,128)S(1)}, f32[4,16]{1,0:T(4,128)}, u32[]{:S(2)}) copy-start(f32[4,16]{1,0:T(4,128)} %transfer_hbm.1) | copy-start | bytes 772
  1.3 7.8 %copy-start.1 = (s32[1,32,16]{1,2,0:T(8,128)S(1)}, s32[1,32,16]{1,2,0:T(8,128)}, u32[]{:S(2)}) copy-start(s32[1,32,16]{1,2,0:T(8,128)} %param.9) | copy-start | bytes 6148
  3.3 7.8 %collective-permute-start = (bf16[256,128]{1,0:T(8,128)(2,1)S(1)}, bf16[256,128]{1,0:T(8,128)(2,1)S(1)}, u32[]{:S(2)}, u32[]{:S(2)}) collective-permute-start(bf16[256,128]{1,0:T(8,128)(2,1)S(1)} %get-tuple-element.34), channel_id=1, source_target_pairs={{0,4},{4,0},{8,12},{12,8},{16,20},{20,16},{24,28},{28,24},{32,36},... | collective-permute-start | bytes 196616 | tf_op jit(solution)/shard_map/ppermute | solution.py:349
  6.6 4.5 %collective-permute-start.1 = (bf16[256,128]{1,0:T(8,128)(2,1)S(1)}, bf16[256,128]{1,0:T(8,128)(2,1)S(1)}, u32[]{:S(2)}, u32[]{:S(2)}) collective-permute-start(bf16[256,128]{1,0:T(8,128)(2,1)S(1)} %get-tuple-element.35), channel_id=1, source_target_pairs={{4,8},{8,4},{12,16},{16,12},{20,24},{24,20},{28,32},{32,28},{36,40... | collective-permute-start | bytes 196616 | tf_op jit(solution)/shard_map/ppermute | solution.py:346
  6.6 4.3 %collective-permute-start.2 = (f32[8,256]{1,0:T(8,128)S(1)}, f32[8,256]{1,0:T(8,128)S(1)}, u32[]{:S(2)}, u32[]{:S(2)}) collective-permute-start(f32[8,256]{1,0:T(8,128)S(1)} %get-tuple-element.36), channel_id=1, source_target_pairs={{0,1},{1,0},{2,3},{3,2},{4,5},{5,4},{6,7},{7,6},{8,9},{9,8},{10,11... | collective-permute-start | bytes 24584 | tf_op jit(solution)/shard_map/ppermute | solution.py:347
  7.3 3.7 %collective-permute-start.3 = (f32[8,256]{1,0:T(8,128)S(1)}, f32[8,256]{1,0:T(8,128)S(1)}, u32[]{:S(2)}, u32[]{:S(2)}) collective-permute-start(f32[8,256]{1,0:T(8,128)S(1)} %get-tuple-element.37), channel_id=1, source_target_pairs={{1,2},{2,1},{3,0},{0,3},{5,6},{6,5},{7,4},{4,7},{9,10},{10,9},{11,... | collective-permute-start | bytes 24584 | tf_op jit(solution)/shard_map/ppermute | solution.py:348
  15.8 11.2 %collective-permute-start.4 = (f32[32,16,128]{2,1,0:T(8,128)S(1)}, f32[32,16,128]{2,1,0:T(8,128)S(1)}, u32[]{:S(2)}, u32[]{:S(2)}) collective-permute-start(f32[32,16,128]{2,1,0:T(8,128)S(1)} %get-tuple-element.39), channel_id=1, source_target_pairs={{0,4},{4,0},{1,5},{5,1},{2,6},{6,2},{3,7},{7,3},{8,12},{12,8},{9,1... | collective-permute-start | bytes 786440 | tf_op jit(solution)/shard_map/ppermute | solution.py:354
  24.4 2.6 %collective-permute-start.5 = (f32[8,512]{1,0:T(8,128)S(1)}, f32[8,512]{1,0:T(8,128)S(1)}, u32[]{:S(2)}, u32[]{:S(2)}) collective-permute-start(f32[8,512]{1,0:T(8,128)S(1)} %get-tuple-element.41), channel_id=1, source_target_pairs={{0,1},{1,0},{2,3},{3,2},{4,5},{5,4},{6,7},{7,6},{8,9},{9,8},{10,11... | collective-permute-start | bytes 49160 | tf_op jit(solution)/shard_map/ppermute | solution.py:355
  28.4 13.3 %all-to-all-start = ((s16[32,16,128]{2,1,0:T(8,128)(2,1)}), s16[32,16,128]{2,1,0:T(8,128)(2,1)S(1)}, u32[]{:S(2)}, u32[]{:S(2)}) async-start(s16[32,16,128]{2,1,0:T(8,128)(2,1)} %get-tuple-element.42), calls=%async_computation | async-start | bytes 262144 | tf_op jit(solution)/shard_map/all_to_all | solution.py:358
  32.2 3.9 %collective-permute-start.6 = (f32[8,512]{1,0:T(8,128)S(1)}, f32[8,512]{1,0:T(8,128)S(1)}, u32[]{:S(2)}, u32[]{:S(2)}) collective-permute-start(f32[8,512]{1,0:T(8,128)S(1)} %get-tuple-element.43.z_mine), channel_id=1, source_target_pairs={{0,3},{3,0},{1,2},{2,1},{4,7},{7,4},{5,6},{6,5},{8,11},{11,8},{9,1... | collective-permute-start | bytes 49160 | tf_op jit(solution)/shard_map/ppermute | solution.py:357

commit v3 on v2

v3 whole, which is shorter than its diff:
```python
import jax
import jax.numpy as jnp
from jax import lax
from jax.experimental import pallas as pl
from jax.experimental.pallas import tpu as pltpu
from jax.sharding import Mesh, PartitionSpec as P

MEMBRANE_COLOR = (0.9, 0.2, 0.1)
SYNAPSE_COLOR = (0.1, 0.8, 0.3)
LX, H, LZ = 8, 256, 128
KNOTS = 16
ROWS = 64
CHIPS = 32
ACROSS = ()
WIDE = 52 * 2**20
F32, BF16 = jnp.float32, jnp.bfloat16
CODE_SCALE = 32760.0 / 12.0
CODE_MID = 13.0
LN2 = 0.6931471805599453
NN = (((1,), (0,)), ((), ()))
NT = (((1,), (1,)), ((), ()))
TN = (((0,), (0,)), ((), ()))


def mxu(a, b, dims):
    return lax.dot_general(a, b, dims, preferred_element_type=F32)


def iota(shape, dim):
    return lax.broadcasted_iota(jnp.int32, shape, dim)


def as_bf16(mask, value=1.0):
    return jnp.where(mask, value, 0.0).astype(BF16)


def split(value):
    high = value.astype(BF16)
    return high, (value - high.astype(F32)).astype(BF16)


def faces_kernel(
    pos, inten_hbm, memb_hbm, syn_hbm,
    odd_x, face_a, face_b, even_x, intensity, memb, syn, sems,
):
    pairs = ((inten_hbm, intensity), (memb_hbm, memb), (syn_hbm, syn))
    copies = [pltpu.make_async_copy(a, b, sems.at[i]) for i, (a, b) in enumerate(pairs)]
    for copy in copies:
        copy.start()
    copies[0].wait()
    core, odd_z = pos[0], pos[1] % 2
    even_x[...] = intensity[jnp.where(core == 0, LX - 1, 0)]
    odd_x[...] = intensity[jnp.where(core == 0, 0, LX - 1)]
    row, lane = iota((16, LZ), 0), iota((16, LZ), 1)
    lane_a = jnp.where(odd_z == 0, LZ - 1, 0)
    wanted = jnp.where(row < LX, lane_a, LZ - 1 - lane_a)
    total = jnp.zeros((16, H), F32)
    for x in range(LX):
        pick = as_bf16((row % LX == x) & (lane == wanted))
        total = total + mxu(pick, intensity[x], NT)
    face_a[...] = total[:LX]
    face_b[...] = total[LX:]
    for copy in copies[1:]:
        copy.wait()


def lookup(value):
    t = jnp.clip(value, 0.0, 1.0) * (KNOTS - 1.0)
    index = jnp.minimum(t.astype(jnp.int32), KNOTS - 2)
    return index, t - index.astype(F32)


def gather(table, index, dim):
    numbers = lax.GatherDimensionNumbers(
        offset_dims=(), collapsed_slice_dims=(dim,), start_index_map=(dim,),
        operand_batching_dims=(1 - dim,), start_indices_batching_dims=(1 - dim,),
    )
    return lax.gather(
        table, index[..., None], numbers, (1, 1), mode=lax.GatherScatterMode.PROMISE_IN_BOUNDS
    )


def knot_table(transfer, channel, factor, across):
    knots = transfer[...] * factor
    steps = pltpu.roll(knots, LZ - 1, 1) - knots
    out = []
    for values in (knots, steps):
        line = jnp.broadcast_to(values[channel : channel + 1], (8, LZ))
        if across:
            out.append(line)
            continue
        for first in (0, 8):
            own = jnp.where(iota((8, LZ), 1) == iota((8, LZ), 0) + first, line, 0.0)
            out.append(jnp.broadcast_to(jnp.sum(own, axis=1, keepdims=True), (8, LZ)))
    return out


def interpolate(tables, index, frac):
    halves = []
    for h in (slice(0, 8), slice(8, 16)):
        if len(tables) == 2:
            first, step = gather(tables[0], index[h], 1), gather(tables[1], index[h], 1)
        else:
            row, upper = index[h] & 7, index[h] >= 8
            first = jnp.where(upper, gather(tables[1], row, 0), gather(tables[0], row, 0))
            step = jnp.where(upper, gather(tables[3], row, 0), gather(tables[2], row, 0))
        halves.append(first + frac[h] * step)
    return jnp.concatenate(halves, axis=0)


def depth_kernel(
    inten, memb, syn, transfer, occ,
    weight_x, weight_z, steep, spot, along, tables, own_x, total_x, total_z,
    occ_rows, sigma, prefix, parts,
):
    scale = -2.0 / (LX * 64) / LN2
    dense = knot_table(transfer, 3, scale, False)
    for c in range(3):
        for i, table in enumerate(knot_table(transfer, c, 1.0, c in ACROSS)):
            tables[c, i] = table
    spread = as_bf16(iota((KNOTS, LZ), 1) // 8 == iota((KNOTS, LZ), 0))
    occ_rows[...] = mxu(occ[0].astype(F32).astype(BF16), spread, NN)
    r, k = iota((H, H), 0), iota((H, H), 1)
    diff_y = (jnp.where(k == r + 1, 1.0, 0.0) - jnp.where(k == r - 1, 1.0, 0.0)).astype(BF16)
    k, n = iota((2 * LZ, LZ), 0), iota((2 * LZ, LZ), 1)
    before = as_bf16(k % LZ < n)
    ones = jnp.ones((8, 2 * LZ), BF16)
    for x in range(LX):
        grad_y = mxu(diff_y, inten[x], NN)
        steep[x] = grad_y * grad_y + 1.0
    def cells(j):
        buf = j % 3
        for b in range(0, ROWS, 16):
            rows = pl.ds(j * ROWS + b, 16)
            block = (j * ROWS + b) // 8
            mask = jnp.concatenate(
                [jnp.broadcast_to(occ_rows[block + i : block + i + 1, :], (8, LZ)) for i in range(2)], axis=0
            )
            total = jnp.zeros((16, LZ), F32)
            trans = jnp.ones((16, LZ), F32)
            own_m = jnp.zeros((16, LZ), F32)
            own_s = jnp.zeros((16, LZ), F32)
            for x in range(LX):
                index, frac = lookup(inten[x, rows, :].astype(F32))
                spot[x, rows, :] = index
                along[x, rows, :] = frac
                mem = memb[x, rows, :].astype(F32)
                sy = syn[x, rows, :].astype(F32)
                depth = interpolate(dense, index, frac) + mem * (1.5 * scale)
                depth = (depth + sy * (0.5 * scale)) * mask
                high, low = split(depth)
                row = x * ROWS + b
                parts[buf, 0, row : row + 16, 0:LZ] = high
                parts[buf, 0, row : row + 16, LZ:] = low
                passed = jnp.exp2(depth)
                alpha = 1.0 - passed
                sigma[buf, row : row + 16, :] = alpha
                weight = trans * alpha
                weight_x[x, rows, :] = weight
                own_m = own_m + weight * mem
                own_s = own_s + weight * sy
                trans = trans * passed
                total = total + depth
            total_x[rows, :] = total
            own_x[0, rows, :] = own_m
            own_x[1, rows, :] = own_s
        prefix[buf] = mxu(parts[buf, 0], before, NN)

    def weights(j):
        buf = j % 3
        for x in range(LX):
            for b in range(0, ROWS, 16):
                rows = pl.ds(j * ROWS + b, 16)
                here = slice(x * ROWS + b, x * ROWS + b + 16)
                weight = jnp.exp2(prefix[buf, here, :]) * sigma[buf, here, :]
                weight_z[x, rows, :] = weight
                for i, probability in enumerate((memb, syn)):
                    high, low = split(weight * probability[x, rows, :].astype(F32))
                    parts[buf, 1 + i, here, 0:LZ] = high
                    parts[buf, 1 + i, here, LZ:] = low

    def sums(j):
        buf = j % 3
        deep, own_m, own_s = [mxu(ones, parts[buf, i], NT) for i in range(3)]
        channel = iota((8, LX * ROWS), 0) % 4
        rest = jnp.where(channel == 3, -deep, 0.0)
        for c in range(3):
            rest = jnp.where(channel == c, MEMBRANE_COLOR[c] * own_m + SYNAPSE_COLOR[c] * own_s, rest)
        total_z[j] = rest

    for step in range(H // ROWS + 2):
        if step < H // ROWS:
            cells(step)
        if 1 <= step <= H // ROWS:
            weights(step - 1)
        if step >= 2:
            sums(step - 2)


def shade_kernel(
    pos, inten, weight_x, weight_z, steep, spot, along, tables, own_x, total_x, total_z,
    odd_x, face_a, face_b, even_x,
    keep, send, z_keep, z_send,
    pad, halo, left, dz, parts, zsum, image,
):
    core, zpos = pos[0], pos[1]
    odd_z = zpos % 2
    gx = pos[2]
    low = jnp.where(core == 0, odd_x[...].astype(F32), even_x[...].astype(F32))
    high = jnp.where(core == 0, even_x[...].astype(F32), odd_x[...].astype(F32))
    pad[0] = jnp.where(gx == 0, 0.0, low)
    pad[1] = jnp.where(gx == 63, 0.0, high)
    near = jnp.where(zpos == 0, 0.0, jnp.where(odd_z == 0, face_b[...], face_a[...]))
    far = jnp.where(zpos == 3, 0.0, jnp.where(odd_z == 0, face_a[...], face_b[...]))
    both = jnp.concatenate([near, far], axis=0).astype(BF16)
    halo[...] = mxu(both, as_bf16(iota((16, LZ), 0) == iota((16, LZ), 1)), TN).astype(BF16)
    k, n = iota((2 * LZ, LZ), 0), iota((2 * LZ, LZ), 1)
    up = ((k < LZ) & (k == n + 1)) | ((k >= LZ + LX) & (k < LZ + 2 * LX) & (n == LZ - 1))
    down = ((k < LZ) & (k == n - 1)) | ((k >= LZ) & (k < LZ + LX) & (n == 0))
    diff_z = (jnp.where(up, 1.0, 0.0) - jnp.where(down, 1.0, 0.0)).astype(BF16)
    lanes = iota((ROWS, LZ), 1)
    ones_row = iota((8, 2 * LZ), 0)
    first_half = iota((8, LZ), 0) < 4
    knots = [[tables[c, i] for i in range(2 if c in ACROSS else 4)] for c in range(3)]

    def slopes(j):
        buf, base = j % 2, j * ROWS
        halo_rows = halo[base : base + ROWS, :]
        for x in range(LX):
            mine = jnp.where((lanes == x) | (lanes == LX + x), halo_rows, jnp.zeros_like(halo_rows))
            left[buf, x * ROWS : (x + 1) * ROWS, 0:LZ] = inten[x, base : base + ROWS, :]
            left[buf, x * ROWS : (x + 1) * ROWS, LZ:] = mine
        dz[buf] = mxu(left[buf], diff_z, NN)

    def cells(j, b):
        buf = j % 2
        rows = pl.ds(j * ROWS + b, 16)
        own_m, own_s = own_x[0, rows, :], own_x[1, rows, :]
        acc = [MEMBRANE_COLOR[c] * own_m + SYNAPSE_COLOR[c] * own_s for c in range(3)]
        values = [pad[0, rows, :]] + [inten[x, rows, :].astype(F32) for x in range(LX)] + [pad[1, rows, :]]
        for x in range(LX):
            row = x * ROWS + b
            grad_x = values[x + 2] - values[x]
            grad_z = dz[buf, row : row + 16, :]
            norm = lax.rsqrt(grad_x * grad_x + (grad_z * grad_z + steep[x, rows, :])) * 0.7
            lit_x = (0.3 + jnp.abs(grad_x) * norm) * weight_x[x, rows, :]
            lit_z = (0.3 + jnp.abs(grad_z) * norm) * weight_z[x, rows, :]
            index, frac = spot[x, rows, :], along[x, rows, :]
            for c in range(3):
                color = interpolate(knots[c], index, frac)
                acc[c] = acc[c] + lit_x * color
                high, low = split(lit_z * color)
                parts[buf, c, row : row + 16, 0:LZ] = high
                parts[buf, c, row : row + 16, LZ:] = low
        for c in range(3):
            image[c, rows, :] = acc[c]

    def sums(j, c):
        if c == 0:
            zsum[j] = total_z[j]
        zsum[j] += mxu(as_bf16(ones_row % 4 == c), parts[j % 2, c], NT)

    chunks = H // ROWS
    slopes(0)
    for j in range(chunks):
        for i, b in enumerate(range(0, ROWS, 16)):
            if i == 0 and j + 1 < chunks:
                slopes(j + 1)
            if i < 3 and j > 0:
                sums(j - 1, i)
            cells(j, b)
    for c in range(3):
        sums(chunks - 1, c)
    swap = lambda v: pltpu.roll(v, 4, 0)
    for first in range(0, CHIPS, 8):
        ready = []
        for chip in range(first, first + 8):
            rows = pl.ds(8 * chip, 8)
            a, d, g = [image[c, rows, :] for c in range(3)]
            t = -total_x[rows, :]
            for i, (p, q) in enumerate(((a, d), (g, t))):
                crossed = swap(jnp.where(first_half, q, p))
                for_0 = jnp.where(first_half, p, crossed)
                for_1 = jnp.where(first_half, crossed, q)
                ready.append((keep, chip, i, jnp.where(core == 0, for_0, for_1)))
                ready.append((send, chip, i, jnp.where(core == 0, for_1, for_0)))
        for out, chip, i, value in ready:
            out[chip, 8 * i : 8 * i + 8, :] = value
    for out, chip in ((z_keep, zpos), (z_send, zpos ^ 1)):
        out[...] = jnp.where(iota((8, LX * ROWS), 0) < 4, zsum[chip], zsum[3 - chip])


def depth_rows(b):
    return jnp.where(iota((8, LZ), 0) < 4, pltpu.roll(b, 4, 0), b)


def z_rows(z):
    upper = iota(z.shape, 0) < 4
    return jnp.where(upper, jnp.broadcast_to(z[3:4], z.shape), jnp.broadcast_to(z[7:8], z.shape))


def z_merge(first, second):
    depth_row = iota(first.shape, 0) % 4 == 3
    return first + jnp.where(depth_row, 1.0, jnp.exp2(-z_rows(first))) * second


def z_kernel(pos, z_mine, z_other, z_pair):
    even = pos[1] % 2 == 0
    zm, zo = z_mine[...], z_other[...]
    z_pair[...] = z_merge(jnp.where(even, zm, zo), jnp.where(even, zo, zm))


def pair_kernel(pos, mine, other, code):
    core = pos[0]
    first_half = iota((8, LZ), 0) < 4
    for i in range(CHIPS):
        ma, mb = mine[i, 0:8, :], mine[i, 8:16, :]
        oa, ob = other[i, 0:8, :], other[i, 8:16, :]
        fa, fb = jnp.where(core == 0, ma, oa), jnp.where(core == 0, mb, ob)
        sa, sb = jnp.where(core == 0, oa, ma), jnp.where(core == 0, ob, mb)
        passed = jnp.exp2(-depth_rows(fb))
        a = fa + passed * sa
        b = fb + jnp.where(first_half, passed, 1.0) * sb
        v = jnp.concatenate([a, b], axis=0)
        q = jnp.log2(jnp.maximum(v, 2.0**-25)) * CODE_SCALE + (CODE_MID * CODE_SCALE)
        q = jnp.where(v > 2.0**-25, jnp.round(jnp.minimum(q, 32766.0)), -32768.0)
        code[i] = q.astype(jnp.int32).astype(jnp.int16)


def final_kernel(pos, code, z_mine, z_other, x_image, z_image):
    front = pos[1] < 2
    a = b = deep = jnp.zeros((8, LZ), F32)
    for i in range(CHIPS):
        q = code[i].astype(F32)
        v = jnp.exp2(q * (1.0 / CODE_SCALE) - CODE_MID)
        v = jnp.where(q < -32767.0, 0.0, v)
        passed = jnp.exp2(-deep)
        a = a + passed * v[0:8]
        b = b + passed * v[8:16]
        deep = deep + depth_rows(v[8:16])
    x_image[0] = a[0:4]
    x_image[1] = a[4:8]
    x_image[2] = b[0:4]
    x_image[3] = (1.0 - jnp.exp2(-deep))[0:4]

    zm, zo = z_mine[...], pltpu.roll(z_other[...], 4, 0)
    image = z_merge(jnp.where(front, zm, zo), jnp.where(front, zo, zm))
    image = jnp.where(iota(image.shape, 0) == 3, 1.0 - jnp.exp2(-image), image)
    for x in range(LX):
        z_image[:, x, :] = image[0:4, x * ROWS : (x + 1) * ROWS]


def call(kernel, out_shape, scratch, cost, *operands, wide=False):
    specs = [
        pl.BlockSpec(memory_space=pltpu.SMEM if a.shape == (3,) else pl.ANY if wide else pltpu.VMEM)
        for a in operands
    ]
    return pl.pallas_call(
        kernel,
        out_shape=out_shape,
        in_specs=specs,
        out_specs=[pl.BlockSpec(memory_space=pltpu.VMEM)] * len(out_shape),
        scratch_shapes=scratch,
        compiler_params=pltpu.CompilerParams(vmem_limit_bytes=WIDE if wide else 32 * 2**20),
        cost_estimate=pl.CostEstimate(flops=cost, bytes_accessed=2**20, transcendentals=0),
    )(*operands)


LAYER, FACE = jax.ShapeDtypeStruct((H, LZ), BF16), jax.ShapeDtypeStruct((LX, H), F32)
BRICK = jax.ShapeDtypeStruct((LX, H, LZ), F32)
HALF = jax.ShapeDtypeStruct((CHIPS, 16, LZ), F32)
ZPART = jax.ShapeDtypeStruct((8, LX * ROWS), F32)
IMAGES = [jax.ShapeDtypeStruct((4, 4, LZ), F32), jax.ShapeDtypeStruct((4, LX, ROWS), F32)]
CODE = jax.ShapeDtypeStruct((CHIPS, 16, LZ), jnp.int16)


def faces(*operands):
    brick = jax.ShapeDtypeStruct((LX, H, LZ), BF16)
    outs = [LAYER, FACE, FACE, LAYER, brick, brick, brick]
    return call(faces_kernel, outs, [pltpu.SemaphoreType.DMA((3,))], 10**6, *operands, wide=True)


def depths(intensity, membrane, synapse, transfer, occupancy):
    outs = [BRICK] * 3 + [jax.ShapeDtypeStruct((LX, H, LZ), jnp.int32), BRICK] + [
        jax.ShapeDtypeStruct((3, 4, 8, LZ), F32),
        jax.ShapeDtypeStruct((2, H, LZ), F32),
        jax.ShapeDtypeStruct((H, LZ), F32),
        jax.ShapeDtypeStruct((H // ROWS, 8, LX * ROWS), F32),
    ]
    scratch = [
        pltpu.VMEM((H // 8, LZ), F32),
        pltpu.VMEM((3, LX * ROWS, LZ), F32),
        pltpu.VMEM((3, LX * ROWS, LZ), F32),
        pltpu.VMEM((3, 3, LX * ROWS, 2 * LZ), BF16),
    ]
    return call(depth_kernel, outs, scratch, 10**8, intensity, membrane, synapse, transfer, occupancy)


def shades(*operands):
    scratch = [
        pltpu.VMEM((2, H, LZ), F32),
        pltpu.VMEM((H, LZ), BF16),
        pltpu.VMEM((2, LX * ROWS, 2 * LZ), BF16),
        pltpu.VMEM((2, LX * ROWS, LZ), F32),
        pltpu.VMEM((2, 3, LX * ROWS, 2 * LZ), BF16),
        pltpu.VMEM((H // ROWS, 8, LX * ROWS), F32),
        pltpu.VMEM((3, H, LZ), F32),
    ]
    return call(shade_kernel, [HALF, HALF, ZPART, ZPART], scratch, 10**8, *operands)


def body(intensity, membrane, synapse, transfer, occupancy):
    gx = ("z", "y", "core")
    pos = jnp.stack([lax.axis_index("core"), lax.axis_index("x"), lax.axis_index(gx)]).astype(jnp.int32)
    odd_x, face_a, face_b, even_x, intensity, membrane, synapse = faces(pos, intensity, membrane, synapse)
    even = [p for i in range(0, 64, 2) for p in ((i, i + 1), (i + 1, i))]
    odd = [p for i in range(1, 64, 2) for p in ((i, (i + 1) % 64), ((i + 1) % 64, i))]
    odd_x = lax.ppermute(odd_x, gx, odd)
    face_a = lax.ppermute(face_a, "x", [(0, 1), (1, 0), (2, 3), (3, 2)])
    face_b = lax.ppermute(face_b, "x", [(1, 2), (2, 1), (3, 0), (0, 3)])
    even_x = lax.ppermute(even_x, gx, even)
    transfer = jnp.pad(transfer, ((0, 4), (0, LZ - KNOTS)))
    deep = depths(intensity, membrane, synapse, transfer, occupancy)
    keep, send, z_keep, z_send = shades(
        pos, intensity, *deep, odd_x, face_a, face_b, even_x
    )
    other = lax.ppermute(send, "core", [(0, 1), (1, 0)])
    z_other = lax.ppermute(z_send, "x", [(0, 1), (1, 0), (2, 3), (3, 2)])
    (code,) = call(pair_kernel, [CODE], [], 10**6, pos, keep, other)
    (z_pair,) = call(z_kernel, [ZPART], [], 10**11, pos, z_keep, z_other)
    z_other = lax.ppermute(z_pair, "x", [(0, 3), (3, 0), (1, 2), (2, 1)])
    code = lax.all_to_all(code, ("z", "y"), split_axis=0, concat_axis=0, tiled=True)
    return tuple(call(final_kernel, IMAGES, [], 10**6, pos, code, z_pair, z_other))


def solution(mesh):
    split_mesh = Mesh(mesh.devices.reshape(8, 4, 2, 4), ("z", "y", "core", "x"))
    gx = ("z", "y", "core")
    brick = P(gx, None, "x")
    return jax.shard_map(
        body,
        mesh=split_mesh,
        in_specs=(brick, brick, brick, P(), brick),
        out_specs=(P(None, gx, "x"), P(None, gx, "x")),
        check_vma=False,
    )
```

time: 43.3 us -> 40.2 us (0.928)
  waiting for transfers between devices: 10.3 us -> 7.95 us
  local copies, waits for them, and re-layouts: 0.68 us -> 0.09 us
    ppermute x1, starting transfers between devices: 8.58 us -> 0.84 us  [body(): other = lax.ppermute(send, 'core', [(0, 1), (1, 0)])]
    ppermute x1, starting transfers between devices: 3.33 us -> 6.56 us  [body(): even_x = lax.ppermute(even_x, gx, even)]
    ppermute x1, starting transfers between devices: 0.01 us -> 2.77 us  [body(): odd_x = lax.ppermute(odd_x, gx, odd)]
    ppermute x1, waiting for transfers between devices: 2.6 us -> 0.01 us  [body(): z_other = lax.ppermute(z_send, 'x', [(0, 1), (1, 0), (2, 3), (3, 2)])]
    ppermute x1, waiting for transfers between devices: 0.01 us -> 1.07 us  [body(): other = lax.ppermute(send, 'core', [(0, 1), (1, 0)])]
    all_to_all x1, starting transfers between devices: 3.85 us -> 4.85 us  [body(): lax.all_to_all(code, ('z', 'y'), split_axis=0, concat_axis=0, tiled=True)]
    all_to_all x1, waiting for transfers between devices: 5.52 us -> 4.88 us  [body(): lax.all_to_all(code, ('z', 'y'), split_axis=0, concat_axis=0, tiled=True)]
    unnamed x5, local copies, waits for them, and re-layouts: 0.68 us -> 0.08 us
  transfers between devices with their start and end apart: 8 -> 8, of which waited for: 4 -> 3; matrix products, arithmetic and copies ran while one was open for 0% -> 0% of each run, Pallas kernels for 4% -> 11%
where the time goes in v3:
time: 40.2 us; the launch traced here: 40 us
  starting transfers between devices  20.1 us (50%)
  Pallas kernels  11.1 us (28%)
  waiting for transfers between devices  7.95 us (20%)
  between operations  0.72 us (2%)
    pallas_call x6, Pallas kernels, call(): pl.pallas_call(kernel, out_shape=out_shape, in_specs=specs, out_specs=[pl...  11.1 us
    ppermute x1, starting transfers between devices, body(): even_x = lax.ppermute(even_x, gx, even)  6.56 us
    all_to_all x1, waiting for transfers between devices, body(): lax.all_to_all(code, ('z', 'y'), split_axis=0, concat_axis=0, tiled=True)  4.88 us
    all_to_all x1, starting transfers between devices, body(): lax.all_to_all(code, ('z', 'y'), split_axis=0, concat_axis=0, tiled=True)  4.85 us
    ppermute x1, starting transfers between devices, body(): odd_x = lax.ppermute(odd_x, gx, odd)  2.77 us
    ppermute x1, waiting for transfers between devices, body(): z_other = lax.ppermute(z_pair, 'x', [(0, 3), (3, 0), (1, 2), (2, 1)])  1.98 us
    ppermute x1, starting transfers between devices, body(): z_other = lax.ppermute(z_pair, 'x', [(0, 3), (3, 0), (1, 2), (2, 1)])  1.9 us
    ppermute x1, starting transfers between devices, body(): face_b = lax.ppermute(face_b, 'x', [(1, 2), (2, 1), (3, 0), (0, 3)])  1.82 us
  transfers between devices with their start and end apart: 8, of which 3 were waited for; matrix products, arithmetic and copies ran while one was open for 0% of the time, Pallas kernels for 11%

profile of v3, /device:TPU:1, one launch (start us, length us, event | category | flops | bytes accessed | tf_op | source)
XLA Modules:
  0.0 40.0 jit_solution(3252923940699132394)
XLA Ops:
  0.6 0.1 pad_add_fusion.pos
  0.7 1.9 %shard_map.68 = (bf16[256,128]{1,0:T(8,128)(2,1)S(1)}, f32[8,256]{1,0:T(8,128)S(1)}, f32[8,256]{1,0:T(8,128)S(1)}, bf16[256,128]{1,0:T(8,128)(2,1)S(1)}, bf16[8,...) custom-call(s32[3]{0:T(128)S(1)} %pad_add_fusion.pos, ...), custom_call_target="tpu_custom_call" | custom-call | flops 1000000 | bytes 1048576 | tf_op jit(solution)/shard_map/pallas_call | solution.py:358
  2.6 2.8 %collective-permute-start = (bf16[256,128]{1,0:T(8,128)(2,1)S(1)}, bf16[256,128]{1,0:T(8,128)(2,1)S(1)}, u32[]{:S(2)}, u32[]{:S(2)}) collective-permute-start(bf16[256,128]{1,0:T(8,128)(2,1)S(1)} %get-tuple-element.34), channel_id=1, source_target_pairs={{4,8},{8,4},{12,16},{16,12},{20,24},{24,20},{28,32},{32,28},{36,40... | collective-permute-start | bytes 196616 | tf_op jit(solution)/shard_map/ppermute | solution.py:418
  5.4 6.6 %collective-permute-start.3 = (bf16[256,128]{1,0:T(8,128)(2,1)S(1)}, bf16[256,128]{1,0:T(8,128)(2,1)S(1)}, u32[]{:S(2)}, u32[]{:S(2)}) collective-permute-start(bf16[256,128]{1,0:T(8,128)(2,1)S(1)} %get-tuple-element.37), channel_id=1, source_target_pairs={{0,4},{4,0},{8,12},{12,8},{16,20},{20,16},{24,28},{28,24},{32,36},... | collective-permute-start | bytes 196616 | tf_op jit(solution)/shard_map/ppermute | solution.py:421
  12.0 1.2 %collective-permute-start.1 = (f32[8,256]{1,0:T(8,128)S(1)}, f32[8,256]{1,0:T(8,128)S(1)}, u32[]{:S(2)}, u32[]{:S(2)}) collective-permute-start(f32[8,256]{1,0:T(8,128)S(1)} %get-tuple-element.35), channel_id=1, source_target_pairs={{0,1},{1,0},{2,3},{3,2},{4,5},{5,4},{6,7},{7,6},{8,9},{9,8},{10,11... | collective-permute-start | bytes 24584 | tf_op jit(solution)/shard_map/ppermute | solution.py:419
  13.2 1.8 %collective-permute-start.2 = (f32[8,256]{1,0:T(8,128)S(1)}, f32[8,256]{1,0:T(8,128)S(1)}, u32[]{:S(2)}, u32[]{:S(2)}) collective-permute-start(f32[8,256]{1,0:T(8,128)S(1)} %get-tuple-element.36), channel_id=1, source_target_pairs={{1,2},{2,1},{3,0},{0,3},{5,6},{6,5},{7,4},{4,7},{9,10},{10,9},{11,... | collective-permute-start | bytes 24584 | tf_op jit(solution)/shard_map/ppermute | solution.py:420
  15.0 0.1 copy.7.occ
  15.1 2.4 %shard_map.69 = (f32[8,256,128]{2,1,0:T(8,128)S(1)}, f32[8,256,128]{2,1,0:T(8,128)S(1)}, f32[8,256,128]{2,1,0:T(8,128)S(1)}, s32[8,256,128]{2,1,0:T(8,128)S(1)},...) custom-call(bf16[8,256,128]{2,1,0:T(8,128)(2,1)S(1)} %get-tuple-elem, ...), custom_call_target="tpu_custom_call" | custom-call | flops 100000000 | bytes 1048576 | tf_op jit(solution)/shard_map/pallas_call | solution.py:358
  17.5 0.0 collective-permute-done.1.face_a
  17.5 0.0 collective-permute-done.2.face_b
  17.5 0.0 collective-permute-done.odd_x
  17.5 0.0 collective-permute-done.3.even_x
  17.5 3.6 %shard_map.70 = (f32[32,16,128]{2,1,0:T(8,128)S(1)}, f32[32,16,128]{2,1,0:T(8,128)S(1)}, f32[8,512]{1,0:T(8,128)S(1)}, f32[8,512]{1,0:T(8,128)S(1)}) custom-call(s32[3]{0:T(128)S(1)} %pad_add_fusion.pos, bf16[8,256,128]{2,1,0:T(8,128)(2,1)S(1)} %get-tuple-element.22.inten, f32[8,256,128]{2,1,0:T(8,128)S(1)} %get-tuple-element.25.weight_x, ...), custom_call_target="tpu_custom_call" | custom-call | flops 100000000 | bytes 1048576 | tf_op jit(solution)/shard_map/pallas_call | solution.py:358
  21.1 0.8 %collective-permute-start.4 = (f32[32,16,128]{2,1,0:T(8,128)S(1)}, f32[32,16,128]{2,1,0:T(8,128)S(1)}, u32[]{:S(2)}, u32[]{:S(2)}) collective-permute-start(f32[32,16,128]{2,1,0:T(8,128)S(1)} %get-tuple-element.39), channel_id=1, source_target_pairs={{0,4},{4,0},{1,5},{5,1},{2,6},{6,2},{3,7},{7,3},{8,12},{12,8},{9,1... | collective-permute-start | bytes 786440 | tf_op jit(solution)/shard_map/ppermute | solution.py:427
  22.0 0.1 collective-permute-start.5
  22.1 1.1 %collective-permute-done.4.other = f32[32,16,128]{2,1,0:T(8,128)S(1)} collective-permute-done((f32[32,16,128]{2,1,0:T(8,128)S(1)}, f32[32,16,128]{2,1,0:T(8,128)S(1)}, u32[]{:S(2)}, u32[]{:S(2)}) %collective-permute-start.4) | collective-permute-done | bytes 262176 | tf_op jit(solution)/shard_map/ppermute | solution.py:427
  23.1 1.4 %shard_map.71 = s16[32,16,128]{2,1,0:T(8,128)(2,1)} custom-call(s32[3]{0:T(128)S(1)} %pad_add_fusion.pos, f32[32,16,128]{2,1,0:T(8,128)S(1)} %get-tuple-element.38.mine, f32[32,16,128]{2,1,0:T(8,128)S(1)} %collective-permute-done.4.other), custom_call_target="tpu_custom_call" | custom-call | flops 1000000 | bytes 1048576 | tf_op jit(solution)/shard_map/pallas_call | solution.py:358
  24.5 4.9 %all-to-all-start = ((s16[32,16,128]{2,1,0:T(8,128)(2,1)}), s16[32,16,128]{2,1,0:T(8,128)(2,1)S(1)}, u32[]{:S(2)}, u32[]{:S(2)}) async-start(s16[32,16,128]{2,1,0:T(8,128)(2,1)} %shard_map.71), calls=%async_computation | async-start | bytes 262144 | tf_op jit(solution)/shard_map/all_to_all | solution.py:432
  29.3 0.0 collective-permute-done.5.z_other
  29.4 0.6 %shard_map.72.z_mine = f32[8,512]{1,0:T(8,128)S(1)} custom-call(s32[3]{0:T(128)S(1)} %pad_add_fusion.pos, f32[8,512]{1,0:T(8,128)S(1)} %get-tuple-element.40.z_mine, f32[8,512]{1,0:T(8,128)S(1)} %collective-permute-done.5.z_other), custom_call_target="tpu_custom_call" | custom-call | flops 99999997952 | bytes 1048576 | tf_op jit(solution)/shard_map/pallas_call | solution.py:358
  29.9 1.9 %collective-permute-start.6 = (f32[8,512]{1,0:T(8,128)S(1)}, f32[8,512]{1,0:T(8,128)S(1)}, u32[]{:S(2)}, u32[]{:S(2)}) collective-permute-start(f32[8,512]{1,0:T(8,128)S(1)} %shard_map.72.z_mine), channel_id=1, source_target_pairs={{0,3},{3,0},{1,2},{2,1},{4,7},{7,4},{5,6},{6,5},{8,11},{11,8},{9,1... | collective-permute-start | bytes 49160 | tf_op jit(solution)/shard_map/ppermute | solution.py:431
  31.8 2.0 %collective-permute-done.6.z_other = f32[8,512]{1,0:T(8,128)S(1)} collective-permute-done((f32[8,512]{1,0:T(8,128)S(1)}, f32[8,512]{1,0:T(8,128)S(1)}, u32[]{:S(2)}, u32[]{:S(2)}) %collective-permute-start.6) | collective-permute-done | bytes 16416 | tf_op jit(solution)/shard_map/ppermute | solution.py:431
  33.8 4.9 %all-to-all-done.code = s16[32,16,128]{2,1,0:T(8,128)(2,1)S(1)} async-done(((s16[32,16,128]{2,1,0:T(8,128)(2,1)}), s16[32,16,128]{2,1,0:T(8,128)(2,1)S(1)}, u32[]{:S(2)}, u32[]{:S(2)}) %all-to-all-start) | async-done | bytes 131104 | tf_op jit(solution)/shard_map/all_to_all | solution.py:432
  38.7 1.3 %shard_map.73 = (f32[4,4,128]{2,1,0:T(4,128)}, f32[4,8,64]{2,1,0:T(8,128)}) custom-call(s32[3]{0:T(128)S(1)} %pad_add_fusion.pos, s16[32,16,128]{2,1,0:T(8,128)(2,1)S(1)} %all-to-all-done.code, f32[8,512]{1,0:T(8,128)S(1)} %shard_map.72.z_mine, f32[8,512]{1,0:T(8,128)S(1)} %collective-permute-done.6.z_other), custom_call_target="tpu_custom_call" | custom-call | flops 1000000 | bytes 1048576 | tf_op jit(solution)/shard_map/pallas_call | solution.py:358
  (5 shorter events, 0.0 us)
Async XLA Ops:
  0.7 14.3 %copy-start = (s32[1,32,16]{1,2,0:T(8,128)S(1)}, s32[1,32,16]{1,2,0:T(8,128)}, u32[]{:S(2)}) copy-start(s32[1,32,16]{1,2,0:T(8,128)} %param.9) | copy-start | bytes 6148
  2.6 14.9 %collective-permute-start = (bf16[256,128]{1,0:T(8,128)(2,1)S(1)}, bf16[256,128]{1,0:T(8,128)(2,1)S(1)}, u32[]{:S(2)}, u32[]{:S(2)}) collective-permute-start(bf16[256,128]{1,0:T(8,128)(2,1)S(1)} %get-tuple-element.34), channel_id=1, source_target_pairs={{4,8},{8,4},{12,16},{16,12},{20,24},{24,20},{28,32},{32,28},{36,40... | collective-permute-start | bytes 196616 | tf_op jit(solution)/shard_map/ppermute | solution.py:418
  5.4 12.1 %collective-permute-start.3 = (bf16[256,128]{1,0:T(8,128)(2,1)S(1)}, bf16[256,128]{1,0:T(8,128)(2,1)S(1)}, u32[]{:S(2)}, u32[]{:S(2)}) collective-permute-start(bf16[256,128]{1,0:T(8,128)(2,1)S(1)} %get-tuple-element.37), channel_id=1, source_target_pairs={{0,4},{4,0},{8,12},{12,8},{16,20},{20,16},{24,28},{28,24},{32,36},... | collective-permute-start | bytes 196616 | tf_op jit(solution)/shard_map/ppermute | solution.py:421
  12.0 5.5 %collective-permute-start.1 = (f32[8,256]{1,0:T(8,128)S(1)}, f32[8,256]{1,0:T(8,128)S(1)}, u32[]{:S(2)}, u32[]{:S(2)}) collective-permute-start(f32[8,256]{1,0:T(8,128)S(1)} %get-tuple-element.35), channel_id=1, source_target_pairs={{0,1},{1,0},{2,3},{3,2},{4,5},{5,4},{6,7},{7,6},{8,9},{9,8},{10,11... | collective-permute-start | bytes 24584 | tf_op jit(solution)/shard_map/ppermute | solution.py:419
  13.2 1.9 %copy-start.1 = (f32[4,16]{1,0:T(4,128)S(1)}, f32[4,16]{1,0:T(4,128)}, u32[]{:S(2)}) copy-start(f32[4,16]{1,0:T(4,128)} %param.8) | copy-start | bytes 772
  13.2 4.3 %collective-permute-start.2 = (f32[8,256]{1,0:T(8,128)S(1)}, f32[8,256]{1,0:T(8,128)S(1)}, u32[]{:S(2)}, u32[]{:S(2)}) collective-permute-start(f32[8,256]{1,0:T(8,128)S(1)} %get-tuple-element.36), channel_id=1, source_target_pairs={{1,2},{2,1},{3,0},{0,3},{5,6},{6,5},{7,4},{4,7},{9,10},{10,9},{11,... | collective-permute-start | bytes 24584 | tf_op jit(solution)/shard_map/ppermute | solution.py:420
  21.1 2.0 %collective-permute-start.4 = (f32[32,16,128]{2,1,0:T(8,128)S(1)}, f32[32,16,128]{2,1,0:T(8,128)S(1)}, u32[]{:S(2)}, u32[]{:S(2)}) collective-permute-start(f32[32,16,128]{2,1,0:T(8,128)S(1)} %get-tuple-element.39), channel_id=1, source_target_pairs={{0,4},{4,0},{1,5},{5,1},{2,6},{6,2},{3,7},{7,3},{8,12},{12,8},{9,1... | collective-permute-start | bytes 786440 | tf_op jit(solution)/shard_map/ppermute | solution.py:427
  22.0 7.4 %collective-permute-start.5 = (f32[8,512]{1,0:T(8,128)S(1)}, f32[8,512]{1,0:T(8,128)S(1)}, u32[]{:S(2)}, u32[]{:S(2)}) collective-permute-start(f32[8,512]{1,0:T(8,128)S(1)} %get-tuple-element.41), channel_id=1, source_target_pairs={{0,1},{1,0},{2,3},{3,2},{4,5},{5,4},{6,7},{7,6},{8,9},{9,8},{10,11... | collective-permute-start | bytes 49160 | tf_op jit(solution)/shard_map/ppermute | solution.py:428
  24.5 14.2 %all-to-all-start = ((s16[32,16,128]{2,1,0:T(8,128)(2,1)}), s16[32,16,128]{2,1,0:T(8,128)(2,1)S(1)}, u32[]{:S(2)}, u32[]{:S(2)}) async-start(s16[32,16,128]{2,1,0:T(8,128)(2,1)} %shard_map.71), calls=%async_computation | async-start | bytes 262144 | tf_op jit(solution)/shard_map/all_to_all | solution.py:432
  29.9 3.9 %collective-permute-start.6 = (f32[8,512]{1,0:T(8,128)S(1)}, f32[8,512]{1,0:T(8,128)S(1)}, u32[]{:S(2)}, u32[]{:S(2)}) collective-permute-start(f32[8,512]{1,0:T(8,128)S(1)} %shard_map.72.z_mine), channel_id=1, source_target_pairs={{0,3},{3,0},{1,2},{2,1},{4,7},{7,4},{5,6},{6,5},{8,11},{11,8},{9,1... | collective-permute-start | bytes 49160 | tf_op jit(solution)/shard_map/ppermute | solution.py:431

commit v4 on v3

--- a/solution.py
+++ b/solution.py
@@ -111,12 +111,12 @@
 def depth_kernel(
     inten, memb, syn, transfer, occ,
     weight_x, weight_z, steep, spot, along, tables, own_x, total_x, total_z,
-    occ_rows, sigma, prefix, parts,
+    occ_rows, sigma, prefix, parts, columns,
 ):
     scale = -2.0 / (LX * 64) / LN2
     dense = knot_table(transfer, 3, scale, False)
     for c in range(3):
-        for i, table in enumerate(knot_table(transfer, c, 1.0, c in ACROSS)):
+        for i, table in enumerate(knot_table(transfer, c, 0.7, c in ACROSS)):
             tables[c, i] = table
     spread = as_bf16(iota((KNOTS, LZ), 1) // 8 == iota((KNOTS, LZ), 0))
     occ_rows[...] = mxu(occ[0].astype(F32).astype(BF16), spread, NN)
@@ -124,12 +124,12 @@
     diff_y = (jnp.where(k == r + 1, 1.0, 0.0) - jnp.where(k == r - 1, 1.0, 0.0)).astype(BF16)
     k, n = iota((2 * LZ, LZ), 0), iota((2 * LZ, LZ), 1)
     before = as_bf16(k % LZ < n)
-    ones = jnp.ones((8, 2 * LZ), BF16)
+    lane = iota((16, LZ), 1)
     for x in range(LX):
         grad_y = mxu(diff_y, inten[x], NN)
         steep[x] = grad_y * grad_y + 1.0
     def cells(j):
-        buf = j % 3
+        buf = j % 2
         for b in range(0, ROWS, 16):
             rows = pl.ds(j * ROWS + b, 16)
             block = (j * ROWS + b) // 8
@@ -140,6 +140,7 @@
             trans = jnp.ones((16, LZ), F32)
             own_m = jnp.zeros((16, LZ), F32)
             own_s = jnp.zeros((16, LZ), F32)
+            column = jnp.zeros((16, LZ), F32)
             for x in range(LX):
                 index, frac = lookup(inten[x, rows, :].astype(F32))
                 spot[x, rows, :] = index
@@ -150,8 +151,8 @@
                 depth = (depth + sy * (0.5 * scale)) * mask
                 high, low = split(depth)
                 row = x * ROWS + b
-                parts[buf, 0, row : row + 16, 0:LZ] = high
-                parts[buf, 0, row : row + 16, LZ:] = low
+                parts[buf, row : row + 16, 0:LZ] = high
+                parts[buf, row : row + 16, LZ:] = low
                 passed = jnp.exp2(depth)
                 alpha = 1.0 - passed
                 sigma[buf, row : row + 16, :] = alpha
@@ -161,47 +162,49 @@
                 own_s = own_s + weight * sy
                 trans = trans * passed
                 total = total + depth
+                column = put(column, 3 * LX + x, depth)
+            columns[rows, :] = column
             total_x[rows, :] = total
             own_x[0, rows, :] = own_m
             own_x[1, rows, :] = own_s
-        prefix[buf] = mxu(parts[buf, 0], before, NN)
+        prefix[buf] = mxu(parts[buf], before, NN)
 
     def weights(j):
-        buf = j % 3
-        for x in range(LX):
-            for b in range(0, ROWS, 16):
-                rows = pl.ds(j * ROWS + b, 16)
+        buf = j % 2
+        for b in range(0, ROWS, 16):
+            rows = pl.ds(j * ROWS + b, 16)
+            column = columns[rows, :]
+            for x in range(LX):
                 here = slice(x * ROWS + b, x * ROWS + b + 16)
                 weight = jnp.exp2(prefix[buf, here, :]) * sigma[buf, here, :]
                 weight_z[x, rows, :] = weight
-                for i, probability in enumerate((memb, syn)):
-                    high, low = split(weight * probability[x, rows, :].astype(F32))
-                    parts[buf, 1 + i, here, 0:LZ] = high
-                    parts[buf, 1 + i, here, LZ:] = low
-
-    def sums(j):
-        buf = j % 3
-        deep, own_m, own_s = [mxu(ones, parts[buf, i], NT) for i in range(3)]
-        channel = iota((8, LX * ROWS), 0) % 4
-        rest = jnp.where(channel == 3, -deep, 0.0)
-        for c in range(3):
-            rest = jnp.where(channel == c, MEMBRANE_COLOR[c] * own_m + SYNAPSE_COLOR[c] * own_s, rest)
-        total_z[j] = rest
-
-    for step in range(H // ROWS + 2):
+                column = put(column, x, weight * memb[x, rows, :].astype(F32))
+                column = put(column, LX + x, weight * syn[x, rows, :].astype(F32))
+            columns[rows, :] = column
+
+    def put(column, place, value):
+        return jnp.where(lane == place, jnp.sum(value, axis=1, keepdims=True), column)
+
+    for step in range(H // ROWS + 1):
         if step < H // ROWS:
             cells(step)
-        if 1 <= step <= H // ROWS:
+        if step >= 1:
             weights(step - 1)
-        if step >= 2:
-            sums(step - 2)
+    for half in range(2):
+        lines = jnp.transpose(columns[half * LZ : (half + 1) * LZ, :])
+        own_m, own_s, deep = lines[0:LX], lines[LX : 2 * LX], lines[3 * LX : 4 * LX]
+        for c in range(3):
+            total_z[c * LX : (c + 1) * LX, half * LZ : (half + 1) * LZ] = (
+                MEMBRANE_COLOR[c] * own_m + SYNAPSE_COLOR[c] * own_s
+            )
+        total_z[3 * LX :, half * LZ : (half + 1) * LZ] = -deep
 
 
 def shade_kernel(
     pos, inten, weight_x, weight_z, steep, spot, along, tables, own_x, total_x, total_z,
     odd_x, face_a, face_b, even_x,
     keep, send, z_keep, z_send,
-    pad, halo, left, dz, parts, zsum, image,
+    pad, halo, left, dz, image, columns,
 ):
     core, zpos = pos[0], pos[1]
     odd_z = zpos % 2
@@ -219,7 +222,7 @@
     down = ((k < LZ) & (k == n - 1)) | ((k >= LZ) & (k < LZ + LX) & (n == 0))
     diff_z = (jnp.where(up, 1.0, 0.0) - jnp.where(down, 1.0, 0.0)).astype(BF16)
     lanes = iota((ROWS, LZ), 1)
-    ones_row = iota((8, 2 * LZ), 0)
+    lane = iota((16, LZ), 1)
     first_half = iota((8, LZ), 0) < 4
     knots = [[tables[c, i] for i in range(2 if c in ACROSS else 4)] for c in range(3)]
 
@@ -237,28 +240,24 @@
         rows = pl.ds(j * ROWS + b, 16)
         own_m, own_s = own_x[0, rows, :], own_x[1, rows, :]
         acc = [MEMBRANE_COLOR[c] * own_m + SYNAPSE_COLOR[c] * own_s for c in range(3)]
+        column = jnp.zeros((16, LZ), F32)
         values = [pad[0, rows, :]] + [inten[x, rows, :].astype(F32) for x in range(LX)] + [pad[1, rows, :]]
         for x in range(LX):
             row = x * ROWS + b
             grad_x = values[x + 2] - values[x]
             grad_z = dz[buf, row : row + 16, :]
-            norm = lax.rsqrt(grad_x * grad_x + (grad_z * grad_z + steep[x, rows, :])) * 0.7
-            lit_x = (0.3 + jnp.abs(grad_x) * norm) * weight_x[x, rows, :]
-            lit_z = (0.3 + jnp.abs(grad_z) * norm) * weight_z[x, rows, :]
+            norm = lax.rsqrt(grad_x * grad_x + (grad_z * grad_z + steep[x, rows, :]))
+            lit_x = (0.3 / 0.7 + jnp.abs(grad_x) * norm) * weight_x[x, rows, :]
+            lit_z = (0.3 / 0.7 + jnp.abs(grad_z) * norm) * weight_z[x, rows, :]
             index, frac = spot[x, rows, :], along[x, rows, :]
             for c in range(3):
                 color = interpolate(knots[c], index, frac)
                 acc[c] = acc[c] + lit_x * color
-                high, low = split(lit_z * color)
-                parts[buf, c, row : row + 16, 0:LZ] = high
-                parts[buf, c, row : row + 16, LZ:] = low
+                summed = jnp.sum(lit_z * color, axis=1, keepdims=True)
+                column = jnp.where(lane == c * LX + x, summed, column)
         for c in range(3):
             image[c, rows, :] = acc[c]
-
-    def sums(j, c):
-        if c == 0:
-            zsum[j] = total_z[j]
-        zsum[j] += mxu(as_bf16(ones_row % 4 == c), parts[j % 2, c], NT)
+        columns[rows, :] = column
 
     chunks = H // ROWS
     slopes(0)
@@ -266,11 +265,7 @@
         for i, b in enumerate(range(0, ROWS, 16)):
             if i == 0 and j + 1 < chunks:
                 slopes(j + 1)
-            if i < 3 and j > 0:
-                sums(j - 1, i)
             cells(j, b)
-    for c in range(3):
-        sums(chunks - 1, c)
     swap = lambda v: pltpu.roll(v, 4, 0)
     for first in range(0, CHIPS, 8):
         ready = []
@@ -286,22 +281,29 @@
                 ready.append((send, chip, i, jnp.where(core == 0, for_1, for_0)))
         for out, chip, i, value in ready:
             out[chip, 8 * i : 8 * i + 8, :] = value
-    for out, chip in ((z_keep, zpos), (z_send, zpos ^ 1)):
-        out[...] = jnp.where(iota((8, LX * ROWS), 0) < 4, zsum[chip], zsum[3 - chip])
+    low, high = [
+        total_z[:, half * LZ : (half + 1) * LZ]
+        + jnp.where(
+            iota((4 * LX, LZ), 0) < 3 * LX, jnp.transpose(columns[half * LZ : (half + 1) * LZ, :])[: 4 * LX], 0.0
+        )
+        for half in range(2)
+    ]
+    near_half = iota((4 * LX, LZ), 1) < ROWS
+    outer = jnp.where(near_half, low, high)
+    inner = pltpu.roll(jnp.where(near_half, high, low), ROWS, 1)
+    edge = (zpos == 0) | (zpos == 3)
+    z_keep[...] = jnp.where(edge, outer, inner)
+    z_send[...] = jnp.where(edge, inner, outer)
 
 
 def depth_rows(b):
     return jnp.where(iota((8, LZ), 0) < 4, pltpu.roll(b, 4, 0), b)
 
 
-def z_rows(z):
-    upper = iota(z.shape, 0) < 4
-    return jnp.where(upper, jnp.broadcast_to(z[3:4], z.shape), jnp.broadcast_to(z[7:8], z.shape))
-
-
 def z_merge(first, second):
-    depth_row = iota(first.shape, 0) % 4 == 3
-    return first + jnp.where(depth_row, 1.0, jnp.exp2(-z_rows(first))) * second
+    passed = jnp.exp2(-first[3 * LX :])
+    rows = [first[c * LX : (c + 1) * LX] + passed * second[c * LX : (c + 1) * LX] for c in range(3)]
+    return jnp.concatenate(rows + [first[3 * LX :] + second[3 * LX :]], axis=0)
 
 
 def z_kernel(pos, z_mine, z_other, z_pair):
@@ -343,11 +345,12 @@
     x_image[2] = b[0:4]
     x_image[3] = (1.0 - jnp.exp2(-deep))[0:4]
 
-    zm, zo = z_mine[...], pltpu.roll(z_other[...], 4, 0)
+    zm, zo = z_mine[...], z_other[...]
     image = z_merge(jnp.where(front, zm, zo), jnp.where(front, zo, zm))
-    image = jnp.where(iota(image.shape, 0) == 3, 1.0 - jnp.exp2(-image), image)
-    for x in range(LX):
-        z_image[:, x, :] = image[0:4, x * ROWS : (x + 1) * ROWS]
+    image = jnp.where(front, image, pltpu.roll(image, ROWS, 1))[:, 0:ROWS]
+    for c in range(3):
+        z_image[c] = image[c * LX : (c + 1) * LX]
+    z_image[3] = 1.0 - jnp.exp2(-image[3 * LX :])
 
 
 def call(kernel, out_shape, scratch, cost, *operands, wide=False):
@@ -369,7 +372,7 @@
 LAYER, FACE = jax.ShapeDtypeStruct((H, LZ), BF16), jax.ShapeDtypeStruct((LX, H), F32)
 BRICK = jax.ShapeDtypeStruct((LX, H, LZ), F32)
 HALF = jax.ShapeDtypeStruct((CHIPS, 16, LZ), F32)
-ZPART = jax.ShapeDtypeStruct((8, LX * ROWS), F32)
+ZPART = jax.ShapeDtypeStruct((4 * LX, LZ), F32)
 IMAGES = [jax.ShapeDtypeStruct((4, 4, LZ), F32), jax.ShapeDtypeStruct((4, LX, ROWS), F32)]
 CODE = jax.ShapeDtypeStruct((CHIPS, 16, LZ), jnp.int16)
 
@@ -385,13 +388,14 @@
         jax.ShapeDtypeStruct((3, 4, 8, LZ), F32),
         jax.ShapeDtypeStruct((2, H, LZ), F32),
         jax.ShapeDtypeStruct((H, LZ), F32),
-        jax.ShapeDtypeStruct((H // ROWS, 8, LX * ROWS), F32),
+        jax.ShapeDtypeStruct((4 * LX, H), F32),
     ]
     scratch = [
         pltpu.VMEM((H // 8, LZ), F32),
-        pltpu.VMEM((3, LX * ROWS, LZ), F32),
-        pltpu.VMEM((3, LX * ROWS, LZ), F32),
-        pltpu.VMEM((3, 3, LX * ROWS, 2 * LZ), BF16),
+        pltpu.VMEM((2, LX * ROWS, LZ), F32),
+        pltpu.VMEM((2, LX * ROWS, LZ), F32),
+        pltpu.VMEM((2, LX * ROWS, 2 * LZ), BF16),
+        pltpu.VMEM((H, LZ), F32),
     ]
     return call(depth_kernel, outs, scratch, 10**8, intensity, membrane, synapse, transfer, occupancy)
 
@@ -402,9 +406,8 @@
         pltpu.VMEM((H, LZ), BF16),
         pltpu.VMEM((2, LX * ROWS, 2 * LZ), BF16),
         pltpu.VMEM((2, LX * ROWS, LZ), F32),
-        pltpu.VMEM((2, 3, LX * ROWS, 2 * LZ), BF16),
-        pltpu.VMEM((H // ROWS, 8, LX * ROWS), F32),
         pltpu.VMEM((3, H, LZ), F32),
+        pltpu.VMEM((H, LZ), F32),
     ]
     return call(shade_kernel, [HALF, HALF, ZPART, ZPART], scratch, 10**8, *operands)
 

time: 40.2 us -> 39.8 us (0.990)
  Pallas kernels: 11.1 us -> 10.5 us
    pallas_call x6, Pallas kernels: 11.1 us -> 10.5 us  [call(): pl.pallas_call(kernel, out_shape=out_shape, in_specs=specs, out_specs=[pl...]
  transfers between devices with their start and end apart: 8 -> 8, of which waited for: 3 -> 3; matrix products, arithmetic and copies ran while one was open for 0% -> 0% of each run, Pallas kernels for 11% -> 10%
where the time goes in v4:
time: 39.8 us; the launch traced here: 39.6 us
  starting transfers between devices  20.2 us (51%)
  Pallas kernels  10.5 us (26%)
  waiting for transfers between devices  8.04 us (20%)
  between operations  0.7 us (2%)
    pallas_call x6, Pallas kernels, call(): pl.pallas_call(kernel, out_shape=out_shape, in_specs=specs, out_specs=[pl...  10.5 us
    ppermute x1, starting transfers between devices, body(): even_x = lax.ppermute(even_x, gx, even)  6.56 us
    all_to_all x1, waiting for transfers between devices, body(): lax.all_to_all(code, ('z', 'y'), split_axis=0, concat_axis=0, tiled=True)  4.89 us
    all_to_all x1, starting transfers between devices, body(): lax.all_to_all(code, ('z', 'y'), split_axis=0, concat_axis=0, tiled=True)  4.85 us
    ppermute x1, starting transfers between devices, body(): odd_x = lax.ppermute(odd_x, gx, odd)  2.77 us
    ppermute x1, waiting for transfers between devices, body(): z_other = lax.ppermute(z_pair, 'x', [(0, 3), (3, 0), (1, 2), (2, 1)])  1.98 us
    ppermute x1, starting transfers between devices, body(): z_other = lax.ppermute(z_pair, 'x', [(0, 3), (3, 0), (1, 2), (2, 1)])  1.9 us
    ppermute x1, starting transfers between devices, body(): face_b = lax.ppermute(face_b, 'x', [(1, 2), (2, 1), (3, 0), (0, 3)])  1.82 us
  transfers between devices with their start and end apart: 8, of which 3 were waited for; matrix products, arithmetic and copies ran while one was open for 0% of the time, Pallas kernels for 10%

profile of v4, /device:TPU:1, one launch (start us, length us, event | category | flops | bytes accessed | tf_op | source)
XLA Modules:
  0.0 39.6 jit_solution(4379644828570651253)
XLA Ops:
  0.6 0.1 pad_add_fusion.pos
  0.7 1.9 %shard_map.68 = (bf16[256,128]{1,0:T(8,128)(2,1)S(1)}, f32[8,256]{1,0:T(8,128)S(1)}, f32[8,256]{1,0:T(8,128)S(1)}, bf16[256,128]{1,0:T(8,128)(2,1)S(1)}, bf16[8,...) custom-call(s32[3]{0:T(128)S(1)} %pad_add_fusion.pos, ...), custom_call_target="tpu_custom_call" | custom-call | flops 1000000 | bytes 1048576 | tf_op jit(solution)/shard_map/pallas_call | solution.py:361
  2.6 2.8 %collective-permute-start = (bf16[256,128]{1,0:T(8,128)(2,1)S(1)}, bf16[256,128]{1,0:T(8,128)(2,1)S(1)}, u32[]{:S(2)}, u32[]{:S(2)}) collective-permute-start(bf16[256,128]{1,0:T(8,128)(2,1)S(1)} %get-tuple-element.34), channel_id=1, source_target_pairs={{4,8},{8,4},{12,16},{16,12},{20,24},{24,20},{28,32},{32,28},{36,40... | collective-permute-start | bytes 196616 | tf_op jit(solution)/shard_map/ppermute | solution.py:421
  5.4 6.6 %collective-permute-start.3 = (bf16[256,128]{1,0:T(8,128)(2,1)S(1)}, bf16[256,128]{1,0:T(8,128)(2,1)S(1)}, u32[]{:S(2)}, u32[]{:S(2)}) collective-permute-start(bf16[256,128]{1,0:T(8,128)(2,1)S(1)} %get-tuple-element.37), channel_id=1, source_target_pairs={{0,4},{4,0},{8,12},{12,8},{16,20},{20,16},{24,28},{28,24},{32,36},... | collective-permute-start | bytes 196616 | tf_op jit(solution)/shard_map/ppermute | solution.py:424
  12.0 1.2 %collective-permute-start.1 = (f32[8,256]{1,0:T(8,128)S(1)}, f32[8,256]{1,0:T(8,128)S(1)}, u32[]{:S(2)}, u32[]{:S(2)}) collective-permute-start(f32[8,256]{1,0:T(8,128)S(1)} %get-tuple-element.35), channel_id=1, source_target_pairs={{0,1},{1,0},{2,3},{3,2},{4,5},{5,4},{6,7},{7,6},{8,9},{9,8},{10,11... | collective-permute-start | bytes 24584 | tf_op jit(solution)/shard_map/ppermute | solution.py:422
  13.2 1.8 %collective-permute-start.2 = (f32[8,256]{1,0:T(8,128)S(1)}, f32[8,256]{1,0:T(8,128)S(1)}, u32[]{:S(2)}, u32[]{:S(2)}) collective-permute-start(f32[8,256]{1,0:T(8,128)S(1)} %get-tuple-element.36), channel_id=1, source_target_pairs={{1,2},{2,1},{3,0},{0,3},{5,6},{6,5},{7,4},{4,7},{9,10},{10,9},{11,... | collective-permute-start | bytes 24584 | tf_op jit(solution)/shard_map/ppermute | solution.py:423
  15.0 0.1 copy.7.occ
  15.1 2.2 %shard_map.69 = (f32[8,256,128]{2,1,0:T(8,128)S(1)}, f32[8,256,128]{2,1,0:T(8,128)S(1)}, f32[8,256,128]{2,1,0:T(8,128)S(1)}, s32[8,256,128]{2,1,0:T(8,128)S(1)},...) custom-call(bf16[8,256,128]{2,1,0:T(8,128)(2,1)S(1)} %get-tuple-elem, ...), custom_call_target="tpu_custom_call" | custom-call | flops 100000000 | bytes 1048576 | tf_op jit(solution)/shard_map/pallas_call | solution.py:361
  17.3 0.0 collective-permute-done.1.face_a
  17.3 0.0 collective-permute-done.2.face_b
  17.3 0.0 collective-permute-done.odd_x
  17.3 0.0 collective-permute-done.3.even_x
  17.3 3.3 %shard_map.70 = (f32[32,16,128]{2,1,0:T(8,128)S(1)}, f32[32,16,128]{2,1,0:T(8,128)S(1)}, f32[32,128]{1,0:T(8,128)S(1)}, f32[32,128]{1,0:T(8,128)S(1)}) custom-call(s32[3]{0:T(128)S(1)} %pad_add_fusion.pos, bf16[8,256,128]{2,1,0:T(8,128)(2,1)S(1)} %get-tuple-element.22.inten, f32[8,256,128]{2,1,0:T(8,128)S(1)} %get-tuple-element.25.weight_x, ...), custom_call_target="tpu_custom_call" | custom-call | flops 100000000 | bytes 1048576 | tf_op jit(solution)/shard_map/pallas_call | solution.py:361
  20.6 1.1 %collective-permute-start.4 = (f32[32,16,128]{2,1,0:T(8,128)S(1)}, f32[32,16,128]{2,1,0:T(8,128)S(1)}, u32[]{:S(2)}, u32[]{:S(2)}) collective-permute-start(f32[32,16,128]{2,1,0:T(8,128)S(1)} %get-tuple-element.39), channel_id=1, source_target_pairs={{0,4},{4,0},{1,5},{5,1},{2,6},{6,2},{3,7},{7,3},{8,12},{12,8},{9,1... | collective-permute-start | bytes 786440 | tf_op jit(solution)/shard_map/ppermute | solution.py:430
  21.7 0.0 collective-permute-start.5
  21.7 1.2 %collective-permute-done.4.other = f32[32,16,128]{2,1,0:T(8,128)S(1)} collective-permute-done((f32[32,16,128]{2,1,0:T(8,128)S(1)}, f32[32,16,128]{2,1,0:T(8,128)S(1)}, u32[]{:S(2)}, u32[]{:S(2)}) %collective-permute-start.4) | collective-permute-done | bytes 262176 | tf_op jit(solution)/shard_map/ppermute | solution.py:430
  22.8 1.4 %shard_map.71 = s16[32,16,128]{2,1,0:T(8,128)(2,1)} custom-call(s32[3]{0:T(128)S(1)} %pad_add_fusion.pos, f32[32,16,128]{2,1,0:T(8,128)S(1)} %get-tuple-element.38.mine, f32[32,16,128]{2,1,0:T(8,128)S(1)} %collective-permute-done.4.other), custom_call_target="tpu_custom_call" | custom-call | flops 1000000 | bytes 1048576 | tf_op jit(solution)/shard_map/pallas_call | solution.py:361
  24.2 4.9 %all-to-all-start = ((s16[32,16,128]{2,1,0:T(8,128)(2,1)}), s16[32,16,128]{2,1,0:T(8,128)(2,1)S(1)}, u32[]{:S(2)}, u32[]{:S(2)}) async-start(s16[32,16,128]{2,1,0:T(8,128)(2,1)} %shard_map.71), calls=%async_computation | async-start | bytes 262144 | tf_op jit(solution)/shard_map/all_to_all | solution.py:435
  29.0 0.0 collective-permute-done.5.z_other
  29.1 0.6 %shard_map.72.z_mine = f32[32,128]{1,0:T(8,128)S(1)} custom-call(s32[3]{0:T(128)S(1)} %pad_add_fusion.pos, f32[32,128]{1,0:T(8,128)S(1)} %get-tuple-element.40.z_mine, f32[32,128]{1,0:T(8,128)S(1)} %collective-permute-done.5.z_other), custom_call_target="tpu_custom_call" | custom-call | flops 99999997952 | bytes 1048576 | tf_op jit(solution)/shard_map/pallas_call | solution.py:361
  29.6 1.9 %collective-permute-start.6 = (f32[32,128]{1,0:T(8,128)S(1)}, f32[32,128]{1,0:T(8,128)S(1)}, u32[]{:S(2)}, u32[]{:S(2)}) collective-permute-start(f32[32,128]{1,0:T(8,128)S(1)} %shard_map.72.z_mine), channel_id=1, source_target_pairs={{0,3},{3,0},{1,2},{2,1},{4,7},{7,4},{5,6},{6,5},{8,11},{11,8},{9,1... | collective-permute-start | bytes 49160 | tf_op jit(solution)/shard_map/ppermute | solution.py:434
  31.5 2.0 %collective-permute-done.6.z_other = f32[32,128]{1,0:T(8,128)S(1)} collective-permute-done((f32[32,128]{1,0:T(8,128)S(1)}, f32[32,128]{1,0:T(8,128)S(1)}, u32[]{:S(2)}, u32[]{:S(2)}) %collective-permute-start.6) | collective-permute-done | bytes 16416 | tf_op jit(solution)/shard_map/ppermute | solution.py:434
  33.5 4.9 %all-to-all-done.code = s16[32,16,128]{2,1,0:T(8,128)(2,1)S(1)} async-done(((s16[32,16,128]{2,1,0:T(8,128)(2,1)}), s16[32,16,128]{2,1,0:T(8,128)(2,1)S(1)}, u32[]{:S(2)}, u32[]{:S(2)}) %all-to-all-start) | async-done | bytes 131104 | tf_op jit(solution)/shard_map/all_to_all | solution.py:435
  38.4 1.2 %shard_map.73 = (f32[4,4,128]{2,1,0:T(4,128)}, f32[4,8,64]{2,1,0:T(8,128)}) custom-call(s32[3]{0:T(128)S(1)} %pad_add_fusion.pos, s16[32,16,128]{2,1,0:T(8,128)(2,1)S(1)} %all-to-all-done.code, f32[32,128]{1,0:T(8,128)S(1)} %shard_map.72.z_mine, f32[32,128]{1,0:T(8,128)S(1)} %collective-permute-done.6.z_other), custom_call_target="tpu_custom_call" | custom-call | flops 1000000 | bytes 1048576 | tf_op jit(solution)/shard_map/pallas_call | solution.py:361
  (5 shorter events, 0.0 us)
Async XLA Ops:
  0.7 14.3 %copy-start = (s32[1,32,16]{1,2,0:T(8,128)S(1)}, s32[1,32,16]{1,2,0:T(8,128)}, u32[]{:S(2)}) copy-start(s32[1,32,16]{1,2,0:T(8,128)} %param.9) | copy-start | bytes 6148
  2.6 14.6 %collective-permute-start = (bf16[256,128]{1,0:T(8,128)(2,1)S(1)}, bf16[256,128]{1,0:T(8,128)(2,1)S(1)}, u32[]{:S(2)}, u32[]{:S(2)}) collective-permute-start(bf16[256,128]{1,0:T(8,128)(2,1)S(1)} %get-tuple-element.34), channel_id=1, source_target_pairs={{4,8},{8,4},{12,16},{16,12},{20,24},{24,20},{28,32},{32,28},{36,40... | collective-permute-start | bytes 196616 | tf_op jit(solution)/shard_map/ppermute | solution.py:421
  5.4 11.9 %collective-permute-start.3 = (bf16[256,128]{1,0:T(8,128)(2,1)S(1)}, bf16[256,128]{1,0:T(8,128)(2,1)S(1)}, u32[]{:S(2)}, u32[]{:S(2)}) collective-permute-start(bf16[256,128]{1,0:T(8,128)(2,1)S(1)} %get-tuple-element.37), channel_id=1, source_target_pairs={{0,4},{4,0},{8,12},{12,8},{16,20},{20,16},{24,28},{28,24},{32,36},... | collective-permute-start | bytes 196616 | tf_op jit(solution)/shard_map/ppermute | solution.py:424
  12.0 5.3 %collective-permute-start.1 = (f32[8,256]{1,0:T(8,128)S(1)}, f32[8,256]{1,0:T(8,128)S(1)}, u32[]{:S(2)}, u32[]{:S(2)}) collective-permute-start(f32[8,256]{1,0:T(8,128)S(1)} %get-tuple-element.35), channel_id=1, source_target_pairs={{0,1},{1,0},{2,3},{3,2},{4,5},{5,4},{6,7},{7,6},{8,9},{9,8},{10,11... | collective-permute-start | bytes 24584 | tf_op jit(solution)/shard_map/ppermute | solution.py:422
  13.2 1.9 %copy-start.1 = (f32[4,16]{1,0:T(4,128)S(1)}, f32[4,16]{1,0:T(4,128)}, u32[]{:S(2)}) copy-start(f32[4,16]{1,0:T(4,128)} %param.8) | copy-start | bytes 772
  13.2 4.1 %collective-permute-start.2 = (f32[8,256]{1,0:T(8,128)S(1)}, f32[8,256]{1,0:T(8,128)S(1)}, u32[]{:S(2)}, u32[]{:S(2)}) collective-permute-start(f32[8,256]{1,0:T(8,128)S(1)} %get-tuple-element.36), channel_id=1, source_target_pairs={{1,2},{2,1},{3,0},{0,3},{5,6},{6,5},{7,4},{4,7},{9,10},{10,9},{11,... | collective-permute-start | bytes 24584 | tf_op jit(solution)/shard_map/ppermute | solution.py:423
  20.6 2.2 %collective-permute-start.4 = (f32[32,16,128]{2,1,0:T(8,128)S(1)}, f32[32,16,128]{2,1,0:T(8,128)S(1)}, u32[]{:S(2)}, u32[]{:S(2)}) collective-permute-start(f32[32,16,128]{2,1,0:T(8,128)S(1)} %get-tuple-element.39), channel_id=1, source_target_pairs={{0,4},{4,0},{1,5},{5,1},{2,6},{6,2},{3,7},{7,3},{8,12},{12,8},{9,1... | collective-permute-start | bytes 786440 | tf_op jit(solution)/shard_map/ppermute | solution.py:430
  21.7 7.4 %collective-permute-start.5 = (f32[32,128]{1,0:T(8,128)S(1)}, f32[32,128]{1,0:T(8,128)S(1)}, u32[]{:S(2)}, u32[]{:S(2)}) collective-permute-start(f32[32,128]{1,0:T(8,128)S(1)} %get-tuple-element.41), channel_id=1, source_target_pairs={{0,1},{1,0},{2,3},{3,2},{4,5},{5,4},{6,7},{7,6},{8,9},{9,8},{10,11... | collective-permute-start | bytes 49160 | tf_op jit(solution)/shard_map/ppermute | solution.py:431
  24.2 14.2 %all-to-all-start = ((s16[32,16,128]{2,1,0:T(8,128)(2,1)}), s16[32,16,128]{2,1,0:T(8,128)(2,1)S(1)}, u32[]{:S(2)}, u32[]{:S(2)}) async-start(s16[32,16,128]{2,1,0:T(8,128)(2,1)} %shard_map.71), calls=%async_computation | async-start | bytes 262144 | tf_op jit(solution)/shard_map/all_to_all | solution.py:435
  29.6 3.9 %collective-permute-start.6 = (f32[32,128]{1,0:T(8,128)S(1)}, f32[32,128]{1,0:T(8,128)S(1)}, u32[]{:S(2)}, u32[]{:S(2)}) collective-permute-start(f32[32,128]{1,0:T(8,128)S(1)} %shard_map.72.z_mine), channel_id=1, source_target_pairs={{0,3},{3,0},{1,2},{2,1},{4,7},{7,4},{5,6},{6,5},{8,11},{11,8},{9,1... | collective-permute-start | bytes 49160 | tf_op jit(solution)/shard_map/ppermute | solution.py:434

commit v5 on v4

--- a/solution.py
+++ b/solution.py
@@ -40,7 +40,7 @@
 
 
 def faces_kernel(
-    pos, inten_hbm, memb_hbm, syn_hbm,
+    marks, inten_hbm, memb_hbm, syn_hbm,
     odd_x, face_a, face_b, even_x, intensity, memb, syn, sems,
 ):
     pairs = ((inten_hbm, intensity), (memb_hbm, memb), (syn_hbm, syn))
@@ -48,9 +48,10 @@
     for copy in copies:
         copy.start()
     copies[0].wait()
-    core, odd_z = pos[0], pos[1] % 2
-    even_x[...] = intensity[jnp.where(core == 0, LX - 1, 0)]
-    odd_x[...] = intensity[jnp.where(core == 0, 0, LX - 1)]
+    core, odd_z = marks[0:1, :], marks[1:2, :] & 1
+    first, last = intensity[0].astype(F32), intensity[LX - 1].astype(F32)
+    even_x[...] = jnp.where(core == 0, last, first).astype(BF16)
+    odd_x[...] = jnp.where(core == 0, first, last).astype(BF16)
     row, lane = iota((16, LZ), 0), iota((16, LZ), 1)
     lane_a = jnp.where(odd_z == 0, LZ - 1, 0)
     wanted = jnp.where(row < LX, lane_a, LZ - 1 - lane_a)
@@ -201,20 +202,20 @@
 
 
 def shade_kernel(
-    pos, inten, weight_x, weight_z, steep, spot, along, tables, own_x, total_x, total_z,
+    marks, inten, weight_x, weight_z, steep, spot, along, tables, own_x, total_x, total_z,
     odd_x, face_a, face_b, even_x,
     keep, send, z_keep, z_send,
     pad, halo, left, dz, image, columns,
 ):
-    core, zpos = pos[0], pos[1]
-    odd_z = zpos % 2
-    gx = pos[2]
+    core, zpos, gx = marks[0:1, :], marks[1:2, :], marks[2:3, :]
+    lane_z = jnp.concatenate([zpos, zpos], axis=1)
+    odd_z = lane_z & 1
     low = jnp.where(core == 0, odd_x[...].astype(F32), even_x[...].astype(F32))
     high = jnp.where(core == 0, even_x[...].astype(F32), odd_x[...].astype(F32))
     pad[0] = jnp.where(gx == 0, 0.0, low)
     pad[1] = jnp.where(gx == 63, 0.0, high)
-    near = jnp.where(zpos == 0, 0.0, jnp.where(odd_z == 0, face_b[...], face_a[...]))
-    far = jnp.where(zpos == 3, 0.0, jnp.where(odd_z == 0, face_a[...], face_b[...]))
+    near = jnp.where(lane_z == 0, 0.0, jnp.where(odd_z == 0, face_b[...], face_a[...]))
+    far = jnp.where(lane_z == 3, 0.0, jnp.where(odd_z == 0, face_a[...], face_b[...]))
     both = jnp.concatenate([near, far], axis=0).astype(BF16)
     halo[...] = mxu(both, as_bf16(iota((16, LZ), 0) == iota((16, LZ), 1)), TN).astype(BF16)
     k, n = iota((2 * LZ, LZ), 0), iota((2 * LZ, LZ), 1)
@@ -306,14 +307,14 @@
     return jnp.concatenate(rows + [first[3 * LX :] + second[3 * LX :]], axis=0)
 
 
-def z_kernel(pos, z_mine, z_other, z_pair):
-    even = pos[1] % 2 == 0
+def z_kernel(marks, z_mine, z_other, z_pair):
+    even = (marks[1:2, :] & 1) == 0
     zm, zo = z_mine[...], z_other[...]
     z_pair[...] = z_merge(jnp.where(even, zm, zo), jnp.where(even, zo, zm))
 
 
-def pair_kernel(pos, mine, other, code):
-    core = pos[0]
+def pair_kernel(marks, mine, other, code):
+    core = marks[0:1, :]
     first_half = iota((8, LZ), 0) < 4
     for i in range(CHIPS):
         ma, mb = mine[i, 0:8, :], mine[i, 8:16, :]
@@ -329,8 +330,8 @@
         code[i] = q.astype(jnp.int32).astype(jnp.int16)
 
 
-def final_kernel(pos, code, z_mine, z_other, x_image, z_image):
-    front = pos[1] < 2
+def final_kernel(marks, code, z_mine, z_other, x_image, z_image):
+    front = marks[1:2, :] < 2
     a = b = deep = jnp.zeros((8, LZ), F32)
     for i in range(CHIPS):
         q = code[i].astype(F32)
@@ -355,7 +356,7 @@
 
 def call(kernel, out_shape, scratch, cost, *operands, wide=False):
     specs = [
-        pl.BlockSpec(memory_space=pltpu.SMEM if a.shape == (3,) else pl.ANY if wide else pltpu.VMEM)
+        pl.BlockSpec(memory_space=pl.ANY if wide and a.ndim == 3 else pltpu.VMEM)
         for a in operands
     ]
     return pl.pallas_call(
@@ -414,8 +415,9 @@
 
 def body(intensity, membrane, synapse, transfer, occupancy):
     gx = ("z", "y", "core")
-    pos = jnp.stack([lax.axis_index("core"), lax.axis_index("x"), lax.axis_index(gx)]).astype(jnp.int32)
-    odd_x, face_a, face_b, even_x, intensity, membrane, synapse = faces(pos, intensity, membrane, synapse)
+    place = jnp.stack([lax.axis_index("core"), lax.axis_index("x"), lax.axis_index(gx)]).astype(jnp.int32)
+    marks = jnp.broadcast_to(jnp.pad(place, (0, 5))[:, None], (8, LZ))
+    odd_x, face_a, face_b, even_x, intensity, membrane, synapse = faces(marks, intensity, membrane, synapse)
     even = [p for i in range(0, 64, 2) for p in ((i, i + 1), (i + 1, i))]
     odd = [p for i in range(1, 64, 2) for p in ((i, (i + 1) % 64), ((i + 1) % 64, i))]
     odd_x = lax.ppermute(odd_x, gx, odd)
@@ -425,15 +427,15 @@
     transfer = jnp.pad(transfer, ((0, 4), (0, LZ - KNOTS)))
     deep = depths(intensity, membrane, synapse, transfer, occupancy)
     keep, send, z_keep, z_send = shades(
-        pos, intensity, *deep, odd_x, face_a, face_b, even_x
+        marks, intensity, *deep, odd_x, face_a, face_b, even_x
     )
     other = lax.ppermute(send, "core", [(0, 1), (1, 0)])
     z_other = lax.ppermute(z_send, "x", [(0, 1), (1, 0), (2, 3), (3, 2)])
-    (code,) = call(pair_kernel, [CODE], [], 10**6, pos, keep, other)
-    (z_pair,) = call(z_kernel, [ZPART], [], 10**11, pos, z_keep, z_other)
+    (code,) = call(pair_kernel, [CODE], [], 10**6, marks, keep, other)
+    (z_pair,) = call(z_kernel, [ZPART], [], 10**11, marks, z_keep, z_other)
     z_other = lax.ppermute(z_pair, "x", [(0, 3), (3, 0), (1, 2), (2, 1)])
     code = lax.all_to_all(code, ("z", "y"), split_axis=0, concat_axis=0, tiled=True)
-    return tuple(call(final_kernel, IMAGES, [], 10**6, pos, code, z_pair, z_other))
+    return tuple(call(final_kernel, IMAGES, [], 10**6, marks, code, z_pair, z_other))
 
 
 def solution(mesh):

time: 39.8 us -> 37.7 us (0.947)
  Pallas kernels: 10.5 us -> 7.82 us
  waiting for transfers between devices: 8.04 us -> 8.59 us
    pallas_call x6, Pallas kernels: 10.5 us -> 7.82 us  [call(): pl.pallas_call(kernel, out_shape=out_shape, in_specs=specs, out_specs=[pl...]
    all_to_all x1, waiting for transfers between devices: 4.89 us -> 5.43 us  [body(): lax.all_to_all(code, ('z', 'y'), split_axis=0, concat_axis=0, tiled=True)]
  transfers between devices with their start and end apart: 8 -> 8, of which waited for: 3 -> 3; matrix products, arithmetic and copies ran while one was open for 0% -> 0% of each run, Pallas kernels for 10% -> 8%
where the time goes in v5:
time: 37.7 us; the launch traced here: 37.6 us
  starting transfers between devices  20.2 us (54%)
  waiting for transfers between devices  8.59 us (23%)
  Pallas kernels  7.82 us (21%)
  between operations  0.7 us (2%)
    pallas_call x6, Pallas kernels, call(): pl.pallas_call(kernel, out_shape=out_shape, in_specs=specs, out_specs=[pl...  7.82 us
    ppermute x1, starting transfers between devices, body(): even_x = lax.ppermute(even_x, gx, even)  6.56 us
    all_to_all x1, waiting for transfers between devices, body(): lax.all_to_all(code, ('z', 'y'), split_axis=0, concat_axis=0, tiled=True)  5.43 us
    all_to_all x1, starting transfers between devices, body(): lax.all_to_all(code, ('z', 'y'), split_axis=0, concat_axis=0, tiled=True)  4.85 us
    ppermute x1, starting transfers between devices, body(): odd_x = lax.ppermute(odd_x, gx, odd)  2.77 us
    ppermute x1, waiting for transfers between devices, body(): z_other = lax.ppermute(z_pair, 'x', [(0, 3), (3, 0), (1, 2), (2, 1)])  1.98 us
    ppermute x1, starting transfers between devices, body(): z_other = lax.ppermute(z_pair, 'x', [(0, 3), (3, 0), (1, 2), (2, 1)])  1.9 us
    ppermute x1, starting transfers between devices, body(): face_b = lax.ppermute(face_b, 'x', [(1, 2), (2, 1), (3, 0), (0, 3)])  1.82 us
  transfers between devices with their start and end apart: 8, of which 3 were waited for; matrix products, arithmetic and copies ran while one was open for 0% of the time, Pallas kernels for 8%

profile of v5, /device:TPU:1, one launch (start us, length us, event | category | flops | bytes accessed | tf_op | source)
XLA Modules:
  0.0 37.6 jit_solution(4012246409984655373)
XLA Ops:
  0.6 0.1 pad_add_fusion
  0.7 0.1 broadcast_in_dim.2.marks
  0.8 1.4 %shard_map.68 = (bf16[256,128]{1,0:T(8,128)(2,1)S(1)}, f32[8,256]{1,0:T(8,128)S(1)}, f32[8,256]{1,0:T(8,128)S(1)}, bf16[256,128]{1,0:T(8,128)(2,1)S(1)}, bf16[8,...) custom-call(s32[8,128]{1,0:T(8,128)S(1)} %broadcast_in_dim.2.marks, ...), custom_call_target="tpu_custom_call" | custom-call | flops 1000000 | bytes 1048576 | tf_op jit(solution)/shard_map/pallas_call | solution.py:362
  2.2 2.8 %collective-permute-start = (bf16[256,128]{1,0:T(8,128)(2,1)S(1)}, bf16[256,128]{1,0:T(8,128)(2,1)S(1)}, u32[]{:S(2)}, u32[]{:S(2)}) collective-permute-start(bf16[256,128]{1,0:T(8,128)(2,1)S(1)} %get-tuple-element.34), channel_id=1, source_target_pairs={{4,8},{8,4},{12,16},{16,12},{20,24},{24,20},{28,32},{32,28},{36,40... | collective-permute-start | bytes 196616 | tf_op jit(solution)/shard_map/ppermute | solution.py:423
  5.0 6.6 %collective-permute-start.3 = (bf16[256,128]{1,0:T(8,128)(2,1)S(1)}, bf16[256,128]{1,0:T(8,128)(2,1)S(1)}, u32[]{:S(2)}, u32[]{:S(2)}) collective-permute-start(bf16[256,128]{1,0:T(8,128)(2,1)S(1)} %get-tuple-element.37), channel_id=1, source_target_pairs={{0,4},{4,0},{8,12},{12,8},{16,20},{20,16},{24,28},{28,24},{32,36},... | collective-permute-start | bytes 196616 | tf_op jit(solution)/shard_map/ppermute | solution.py:426
  11.5 1.2 %collective-permute-start.1 = (f32[8,256]{1,0:T(8,128)S(1)}, f32[8,256]{1,0:T(8,128)S(1)}, u32[]{:S(2)}, u32[]{:S(2)}) collective-permute-start(f32[8,256]{1,0:T(8,128)S(1)} %get-tuple-element.35), channel_id=1, source_target_pairs={{0,1},{1,0},{2,3},{3,2},{4,5},{5,4},{6,7},{7,6},{8,9},{9,8},{10,11... | collective-permute-start | bytes 24584 | tf_op jit(solution)/shard_map/ppermute | solution.py:424
  12.8 1.8 %collective-permute-start.2 = (f32[8,256]{1,0:T(8,128)S(1)}, f32[8,256]{1,0:T(8,128)S(1)}, u32[]{:S(2)}, u32[]{:S(2)}) collective-permute-start(f32[8,256]{1,0:T(8,128)S(1)} %get-tuple-element.36), channel_id=1, source_target_pairs={{1,2},{2,1},{3,0},{0,3},{5,6},{6,5},{7,4},{4,7},{9,10},{10,9},{11,... | collective-permute-start | bytes 24584 | tf_op jit(solution)/shard_map/ppermute | solution.py:425
  14.6 0.1 copy.7.occ
  14.7 2.2 %shard_map.69 = (f32[8,256,128]{2,1,0:T(8,128)S(1)}, f32[8,256,128]{2,1,0:T(8,128)S(1)}, f32[8,256,128]{2,1,0:T(8,128)S(1)}, s32[8,256,128]{2,1,0:T(8,128)S(1)},...) custom-call(bf16[8,256,128]{2,1,0:T(8,128)(2,1)S(1)} %get-tuple-elem, ...), custom_call_target="tpu_custom_call" | custom-call | flops 100000000 | bytes 1048576 | tf_op jit(solution)/shard_map/pallas_call | solution.py:362
  16.8 0.0 collective-permute-done.1.face_a
  16.8 0.0 collective-permute-done.2.face_b
  16.8 0.0 collective-permute-done.odd_x
  16.8 0.0 collective-permute-done.3.even_x
  16.8 2.7 %shard_map.70 = (f32[32,16,128]{2,1,0:T(8,128)S(1)}, f32[32,16,128]{2,1,0:T(8,128)S(1)}, f32[32,128]{1,0:T(8,128)S(1)}, f32[32,128]{1,0:T(8,128)S(1)}) custom-call(s32[8,128]{1,0:T(8,128)S(1)} %broadcast_in_dim.2.marks, bf16[8,256,128]{2,1,0:T(8,128)(2,1)S(1)} %get-tuple-element.22.inten, f32[8,256,128]{2,1,0:T(8,128)S(1)} %get-tuple-element.25.weight_x, ...), custom_call_target="tpu_custom_call" | custom-call | flops 100000000 | bytes 1048576 | tf_op jit(solution)/shard_map/pallas_call | solution.py:362
  19.6 1.1 %collective-permute-start.4 = (f32[32,16,128]{2,1,0:T(8,128)S(1)}, f32[32,16,128]{2,1,0:T(8,128)S(1)}, u32[]{:S(2)}, u32[]{:S(2)}) collective-permute-start(f32[32,16,128]{2,1,0:T(8,128)S(1)} %get-tuple-element.39), channel_id=1, source_target_pairs={{0,4},{4,0},{1,5},{5,1},{2,6},{6,2},{3,7},{7,3},{8,12},{12,8},{9,1... | collective-permute-start | bytes 786440 | tf_op jit(solution)/shard_map/ppermute | solution.py:432
  20.7 0.0 collective-permute-start.5
  20.7 1.2 %collective-permute-done.4.other = f32[32,16,128]{2,1,0:T(8,128)S(1)} collective-permute-done((f32[32,16,128]{2,1,0:T(8,128)S(1)}, f32[32,16,128]{2,1,0:T(8,128)S(1)}, u32[]{:S(2)}, u32[]{:S(2)}) %collective-permute-start.4) | collective-permute-done | bytes 262176 | tf_op jit(solution)/shard_map/ppermute | solution.py:432
  21.8 0.8 %shard_map.71 = s16[32,16,128]{2,1,0:T(8,128)(2,1)} custom-call(s32[8,128]{1,0:T(8,128)S(1)} %broadcast_in_dim.2.marks, f32[32,16,128]{2,1,0:T(8,128)S(1)} %get-tuple-element.38.mine, f32[32,16,128]{2,1,0:T(8,128)S(1)} %collective-permute-done.4.other), custom_call_target="tpu_custom_call" | custom-call | flops 1000000 | bytes 1048576 | tf_op jit(solution)/shard_map/pallas_call | solution.py:362
  22.6 4.9 %all-to-all-start = ((s16[32,16,128]{2,1,0:T(8,128)(2,1)}), s16[32,16,128]{2,1,0:T(8,128)(2,1)S(1)}, u32[]{:S(2)}, u32[]{:S(2)}) async-start(s16[32,16,128]{2,1,0:T(8,128)(2,1)} %shard_map.71), calls=%async_computation | async-start | bytes 262144 | tf_op jit(solution)/shard_map/all_to_all | solution.py:437
  27.5 0.0 collective-permute-done.5.z_other
  27.5 1.9 %collective-permute-start.6 = (f32[32,128]{1,0:T(8,128)S(1)}, f32[32,128]{1,0:T(8,128)S(1)}, u32[]{:S(2)}, u32[]{:S(2)}) collective-permute-start(f32[32,128]{1,0:T(8,128)S(1)} %shard_map.72.z_mine), channel_id=1, source_target_pairs={{0,3},{3,0},{1,2},{2,1},{4,7},{7,4},{5,6},{6,5},{8,11},{11,8},{9,1... | collective-permute-start | bytes 49160 | tf_op jit(solution)/shard_map/ppermute | solution.py:436
  29.4 2.0 %collective-permute-done.6.z_other = f32[32,128]{1,0:T(8,128)S(1)} collective-permute-done((f32[32,128]{1,0:T(8,128)S(1)}, f32[32,128]{1,0:T(8,128)S(1)}, u32[]{:S(2)}, u32[]{:S(2)}) %collective-permute-start.6) | collective-permute-done | bytes 16416 | tf_op jit(solution)/shard_map/ppermute | solution.py:436
  31.4 5.4 %all-to-all-done.code = s16[32,16,128]{2,1,0:T(8,128)(2,1)S(1)} async-done(((s16[32,16,128]{2,1,0:T(8,128)(2,1)}), s16[32,16,128]{2,1,0:T(8,128)(2,1)S(1)}, u32[]{:S(2)}, u32[]{:S(2)}) %all-to-all-start) | async-done | bytes 131104 | tf_op jit(solution)/shard_map/all_to_all | solution.py:437
  36.8 0.7 %shard_map.73 = (f32[4,4,128]{2,1,0:T(4,128)}, f32[4,8,64]{2,1,0:T(8,128)}) custom-call(s32[8,128]{1,0:T(8,128)S(1)} %broadcast_in_dim.2.marks, s16[32,16,128]{2,1,0:T(8,128)(2,1)S(1)} %all-to-all-done.code, f32[32,128]{1,0:T(8,128)S(1)} %shard_map.72.z_mine, f32[32,128]{1,0:T(8,128)S(1)} %collective-permute-done.6.z_other), custom_call_target="tpu_custom_call" | custom-call | flops 1000000 | bytes 1048576 | tf_op jit(solution)/shard_map/pallas_call | solution.py:362
  (7 shorter events, 0.0 us)
Async XLA Ops:
  0.8 13.8 %copy-start = (s32[1,32,16]{1,2,0:T(8,128)S(1)}, s32[1,32,16]{1,2,0:T(8,128)}, u32[]{:S(2)}) copy-start(s32[1,32,16]{1,2,0:T(8,128)} %param.9) | copy-start | bytes 6148
  2.2 14.6 %collective-permute-start = (bf16[256,128]{1,0:T(8,128)(2,1)S(1)}, bf16[256,128]{1,0:T(8,128)(2,1)S(1)}, u32[]{:S(2)}, u32[]{:S(2)}) collective-permute-start(bf16[256,128]{1,0:T(8,128)(2,1)S(1)} %get-tuple-element.34), channel_id=1, source_target_pairs={{4,8},{8,4},{12,16},{16,12},{20,24},{24,20},{28,32},{32,28},{36,40... | collective-permute-start | bytes 196616 | tf_op jit(solution)/shard_map/ppermute | solution.py:423
  5.0 11.9 %collective-permute-start.3 = (bf16[256,128]{1,0:T(8,128)(2,1)S(1)}, bf16[256,128]{1,0:T(8,128)(2,1)S(1)}, u32[]{:S(2)}, u32[]{:S(2)}) collective-permute-start(bf16[256,128]{1,0:T(8,128)(2,1)S(1)} %get-tuple-element.37), channel_id=1, source_target_pairs={{0,4},{4,0},{8,12},{12,8},{16,20},{20,16},{24,28},{28,24},{32,36},... | collective-permute-start | bytes 196616 | tf_op jit(solution)/shard_map/ppermute | solution.py:426
  11.5 5.3 %collective-permute-start.1 = (f32[8,256]{1,0:T(8,128)S(1)}, f32[8,256]{1,0:T(8,128)S(1)}, u32[]{:S(2)}, u32[]{:S(2)}) collective-permute-start(f32[8,256]{1,0:T(8,128)S(1)} %get-tuple-element.35), channel_id=1, source_target_pairs={{0,1},{1,0},{2,3},{3,2},{4,5},{5,4},{6,7},{7,6},{8,9},{9,8},{10,11... | collective-permute-start | bytes 24584 | tf_op jit(solution)/shard_map/ppermute | solution.py:424
  12.8 1.9 %copy-start.1 = (f32[4,16]{1,0:T(4,128)S(1)}, f32[4,16]{1,0:T(4,128)}, u32[]{:S(2)}) copy-start(f32[4,16]{1,0:T(4,128)} %param.8) | copy-start | bytes 772
  12.8 4.1 %collective-permute-start.2 = (f32[8,256]{1,0:T(8,128)S(1)}, f32[8,256]{1,0:T(8,128)S(1)}, u32[]{:S(2)}, u32[]{:S(2)}) collective-permute-start(f32[8,256]{1,0:T(8,128)S(1)} %get-tuple-element.36), channel_id=1, source_target_pairs={{1,2},{2,1},{3,0},{0,3},{5,6},{6,5},{7,4},{4,7},{9,10},{10,9},{11,... | collective-permute-start | bytes 24584 | tf_op jit(solution)/shard_map/ppermute | solution.py:425
  19.6 2.2 %collective-permute-start.4 = (f32[32,16,128]{2,1,0:T(8,128)S(1)}, f32[32,16,128]{2,1,0:T(8,128)S(1)}, u32[]{:S(2)}, u32[]{:S(2)}) collective-permute-start(f32[32,16,128]{2,1,0:T(8,128)S(1)} %get-tuple-element.39), channel_id=1, source_target_pairs={{0,4},{4,0},{1,5},{5,1},{2,6},{6,2},{3,7},{7,3},{8,12},{12,8},{9,1... | collective-permute-start | bytes 786440 | tf_op jit(solution)/shard_map/ppermute | solution.py:432
  20.7 6.8 %collective-permute-start.5 = (f32[32,128]{1,0:T(8,128)S(1)}, f32[32,128]{1,0:T(8,128)S(1)}, u32[]{:S(2)}, u32[]{:S(2)}) collective-permute-start(f32[32,128]{1,0:T(8,128)S(1)} %get-tuple-element.41), channel_id=1, source_target_pairs={{0,1},{1,0},{2,3},{3,2},{4,5},{5,4},{6,7},{7,6},{8,9},{9,8},{10,11... | collective-permute-start | bytes 49160 | tf_op jit(solution)/shard_map/ppermute | solution.py:433
  22.6 14.2 %all-to-all-start = ((s16[32,16,128]{2,1,0:T(8,128)(2,1)}), s16[32,16,128]{2,1,0:T(8,128)(2,1)S(1)}, u32[]{:S(2)}, u32[]{:S(2)}) async-start(s16[32,16,128]{2,1,0:T(8,128)(2,1)} %shard_map.71), calls=%async_computation | async-start | bytes 262144 | tf_op jit(solution)/shard_map/all_to_all | solution.py:437
  27.5 3.9 %collective-permute-start.6 = (f32[32,128]{1,0:T(8,128)S(1)}, f32[32,128]{1,0:T(8,128)S(1)}, u32[]{:S(2)}, u32[]{:S(2)}) collective-permute-start(f32[32,128]{1,0:T(8,128)S(1)} %shard_map.72.z_mine), channel_id=1, source_target_pairs={{0,3},{3,0},{1,2},{2,1},{4,7},{7,4},{5,6},{6,5},{8,11},{11,8},{9,1... | collective-permute-start | bytes 49160 | tf_op jit(solution)/shard_map/ppermute | solution.py:436

commit v6 on v5

--- a/solution.py
+++ b/solution.py
@@ -11,6 +11,7 @@
 KNOTS = 16
 ROWS = 64
 CHIPS = 32
+EARLY = 1
 ACROSS = ()
 WIDE = 52 * 2**20
 F32, BF16 = jnp.float32, jnp.bfloat16
@@ -111,14 +112,15 @@
 
 def depth_kernel(
     inten, memb, syn, transfer, occ,
-    weight_x, weight_z, steep, spot, along, tables, own_x, total_x, total_z,
+    weight_x, weight_z, steep, hue, spot, along, tables, own_x, total_x, total_z,
     occ_rows, sigma, prefix, parts, columns,
 ):
     scale = -2.0 / (LX * 64) / LN2
     dense = knot_table(transfer, 3, scale, False)
-    for c in range(3):
-        for i, table in enumerate(knot_table(transfer, c, 0.7, c in ACROSS)):
-            tables[c, i] = table
+    knots = [knot_table(transfer, c, 0.7, c in ACROSS) for c in range(3)]
+    for c in range(EARLY, 3):
+        for i, table in enumerate(knots[c]):
+            tables[c - EARLY, i] = table
     spread = as_bf16(iota((KNOTS, LZ), 1) // 8 == iota((KNOTS, LZ), 0))
     occ_rows[...] = mxu(occ[0].astype(F32).astype(BF16), spread, NN)
     r, k = iota((H, H), 0), iota((H, H), 1)
@@ -146,6 +148,8 @@
                 index, frac = lookup(inten[x, rows, :].astype(F32))
                 spot[x, rows, :] = index
                 along[x, rows, :] = frac
+                for c in range(EARLY):
+                    hue[c, x, rows, :] = interpolate(knots[c], index, frac)
                 mem = memb[x, rows, :].astype(F32)
                 sy = syn[x, rows, :].astype(F32)
                 depth = interpolate(dense, index, frac) + mem * (1.5 * scale)
@@ -202,7 +206,7 @@
 
 
 def shade_kernel(
-    marks, inten, weight_x, weight_z, steep, spot, along, tables, own_x, total_x, total_z,
+    marks, inten, weight_x, weight_z, steep, hue, spot, along, tables, own_x, total_x, total_z,
     odd_x, face_a, face_b, even_x,
     keep, send, z_keep, z_send,
     pad, halo, left, dz, image, columns,
@@ -225,7 +229,7 @@
     lanes = iota((ROWS, LZ), 1)
     lane = iota((16, LZ), 1)
     first_half = iota((8, LZ), 0) < 4
-    knots = [[tables[c, i] for i in range(2 if c in ACROSS else 4)] for c in range(3)]
+    knots = [[tables[c, i] for i in range(2 if c + EARLY in ACROSS else 4)] for c in range(3 - EARLY)]
 
     def slopes(j):
         buf, base = j % 2, j * ROWS
@@ -252,7 +256,7 @@
             lit_z = (0.3 / 0.7 + jnp.abs(grad_z) * norm) * weight_z[x, rows, :]
             index, frac = spot[x, rows, :], along[x, rows, :]
             for c in range(3):
-                color = interpolate(knots[c], index, frac)
+                color = hue[c, x, rows, :] if c < EARLY else interpolate(knots[c - EARLY], index, frac)
                 acc[c] = acc[c] + lit_x * color
                 summed = jnp.sum(lit_z * color, axis=1, keepdims=True)
                 column = jnp.where(lane == c * LX + x, summed, column)
@@ -385,8 +389,10 @@
 
 
 def depths(intensity, membrane, synapse, transfer, occupancy):
-    outs = [BRICK] * 3 + [jax.ShapeDtypeStruct((LX, H, LZ), jnp.int32), BRICK] + [
-        jax.ShapeDtypeStruct((3, 4, 8, LZ), F32),
+    outs = [BRICK] * 3 + [jax.ShapeDtypeStruct((EARLY, LX, H, LZ), F32)] + [
+        jax.ShapeDtypeStruct((LX, H, LZ), jnp.int32),
+        BRICK,
+        jax.ShapeDtypeStruct((3 - EARLY, 4, 8, LZ), F32),
         jax.ShapeDtypeStruct((2, H, LZ), F32),
         jax.ShapeDtypeStruct((H, LZ), F32),
         jax.ShapeDtypeStruct((4 * LX, H), F32),

time: 37.7 us -> 37.5 us (level)
  transfers between devices with their start and end apart: 8 -> 8, of which waited for: 3 -> 3; matrix products, arithmetic and copies ran while one was open for 0% -> 0% of each run, Pallas kernels for 8% -> 9%
where the time goes in v6:
time: 37.5 us; the launch traced here: 37.3 us
  starting transfers between devices  20 us (53%)
  waiting for transfers between devices  8.47 us (23%)
  Pallas kernels  7.87 us (21%)
  between operations  0.7 us (2%)
    pallas_call x6, Pallas kernels, call(): pl.pallas_call(kernel, out_shape=out_shape, in_specs=specs, out_specs=[pl...  7.87 us
    ppermute x1, starting transfers between devices, body(): even_x = lax.ppermute(even_x, gx, even)  6.56 us
    all_to_all x1, waiting for transfers between devices, body(): lax.all_to_all(code, ('z', 'y'), split_axis=0, concat_axis=0, tiled=True)  5.43 us
    all_to_all x1, starting transfers between devices, body(): lax.all_to_all(code, ('z', 'y'), split_axis=0, concat_axis=0, tiled=True)  4.85 us
    ppermute x1, starting transfers between devices, body(): odd_x = lax.ppermute(odd_x, gx, odd)  2.77 us
    ppermute x1, waiting for transfers between devices, body(): z_other = lax.ppermute(z_pair, 'x', [(0, 3), (3, 0), (1, 2), (2, 1)])  1.98 us
    ppermute x1, starting transfers between devices, body(): z_other = lax.ppermute(z_pair, 'x', [(0, 3), (3, 0), (1, 2), (2, 1)])  1.9 us
    ppermute x1, starting transfers between devices, body(): face_b = lax.ppermute(face_b, 'x', [(1, 2), (2, 1), (3, 0), (0, 3)])  1.82 us
  transfers between devices with their start and end apart: 8, of which 3 were waited for; matrix products, arithmetic and copies ran while one was open for 0% of the time, Pallas kernels for 9%

profile of v6, /device:TPU:1, one launch (start us, length us, event | category | flops | bytes accessed | tf_op | source)
XLA Modules:
  0.0 37.3 jit_solution(4615311393411772492)
XLA Ops:
  0.6 0.1 pad_add_fusion
  0.7 0.1 broadcast_in_dim.2.marks
  0.8 1.4 %shard_map.68 = (bf16[256,128]{1,0:T(8,128)(2,1)S(1)}, f32[8,256]{1,0:T(8,128)S(1)}, f32[8,256]{1,0:T(8,128)S(1)}, bf16[256,128]{1,0:T(8,128)(2,1)S(1)}, bf16[8,...) custom-call(s32[8,128]{1,0:T(8,128)S(1)} %broadcast_in_dim.2.marks, ...), custom_call_target="tpu_custom_call" | custom-call | flops 1000000 | bytes 1048576 | tf_op jit(solution)/shard_map/pallas_call | solution.py:366
  2.2 2.8 %collective-permute-start = (bf16[256,128]{1,0:T(8,128)(2,1)S(1)}, bf16[256,128]{1,0:T(8,128)(2,1)S(1)}, u32[]{:S(2)}, u32[]{:S(2)}) collective-permute-start(bf16[256,128]{1,0:T(8,128)(2,1)S(1)} %get-tuple-element.36), channel_id=1, source_target_pairs={{4,8},{8,4},{12,16},{16,12},{20,24},{24,20},{28,32},{32,28},{36,40... | collective-permute-start | bytes 196616 | tf_op jit(solution)/shard_map/ppermute | solution.py:429
  5.0 6.6 %collective-permute-start.3 = (bf16[256,128]{1,0:T(8,128)(2,1)S(1)}, bf16[256,128]{1,0:T(8,128)(2,1)S(1)}, u32[]{:S(2)}, u32[]{:S(2)}) collective-permute-start(bf16[256,128]{1,0:T(8,128)(2,1)S(1)} %get-tuple-element.39), channel_id=1, source_target_pairs={{0,4},{4,0},{8,12},{12,8},{16,20},{20,16},{24,28},{28,24},{32,36},... | collective-permute-start | bytes 196616 | tf_op jit(solution)/shard_map/ppermute | solution.py:432
  11.5 1.2 %collective-permute-start.1 = (f32[8,256]{1,0:T(8,128)S(1)}, f32[8,256]{1,0:T(8,128)S(1)}, u32[]{:S(2)}, u32[]{:S(2)}) collective-permute-start(f32[8,256]{1,0:T(8,128)S(1)} %get-tuple-element.37), channel_id=1, source_target_pairs={{0,1},{1,0},{2,3},{3,2},{4,5},{5,4},{6,7},{7,6},{8,9},{9,8},{10,11... | collective-permute-start | bytes 24584 | tf_op jit(solution)/shard_map/ppermute | solution.py:430
  12.8 1.8 %collective-permute-start.2 = (f32[8,256]{1,0:T(8,128)S(1)}, f32[8,256]{1,0:T(8,128)S(1)}, u32[]{:S(2)}, u32[]{:S(2)}) collective-permute-start(f32[8,256]{1,0:T(8,128)S(1)} %get-tuple-element.38), channel_id=1, source_target_pairs={{1,2},{2,1},{3,0},{0,3},{5,6},{6,5},{7,4},{4,7},{9,10},{10,9},{11,... | collective-permute-start | bytes 24584 | tf_op jit(solution)/shard_map/ppermute | solution.py:431
  14.6 0.1 copy.7.occ
  14.7 2.4 %shard_map.69 = (f32[8,256,128]{2,1,0:T(8,128)S(1)}, f32[8,256,128]{2,1,0:T(8,128)S(1)}, f32[8,256,128]{2,1,0:T(8,128)S(1)}, f32[1,8,256,128]{3,2,1,0:T(8,128)S(...) custom-call(bf16[8,256,128]{2,1,0:T(8,128)(2,1)S(1)} %get-tuple-elem, ...), custom_call_target="tpu_custom_call" | custom-call | flops 100000000 | bytes 1048576 | tf_op jit(solution)/shard_map/pallas_call | solution.py:366
  17.1 0.0 collective-permute-done.1.face_a
  17.1 0.0 collective-permute-done.2.face_b
  17.1 0.0 collective-permute-done.odd_x
  17.1 0.0 collective-permute-done.3.even_x
  17.1 2.5 %shard_map.70 = (f32[32,16,128]{2,1,0:T(8,128)S(1)}, f32[32,16,128]{2,1,0:T(8,128)S(1)}, f32[32,128]{1,0:T(8,128)S(1)}, f32[32,128]{1,0:T(8,128)S(1)}) custom-call(s32[8,128]{1,0:T(8,128)S(1)} %broadcast_in_dim.2.marks, bf16[8,256,128]{2,1,0:T(8,128)(2,1)S(1)} %get-tuple-element.23.inten, f32[8,256,128]{2,1,0:T(8,128)S(1)} %get-tuple-element.26.weight_x, ...), custom_call_target="tpu_custom_call" | custom-call | flops 100000000 | bytes 1048576 | tf_op jit(solution)/shard_map/pallas_call | solution.py:366
  19.6 0.8 %collective-permute-start.4 = (f32[32,16,128]{2,1,0:T(8,128)S(1)}, f32[32,16,128]{2,1,0:T(8,128)S(1)}, u32[]{:S(2)}, u32[]{:S(2)}) collective-permute-start(f32[32,16,128]{2,1,0:T(8,128)S(1)} %get-tuple-element.41), channel_id=1, source_target_pairs={{0,4},{4,0},{1,5},{5,1},{2,6},{6,2},{3,7},{7,3},{8,12},{12,8},{9,1... | collective-permute-start | bytes 786440 | tf_op jit(solution)/shard_map/ppermute | solution.py:438
  20.4 0.1 collective-permute-start.5
  20.6 1.0 %collective-permute-done.4.other = f32[32,16,128]{2,1,0:T(8,128)S(1)} collective-permute-done((f32[32,16,128]{2,1,0:T(8,128)S(1)}, f32[32,16,128]{2,1,0:T(8,128)S(1)}, u32[]{:S(2)}, u32[]{:S(2)}) %collective-permute-start.4) | collective-permute-done | bytes 262176 | tf_op jit(solution)/shard_map/ppermute | solution.py:438
  21.6 0.8 %shard_map.71 = s16[32,16,128]{2,1,0:T(8,128)(2,1)} custom-call(s32[8,128]{1,0:T(8,128)S(1)} %broadcast_in_dim.2.marks, f32[32,16,128]{2,1,0:T(8,128)S(1)} %get-tuple-element.40.mine, f32[32,16,128]{2,1,0:T(8,128)S(1)} %collective-permute-done.4.other), custom_call_target="tpu_custom_call" | custom-call | flops 1000000 | bytes 1048576 | tf_op jit(solution)/shard_map/pallas_call | solution.py:366
  22.4 4.9 %all-to-all-start = ((s16[32,16,128]{2,1,0:T(8,128)(2,1)}), s16[32,16,128]{2,1,0:T(8,128)(2,1)S(1)}, u32[]{:S(2)}, u32[]{:S(2)}) async-start(s16[32,16,128]{2,1,0:T(8,128)(2,1)} %shard_map.71), calls=%async_computation | async-start | bytes 262144 | tf_op jit(solution)/shard_map/all_to_all | solution.py:443
  27.3 0.0 collective-permute-done.5.z_other
  27.3 1.9 %collective-permute-start.6 = (f32[32,128]{1,0:T(8,128)S(1)}, f32[32,128]{1,0:T(8,128)S(1)}, u32[]{:S(2)}, u32[]{:S(2)}) collective-permute-start(f32[32,128]{1,0:T(8,128)S(1)} %shard_map.72.z_mine), channel_id=1, source_target_pairs={{0,3},{3,0},{1,2},{2,1},{4,7},{7,4},{5,6},{6,5},{8,11},{11,8},{9,1... | collective-permute-start | bytes 49160 | tf_op jit(solution)/shard_map/ppermute | solution.py:442
  29.2 2.0 %collective-permute-done.6.z_other = f32[32,128]{1,0:T(8,128)S(1)} collective-permute-done((f32[32,128]{1,0:T(8,128)S(1)}, f32[32,128]{1,0:T(8,128)S(1)}, u32[]{:S(2)}, u32[]{:S(2)}) %collective-permute-start.6) | collective-permute-done | bytes 16416 | tf_op jit(solution)/shard_map/ppermute | solution.py:442
  31.2 5.4 %all-to-all-done.code = s16[32,16,128]{2,1,0:T(8,128)(2,1)S(1)} async-done(((s16[32,16,128]{2,1,0:T(8,128)(2,1)}), s16[32,16,128]{2,1,0:T(8,128)(2,1)S(1)}, u32[]{:S(2)}, u32[]{:S(2)}) %all-to-all-start) | async-done | bytes 131104 | tf_op jit(solution)/shard_map/all_to_all | solution.py:443
  36.6 0.7 %shard_map.73 = (f32[4,4,128]{2,1,0:T(4,128)}, f32[4,8,64]{2,1,0:T(8,128)}) custom-call(s32[8,128]{1,0:T(8,128)S(1)} %broadcast_in_dim.2.marks, s16[32,16,128]{2,1,0:T(8,128)(2,1)S(1)} %all-to-all-done.code, f32[32,128]{1,0:T(8,128)S(1)} %shard_map.72.z_mine, f32[32,128]{1,0:T(8,128)S(1)} %collective-permute-done.6.z_other), custom_call_target="tpu_custom_call" | custom-call | flops 1000000 | bytes 1048576 | tf_op jit(solution)/shard_map/pallas_call | solution.py:366
  (7 shorter events, 0.0 us)
Async XLA Ops:
  0.8 13.8 %copy-start = (s32[1,32,16]{1,2,0:T(8,128)S(1)}, s32[1,32,16]{1,2,0:T(8,128)}, u32[]{:S(2)}) copy-start(s32[1,32,16]{1,2,0:T(8,128)} %param.9) | copy-start | bytes 6148
  2.2 14.9 %collective-permute-start = (bf16[256,128]{1,0:T(8,128)(2,1)S(1)}, bf16[256,128]{1,0:T(8,128)(2,1)S(1)}, u32[]{:S(2)}, u32[]{:S(2)}) collective-permute-start(bf16[256,128]{1,0:T(8,128)(2,1)S(1)} %get-tuple-element.36), channel_id=1, source_target_pairs={{4,8},{8,4},{12,16},{16,12},{20,24},{24,20},{28,32},{32,28},{36,40... | collective-permute-start | bytes 196616 | tf_op jit(solution)/shard_map/ppermute | solution.py:429
  5.0 12.1 %collective-permute-start.3 = (bf16[256,128]{1,0:T(8,128)(2,1)S(1)}, bf16[256,128]{1,0:T(8,128)(2,1)S(1)}, u32[]{:S(2)}, u32[]{:S(2)}) collective-permute-start(bf16[256,128]{1,0:T(8,128)(2,1)S(1)} %get-tuple-element.39), channel_id=1, source_target_pairs={{0,4},{4,0},{8,12},{12,8},{16,20},{20,16},{24,28},{28,24},{32,36},... | collective-permute-start | bytes 196616 | tf_op jit(solution)/shard_map/ppermute | solution.py:432
  11.5 5.6 %collective-permute-start.1 = (f32[8,256]{1,0:T(8,128)S(1)}, f32[8,256]{1,0:T(8,128)S(1)}, u32[]{:S(2)}, u32[]{:S(2)}) collective-permute-start(f32[8,256]{1,0:T(8,128)S(1)} %get-tuple-element.37), channel_id=1, source_target_pairs={{0,1},{1,0},{2,3},{3,2},{4,5},{5,4},{6,7},{7,6},{8,9},{9,8},{10,11... | collective-permute-start | bytes 24584 | tf_op jit(solution)/shard_map/ppermute | solution.py:430
  12.8 1.9 %copy-start.1 = (f32[4,16]{1,0:T(4,128)S(1)}, f32[4,16]{1,0:T(4,128)}, u32[]{:S(2)}) copy-start(f32[4,16]{1,0:T(4,128)} %param.8) | copy-start | bytes 772
  12.8 4.3 %collective-permute-start.2 = (f32[8,256]{1,0:T(8,128)S(1)}, f32[8,256]{1,0:T(8,128)S(1)}, u32[]{:S(2)}, u32[]{:S(2)}) collective-permute-start(f32[8,256]{1,0:T(8,128)S(1)} %get-tuple-element.38), channel_id=1, source_target_pairs={{1,2},{2,1},{3,0},{0,3},{5,6},{6,5},{7,4},{4,7},{9,10},{10,9},{11,... | collective-permute-start | bytes 24584 | tf_op jit(solution)/shard_map/ppermute | solution.py:431
  19.6 2.0 %collective-permute-start.4 = (f32[32,16,128]{2,1,0:T(8,128)S(1)}, f32[32,16,128]{2,1,0:T(8,128)S(1)}, u32[]{:S(2)}, u32[]{:S(2)}) collective-permute-start(f32[32,16,128]{2,1,0:T(8,128)S(1)} %get-tuple-element.41), channel_id=1, source_target_pairs={{0,4},{4,0},{1,5},{5,1},{2,6},{6,2},{3,7},{7,3},{8,12},{12,8},{9,1... | collective-permute-start | bytes 786440 | tf_op jit(solution)/shard_map/ppermute | solution.py:438
  20.4 6.8 %collective-permute-start.5 = (f32[32,128]{1,0:T(8,128)S(1)}, f32[32,128]{1,0:T(8,128)S(1)}, u32[]{:S(2)}, u32[]{:S(2)}) collective-permute-start(f32[32,128]{1,0:T(8,128)S(1)} %get-tuple-element.43), channel_id=1, source_target_pairs={{0,1},{1,0},{2,3},{3,2},{4,5},{5,4},{6,7},{7,6},{8,9},{9,8},{10,11... | collective-permute-start | bytes 49160 | tf_op jit(solution)/shard_map/ppermute | solution.py:439
  22.4 14.2 %all-to-all-start = ((s16[32,16,128]{2,1,0:T(8,128)(2,1)}), s16[32,16,128]{2,1,0:T(8,128)(2,1)S(1)}, u32[]{:S(2)}, u32[]{:S(2)}) async-start(s16[32,16,128]{2,1,0:T(8,128)(2,1)} %shard_map.71), calls=%async_computation | async-start | bytes 262144 | tf_op jit(solution)/shard_map/all_to_all | solution.py:443
  27.3 3.9 %collective-permute-start.6 = (f32[32,128]{1,0:T(8,128)S(1)}, f32[32,128]{1,0:T(8,128)S(1)}, u32[]{:S(2)}, u32[]{:S(2)}) collective-permute-start(f32[32,128]{1,0:T(8,128)S(1)} %shard_map.72.z_mine), channel_id=1, source_target_pairs={{0,3},{3,0},{1,2},{2,1},{4,7},{7,4},{5,6},{6,5},{8,11},{11,8},{9,1... | collective-permute-start | bytes 49160 | tf_op jit(solution)/shard_map/ppermute | solution.py:442

commit v7 on v6

--- a/solution.py
+++ b/solution.py
@@ -317,9 +317,10 @@
     z_pair[...] = z_merge(jnp.where(even, zm, zo), jnp.where(even, zo, zm))
 
 
-def pair_kernel(marks, mine, other, code):
+def pair_kernel(marks, mine, other, code_out, code, sems):
     core = marks[0:1, :]
     first_half = iota((8, LZ), 0) < 4
+    copies = []
     for i in range(CHIPS):
         ma, mb = mine[i, 0:8, :], mine[i, 8:16, :]
         oa, ob = other[i, 0:8, :], other[i, 8:16, :]
@@ -332,6 +333,12 @@
         q = jnp.log2(jnp.maximum(v, 2.0**-25)) * CODE_SCALE + (CODE_MID * CODE_SCALE)
         q = jnp.where(v > 2.0**-25, jnp.round(jnp.minimum(q, 32766.0)), -32768.0)
         code[i] = q.astype(jnp.int32).astype(jnp.int16)
+        if i % 8 == 7:
+            part = pl.ds(i - 7, 8)
+            copies.append(pltpu.make_async_copy(code.at[part], code_out.at[part], sems.at[i // 8]))
+            copies[-1].start()
+    for copy in copies:
+        copy.wait()
 
 
 def final_kernel(marks, code, z_mine, z_other, x_image, z_image):
@@ -358,7 +365,7 @@
     z_image[3] = 1.0 - jnp.exp2(-image[3 * LX :])
 
 
-def call(kernel, out_shape, scratch, cost, *operands, wide=False):
+def call(kernel, out_shape, scratch, cost, *operands, wide=False, results=pltpu.VMEM):
     specs = [
         pl.BlockSpec(memory_space=pl.ANY if wide and a.ndim == 3 else pltpu.VMEM)
         for a in operands
@@ -367,7 +374,7 @@
         kernel,
         out_shape=out_shape,
         in_specs=specs,
-        out_specs=[pl.BlockSpec(memory_space=pltpu.VMEM)] * len(out_shape),
+        out_specs=[pl.BlockSpec(memory_space=results)] * len(out_shape),
         scratch_shapes=scratch,
         compiler_params=pltpu.CompilerParams(vmem_limit_bytes=WIDE if wide else 32 * 2**20),
         cost_estimate=pl.CostEstimate(flops=cost, bytes_accessed=2**20, transcendentals=0),
@@ -437,7 +444,8 @@
     )
     other = lax.ppermute(send, "core", [(0, 1), (1, 0)])
     z_other = lax.ppermute(z_send, "x", [(0, 1), (1, 0), (2, 3), (3, 2)])
-    (code,) = call(pair_kernel, [CODE], [], 10**6, marks, keep, other)
+    scratch = [pltpu.VMEM((CHIPS, 16, LZ), jnp.int16), pltpu.SemaphoreType.DMA((4,))]
+    (code,) = call(pair_kernel, [CODE], scratch, 10**6, marks, keep, other, results=pl.ANY)
     (z_pair,) = call(z_kernel, [ZPART], [], 10**11, marks, z_keep, z_other)
     z_other = lax.ppermute(z_pair, "x", [(0, 3), (3, 0), (1, 2), (2, 1)])
     code = lax.all_to_all(code, ("z", "y"), split_axis=0, concat_axis=0, tiled=True)

time: 37.5 us -> 37.5 us (level)
  no operation moved by 1% of the time
where the time goes in v7:
time: 37.5 us; the launch traced here: 37.3 us
  starting transfers between devices  20.1 us (54%)
  waiting for transfers between devices  8.47 us (23%)
  Pallas kernels  7.86 us (21%)
  between operations  0.71 us (2%)
    pallas_call x6, Pallas kernels, call(): pl.pallas_call(kernel, out_shape=out_shape, in_specs=specs, out_specs=[pl...  7.86 us
    ppermute x1, starting transfers between devices, body(): even_x = lax.ppermute(even_x, gx, even)  6.56 us
    all_to_all x1, waiting for transfers between devices, body(): lax.all_to_all(code, ('z', 'y'), split_axis=0, concat_axis=0, tiled=True)  5.43 us
    all_to_all x1, starting transfers between devices, body(): lax.all_to_all(code, ('z', 'y'), split_axis=0, concat_axis=0, tiled=True)  4.86 us
    ppermute x1, starting transfers between devices, body(): odd_x = lax.ppermute(odd_x, gx, odd)  2.77 us
    ppermute x1, waiting for transfers between devices, body(): z_other = lax.ppermute(z_pair, 'x', [(0, 3), (3, 0), (1, 2), (2, 1)])  1.98 us
    ppermute x1, starting transfers between devices, body(): z_other = lax.ppermute(z_pair, 'x', [(0, 3), (3, 0), (1, 2), (2, 1)])  1.9 us
    ppermute x1, starting transfers between devices, body(): face_b = lax.ppermute(face_b, 'x', [(1, 2), (2, 1), (3, 0), (0, 3)])  1.82 us
  transfers between devices with their start and end apart: 8, of which 3 were waited for; matrix products, arithmetic and copies ran while one was open for 0% of the time, Pallas kernels for 9%

profile of v7, /device:TPU:1, one launch (start us, length us, event | category | flops | bytes accessed | tf_op | source)
XLA Modules:
  0.0 37.3 jit_solution(15868926736327579074)
XLA Ops:
  0.6 0.1 pad_add_fusion
  0.7 0.1 broadcast_in_dim.2.marks
  0.8 1.4 %shard_map.68 = (bf16[256,128]{1,0:T(8,128)(2,1)S(1)}, f32[8,256]{1,0:T(8,128)S(1)}, f32[8,256]{1,0:T(8,128)S(1)}, bf16[256,128]{1,0:T(8,128)(2,1)S(1)}, bf16[8,...) custom-call(s32[8,128]{1,0:T(8,128)S(1)} %broadcast_in_dim.2.marks, ...), custom_call_target="tpu_custom_call" | custom-call | flops 1000000 | bytes 1048576 | tf_op jit(solution)/shard_map/pallas_call | solution.py:373
  2.2 2.8 %collective-permute-start = (bf16[256,128]{1,0:T(8,128)(2,1)S(1)}, bf16[256,128]{1,0:T(8,128)(2,1)S(1)}, u32[]{:S(2)}, u32[]{:S(2)}) collective-permute-start(bf16[256,128]{1,0:T(8,128)(2,1)S(1)} %get-tuple-element.36), channel_id=1, source_target_pairs={{4,8},{8,4},{12,16},{16,12},{20,24},{24,20},{28,32},{32,28},{36,40... | collective-permute-start | bytes 196616 | tf_op jit(solution)/shard_map/ppermute | solution.py:436
  5.0 6.6 %collective-permute-start.3 = (bf16[256,128]{1,0:T(8,128)(2,1)S(1)}, bf16[256,128]{1,0:T(8,128)(2,1)S(1)}, u32[]{:S(2)}, u32[]{:S(2)}) collective-permute-start(bf16[256,128]{1,0:T(8,128)(2,1)S(1)} %get-tuple-element.39), channel_id=1, source_target_pairs={{0,4},{4,0},{8,12},{12,8},{16,20},{20,16},{24,28},{28,24},{32,36},... | collective-permute-start | bytes 196616 | tf_op jit(solution)/shard_map/ppermute | solution.py:439
  11.5 1.2 %collective-permute-start.1 = (f32[8,256]{1,0:T(8,128)S(1)}, f32[8,256]{1,0:T(8,128)S(1)}, u32[]{:S(2)}, u32[]{:S(2)}) collective-permute-start(f32[8,256]{1,0:T(8,128)S(1)} %get-tuple-element.37), channel_id=1, source_target_pairs={{0,1},{1,0},{2,3},{3,2},{4,5},{5,4},{6,7},{7,6},{8,9},{9,8},{10,11... | collective-permute-start | bytes 24584 | tf_op jit(solution)/shard_map/ppermute | solution.py:437
  12.8 1.8 %collective-permute-start.2 = (f32[8,256]{1,0:T(8,128)S(1)}, f32[8,256]{1,0:T(8,128)S(1)}, u32[]{:S(2)}, u32[]{:S(2)}) collective-permute-start(f32[8,256]{1,0:T(8,128)S(1)} %get-tuple-element.38), channel_id=1, source_target_pairs={{1,2},{2,1},{3,0},{0,3},{5,6},{6,5},{7,4},{4,7},{9,10},{10,9},{11,... | collective-permute-start | bytes 24584 | tf_op jit(solution)/shard_map/ppermute | solution.py:438
  14.6 0.1 copy.7.occ
  14.7 2.4 %shard_map.69 = (f32[8,256,128]{2,1,0:T(8,128)S(1)}, f32[8,256,128]{2,1,0:T(8,128)S(1)}, f32[8,256,128]{2,1,0:T(8,128)S(1)}, f32[1,8,256,128]{3,2,1,0:T(8,128)S(...) custom-call(bf16[8,256,128]{2,1,0:T(8,128)(2,1)S(1)} %get-tuple-elem, ...), custom_call_target="tpu_custom_call" | custom-call | flops 100000000 | bytes 1048576 | tf_op jit(solution)/shard_map/pallas_call | solution.py:373
  17.1 0.0 collective-permute-done.1.face_a
  17.1 0.0 collective-permute-done.2.face_b
  17.1 0.0 collective-permute-done.odd_x
  17.1 0.0 collective-permute-done.3.even_x
  17.1 2.5 %shard_map.70 = (f32[32,16,128]{2,1,0:T(8,128)S(1)}, f32[32,16,128]{2,1,0:T(8,128)S(1)}, f32[32,128]{1,0:T(8,128)S(1)}, f32[32,128]{1,0:T(8,128)S(1)}) custom-call(s32[8,128]{1,0:T(8,128)S(1)} %broadcast_in_dim.2.marks, bf16[8,256,128]{2,1,0:T(8,128)(2,1)S(1)} %get-tuple-element.23.inten, f32[8,256,128]{2,1,0:T(8,128)S(1)} %get-tuple-element.26.weight_x, ...), custom_call_target="tpu_custom_call" | custom-call | flops 100000000 | bytes 1048576 | tf_op jit(solution)/shard_map/pallas_call | solution.py:373
  19.6 0.8 %collective-permute-start.4 = (f32[32,16,128]{2,1,0:T(8,128)S(1)}, f32[32,16,128]{2,1,0:T(8,128)S(1)}, u32[]{:S(2)}, u32[]{:S(2)}) collective-permute-start(f32[32,16,128]{2,1,0:T(8,128)S(1)} %get-tuple-element.41), channel_id=1, source_target_pairs={{0,4},{4,0},{1,5},{5,1},{2,6},{6,2},{3,7},{7,3},{8,12},{12,8},{9,1... | collective-permute-start | bytes 786440 | tf_op jit(solution)/shard_map/ppermute | solution.py:445
  20.4 0.1 collective-permute-start.5
  20.6 1.0 %collective-permute-done.4.other = f32[32,16,128]{2,1,0:T(8,128)S(1)} collective-permute-done((f32[32,16,128]{2,1,0:T(8,128)S(1)}, f32[32,16,128]{2,1,0:T(8,128)S(1)}, u32[]{:S(2)}, u32[]{:S(2)}) %collective-permute-start.4) | collective-permute-done | bytes 262176 | tf_op jit(solution)/shard_map/ppermute | solution.py:445
  21.6 0.8 %shard_map.71 = s16[32,16,128]{2,1,0:T(8,128)(2,1)} custom-call(s32[8,128]{1,0:T(8,128)S(1)} %broadcast_in_dim.2.marks, f32[32,16,128]{2,1,0:T(8,128)S(1)} %get-tuple-element.40.mine, f32[32,16,128]{2,1,0:T(8,128)S(1)} %collective-permute-done.4.other), custom_call_target="tpu_custom_call" | custom-call | flops 1000000 | bytes 1048576 | tf_op jit(solution)/shard_map/pallas_call | solution.py:373
  22.4 4.9 %all-to-all-start = ((s16[32,16,128]{2,1,0:T(8,128)(2,1)}), s16[32,16,128]{2,1,0:T(8,128)(2,1)S(1)}, u32[]{:S(2)}, u32[]{:S(2)}) async-start(s16[32,16,128]{2,1,0:T(8,128)(2,1)} %shard_map.71), calls=%async_computation | async-start | bytes 262144 | tf_op jit(solution)/shard_map/all_to_all | solution.py:451
  27.3 0.0 collective-permute-done.5.z_other
  27.3 1.9 %collective-permute-start.6 = (f32[32,128]{1,0:T(8,128)S(1)}, f32[32,128]{1,0:T(8,128)S(1)}, u32[]{:S(2)}, u32[]{:S(2)}) collective-permute-start(f32[32,128]{1,0:T(8,128)S(1)} %shard_map.72.z_mine), channel_id=1, source_target_pairs={{0,3},{3,0},{1,2},{2,1},{4,7},{7,4},{5,6},{6,5},{8,11},{11,8},{9,1... | collective-permute-start | bytes 49160 | tf_op jit(solution)/shard_map/ppermute | solution.py:450
  29.2 2.0 %collective-permute-done.6.z_other = f32[32,128]{1,0:T(8,128)S(1)} collective-permute-done((f32[32,128]{1,0:T(8,128)S(1)}, f32[32,128]{1,0:T(8,128)S(1)}, u32[]{:S(2)}, u32[]{:S(2)}) %collective-permute-start.6) | collective-permute-done | bytes 16416 | tf_op jit(solution)/shard_map/ppermute | solution.py:450
  31.2 5.4 %all-to-all-done.code = s16[32,16,128]{2,1,0:T(8,128)(2,1)S(1)} async-done(((s16[32,16,128]{2,1,0:T(8,128)(2,1)}), s16[32,16,128]{2,1,0:T(8,128)(2,1)S(1)}, u32[]{:S(2)}, u32[]{:S(2)}) %all-to-all-start) | async-done | bytes 131104 | tf_op jit(solution)/shard_map/all_to_all | solution.py:451
  36.6 0.7 %shard_map.73 = (f32[4,4,128]{2,1,0:T(4,128)}, f32[4,8,64]{2,1,0:T(8,128)}) custom-call(s32[8,128]{1,0:T(8,128)S(1)} %broadcast_in_dim.2.marks, s16[32,16,128]{2,1,0:T(8,128)(2,1)S(1)} %all-to-all-done.code, f32[32,128]{1,0:T(8,128)S(1)} %shard_map.72.z_mine, f32[32,128]{1,0:T(8,128)S(1)} %collective-permute-done.6.z_other), custom_call_target="tpu_custom_call" | custom-call | flops 1000000 | bytes 1048576 | tf_op jit(solution)/shard_map/pallas_call | solution.py:373
  (7 shorter events, 0.0 us)
Async XLA Ops:
  0.8 13.8 %copy-start = (s32[1,32,16]{1,2,0:T(8,128)S(1)}, s32[1,32,16]{1,2,0:T(8,128)}, u32[]{:S(2)}) copy-start(s32[1,32,16]{1,2,0:T(8,128)} %param.9) | copy-start | bytes 6148
  2.2 14.9 %collective-permute-start = (bf16[256,128]{1,0:T(8,128)(2,1)S(1)}, bf16[256,128]{1,0:T(8,128)(2,1)S(1)}, u32[]{:S(2)}, u32[]{:S(2)}) collective-permute-start(bf16[256,128]{1,0:T(8,128)(2,1)S(1)} %get-tuple-element.36), channel_id=1, source_target_pairs={{4,8},{8,4},{12,16},{16,12},{20,24},{24,20},{28,32},{32,28},{36,40... | collective-permute-start | bytes 196616 | tf_op jit(solution)/shard_map/ppermute | solution.py:436
  5.0 12.1 %collective-permute-start.3 = (bf16[256,128]{1,0:T(8,128)(2,1)S(1)}, bf16[256,128]{1,0:T(8,128)(2,1)S(1)}, u32[]{:S(2)}, u32[]{:S(2)}) collective-permute-start(bf16[256,128]{1,0:T(8,128)(2,1)S(1)} %get-tuple-element.39), channel_id=1, source_target_pairs={{0,4},{4,0},{8,12},{12,8},{16,20},{20,16},{24,28},{28,24},{32,36},... | collective-permute-start | bytes 196616 | tf_op jit(solution)/shard_map/ppermute | solution.py:439
  11.5 5.6 %collective-permute-start.1 = (f32[8,256]{1,0:T(8,128)S(1)}, f32[8,256]{1,0:T(8,128)S(1)}, u32[]{:S(2)}, u32[]{:S(2)}) collective-permute-start(f32[8,256]{1,0:T(8,128)S(1)} %get-tuple-element.37), channel_id=1, source_target_pairs={{0,1},{1,0},{2,3},{3,2},{4,5},{5,4},{6,7},{7,6},{8,9},{9,8},{10,11... | collective-permute-start | bytes 24584 | tf_op jit(solution)/shard_map/ppermute | solution.py:437
  12.8 1.9 %copy-start.1 = (f32[4,16]{1,0:T(4,128)S(1)}, f32[4,16]{1,0:T(4,128)}, u32[]{:S(2)}) copy-start(f32[4,16]{1,0:T(4,128)} %param.8) | copy-start | bytes 772
  12.8 4.3 %collective-permute-start.2 = (f32[8,256]{1,0:T(8,128)S(1)}, f32[8,256]{1,0:T(8,128)S(1)}, u32[]{:S(2)}, u32[]{:S(2)}) collective-permute-start(f32[8,256]{1,0:T(8,128)S(1)} %get-tuple-element.38), channel_id=1, source_target_pairs={{1,2},{2,1},{3,0},{0,3},{5,6},{6,5},{7,4},{4,7},{9,10},{10,9},{11,... | collective-permute-start | bytes 24584 | tf_op jit(solution)/shard_map/ppermute | solution.py:438
  19.6 2.0 %collective-permute-start.4 = (f32[32,16,128]{2,1,0:T(8,128)S(1)}, f32[32,16,128]{2,1,0:T(8,128)S(1)}, u32[]{:S(2)}, u32[]{:S(2)}) collective-permute-start(f32[32,16,128]{2,1,0:T(8,128)S(1)} %get-tuple-element.41), channel_id=1, source_target_pairs={{0,4},{4,0},{1,5},{5,1},{2,6},{6,2},{3,7},{7,3},{8,12},{12,8},{9,1... | collective-permute-start | bytes 786440 | tf_op jit(solution)/shard_map/ppermute | solution.py:445
  20.4 6.9 %collective-permute-start.5 = (f32[32,128]{1,0:T(8,128)S(1)}, f32[32,128]{1,0:T(8,128)S(1)}, u32[]{:S(2)}, u32[]{:S(2)}) collective-permute-start(f32[32,128]{1,0:T(8,128)S(1)} %get-tuple-element.43), channel_id=1, source_target_pairs={{0,1},{1,0},{2,3},{3,2},{4,5},{5,4},{6,7},{7,6},{8,9},{9,8},{10,11... | collective-permute-start | bytes 49160 | tf_op jit(solution)/shard_map/ppermute | solution.py:446
  22.4 14.2 %all-to-all-start = ((s16[32,16,128]{2,1,0:T(8,128)(2,1)}), s16[32,16,128]{2,1,0:T(8,128)(2,1)S(1)}, u32[]{:S(2)}, u32[]{:S(2)}) async-start(s16[32,16,128]{2,1,0:T(8,128)(2,1)} %shard_map.71), calls=%async_computation | async-start | bytes 262144 | tf_op jit(solution)/shard_map/all_to_all | solution.py:451
  27.3 3.9 %collective-permute-start.6 = (f32[32,128]{1,0:T(8,128)S(1)}, f32[32,128]{1,0:T(8,128)S(1)}, u32[]{:S(2)}, u32[]{:S(2)}) collective-permute-start(f32[32,128]{1,0:T(8,128)S(1)} %shard_map.72.z_mine), channel_id=1, source_target_pairs={{0,3},{3,0},{1,2},{2,1},{4,7},{7,4},{5,6},{6,5},{8,11},{11,8},{9,1... | collective-permute-start | bytes 49160 | tf_op jit(solution)/shard_map/ppermute | solution.py:450
